TPU v7x, 32 devices: a whole 2x2x4 slice. The times are simulated.
32 devices in a mesh: side: 2 (over core), grp: 4 (over y, x), tp: 4 (over z).
Axes of the slice: x: 2, y: 2, z: 4, core: 2. Of those that a mesh axis runs over, the one named last changes fastest.
Arguments:
- queries: bfloat16 [96, 4096], P('grp', 'side'), may hold values from -6 to 6
- kv_cache: bfloat16 [96, 8, 384, 256], P('grp', ('side', 'tp')), may hold values from -6 to 6
- lengths: int32 [96], P('grp'), may hold values from 2 to 768, as said below
- out_weight: bfloat16 [4096, 2048], P(('side', 'tp')), may hold values from -1 to 1
- resid: bfloat16 [96, 2048], P('grp'), may hold values from -6 to 6
- norm_gain: float32 [2048], replicated, may hold values from 0.1 to 1.9
- expert_ids: int32 [96, 8], P('grp'), may hold values from 0 to 31, all different within a row; in each aligned block of 24 rows (0 to 23, 24 to 47, ...) at most 12 rows name the same one
- expert_gates: float32 [96, 8], P('grp'), may hold values from 0.05 to 1
- w_gate_up: bfloat16 [32, 2048, 1536], P(('side', 'grp', 'tp')), may hold values from -0.125 to 0.125
- w_down: bfloat16 [32, 768, 2048], P(('side', 'grp', 'tp')), may hold values from -0.21875 to 0.21875
Outputs:
- layer_out: bfloat16 [96, 2048], P('grp', ('side', 'tp'))
Inputs may be any that keep to these rules, and one draw needn't show every extreme that they name: `lengths`: every row's cache holds at least two tokens; some row holds exactly 768. `expert_ids`: each row names 8 different experts. Among the rows of one row group no expert is named by more than 12 rows; in some group an expert is named by exactly 12.
All inputs are finite; a program needn't handle non-finite values.
Results may differ from a plain program's by a relative error of at most 0.017.
Values may be sent and summed in bfloat16 or wider, within the bound.
No kernel may reach another device: no remote copies, remote signals or barrier semaphores. Data moves between devices by JAX's collectives and lax.ppermute only.
A program may use at most 64 MiB of HBM per device.

v0:
```python
import math

import jax
import jax.numpy as jnp
from jax import lax
from jax.sharding import PartitionSpec as P

QH = 32
KVH = 4
HD = 128
TOPK = 8


def swapped(value, axis, distance):
    mask = 2**distance
    pairs = [(source, source ^ mask) for source in range(lax.axis_size(axis))]
    return lax.ppermute(value, axis, pairs)


def body(
    queries,
    kv_cache,
    lengths,
    out_weight,
    resid,
    norm_gain,
    expert_ids,
    expert_gates,
    w_gate_up,
    w_down,
):
    lane_count = lax.axis_size("tp")
    tp_index = lax.axis_index("tp")
    side_count = lax.axis_size("side")
    section = lax.axis_index("side")
    grp_count = lax.axis_size("grp")
    group_size = side_count * lane_count
    member_index = section * lane_count + tp_index
    kv_parts = group_size // KVH
    group_heads = QH // KVH
    per_member = QH // group_size
    part_span = kv_cache.shape[2]
    model_width = out_weight.shape[1]
    piece_width = model_width // group_size
    rows_grp = lengths.shape[0]
    local_experts = w_gate_up.shape[0]
    experts_all = local_experts * side_count * grp_count * lane_count
    capacity = max(2, 2 * rows_grp * TOPK // experts_all)
    head_start = tp_index // kv_parts * group_heads * HD
    part_index = tp_index % kv_parts
    row_count = queries.shape[0]
    query_rows = lax.dynamic_slice_in_dim(queries, head_start, group_heads * HD, 1).reshape(
        row_count, group_heads, HD
    )
    key_rows = kv_cache[:, 0, :, :HD]
    value_rows = kv_cache[:, 0, :, HD:]
    positions = part_index * part_span + jnp.arange(part_span, dtype=jnp.int32)
    valid_mask = (positions[None, :] < lengths[:, None])[:, None, :]
    scores = jnp.einsum(
        "rgd,rpd->rgp", query_rows, key_rows, preferred_element_type=jnp.float32
    ) / math.sqrt(HD)
    scores = jnp.where(valid_mask, scores, -1e30)
    row_max = jnp.max(scores, axis=-1)
    for bit_index in range(kv_parts.bit_length() - 1):
        row_max = jnp.maximum(row_max, swapped(row_max, "tp", bit_index))
    weights = jnp.where(valid_mask, jnp.exp(scores - row_max[..., None]), 0.0)
    weight_sum = jnp.sum(weights, axis=-1)
    numerator = jnp.einsum(
        "rgp,rpd->rgd", weights.astype(jnp.bfloat16), value_rows, preferred_element_type=jnp.float32
    )
    for bit_index in range(kv_parts.bit_length() - 1):
        other_numerator, other_sum = swapped((numerator, weight_sum), "tp", bit_index)
        numerator = numerator + other_numerator
        weight_sum = weight_sum + other_sum
    heads_out = (numerator / weight_sum[..., None]).astype(jnp.bfloat16)
    mine = lax.dynamic_slice_in_dim(heads_out, part_index * per_member, per_member, 1).reshape(
        row_count, per_member * HD
    )
    projected = jnp.dot(mine, out_weight, preferred_element_type=jnp.float32)
    summed = lax.psum(projected, ("side", "tp"))
    middle = (resid.astype(jnp.float32) + summed).astype(jnp.bfloat16)
    middle_wide = middle.astype(jnp.float32)
    inv_rms = lax.rsqrt(jnp.mean(middle_wide * middle_wide, axis=-1, keepdims=True) + 1e-06)
    normed = (middle_wide * inv_rms * norm_gain).astype(jnp.bfloat16)
    column_experts = (
        (
            (section * grp_count + jnp.arange(grp_count, dtype=jnp.int32)[:, None]) * lane_count
            + tp_index
        )
        * local_experts
        + jnp.arange(local_experts, dtype=jnp.int32)[None, :]
    ).reshape(-1)
    matches = expert_ids[:, :, None] == column_experts[None, None, :]
    hit_count = jnp.sum(matches.astype(jnp.int32), axis=1)
    gate_cols = jnp.sum(jnp.where(matches, expert_gates[:, :, None], 0.0), axis=1)
    slot_rank = jnp.cumsum(hit_count, axis=0) - hit_count
    slot_ids = jnp.arange(capacity, dtype=jnp.int32)
    placed = (hit_count[:, :, None] == 1) & (slot_rank[:, :, None] == slot_ids[None, None, :])
    send_map = placed.astype(jnp.bfloat16)
    outgoing = jnp.einsum(
        "rcs,rd->csd", send_map, normed, preferred_element_type=jnp.float32
    ).astype(jnp.bfloat16)
    outgoing = outgoing.reshape(grp_count, local_experts, capacity, model_width)
    hidden = jnp.einsum(
        "gjcd,jdf->gjcf",
        lax.all_to_all(outgoing, "grp", split_axis=0, concat_axis=0, tiled=True),
        w_gate_up,
        preferred_element_type=jnp.float32,
    )
    inner_width = hidden.shape[-1] // 2
    activated = (jax.nn.silu(hidden[..., :inner_width]) * hidden[..., inner_width:]).astype(
        jnp.bfloat16
    )
    produced = jnp.einsum(
        "gjcf,jfd->gjcd", activated, w_down, preferred_element_type=jnp.float32
    ).astype(jnp.bfloat16)
    returned = lax.all_to_all(produced, "grp", split_axis=0, concat_axis=0, tiled=True)
    combine_weights = (send_map.astype(jnp.float32) * gate_cols[:, :, None]).reshape(row_count, -1)
    moe_part = jnp.dot(
        combine_weights,
        returned.reshape(-1, model_width).astype(jnp.float32),
        precision=lax.Precision.HIGHEST,
    )
    middle_mine = lax.dynamic_slice_in_dim(middle_wide, member_index * piece_width, piece_width, 1)
    moe_whole = lax.psum(moe_part, ("side", "tp"))
    return (
        middle_mine
        + lax.dynamic_slice_in_dim(moe_whole, member_index * piece_width, piece_width, 1)
    ).astype(jnp.bfloat16)


def solution(mesh):
    in_specs = (
        P("grp", "side"),
        P("grp", ("side", "tp"), None, None),
        P("grp"),
        P(("side", "tp"), None),
        P("grp", None),
        P(),
        P("grp", None),
        P("grp", None),
        P(("side", "grp", "tp"), None, None),
        P(("side", "grp", "tp"), None, None),
    )
    out_specs = P("grp", ("side", "tp"))
    return jax.shard_map(body, mesh=mesh, in_specs=in_specs, out_specs=out_specs, check_vma=False)
```

profile of v0, /device:TPU:0, one launch (start us, length us, event | category | flops | bytes accessed | tf_op | source)
XLA Modules:
  0.0 170.5 jit_solution(9980699713466857273)
XLA Ops:
  6.5 0.0 copy-start
  6.5 0.0 all-reduce.3.cloned.1.call-start
  6.5 1.0 dynamic-slice_bitcast_fusion
  7.5 0.7 broadcast_compare_fusion
  8.3 2.7 %fusion.48 = (f32[24,8]{1,0:T(8,128)S(1)}, f32[24,8,384]{2,1,0:T(8,128)S(1)}) fusion(bf16[24,8,128]{2,1,0:T(8,128)(2,1)S(1)} %bitcast.70, bf16[24,1,384,256]{3,2,0,1:T(8,128)(2,1)} %bitcast.68, pred[24,384]{1,0:T(8,128)(4,1)S(1)} %broadcast_compare_fusion), kind=kOutput, calls=%fused_computation.58 | convolution fusion | flops 19095360 | bytes 2713344 | tf_op jit(solution)/shard_map/rgd,rpd->rgp/dot_general | solution.py:59
  10.9 3.0 %collective-permute-start = (f32[24,8]{1,0:T(8,128)S(1)}, f32[24,8]{1,0:T(8,128)S(1)}, u32[]{:S(2)}, u32[]{:S(2)}) collective-permute-start(f32[24,8]{1,0:T(8,128)S(1)} %get-tuple-element.7), channel_id=1, source_target_pairs={{0,1},{1,0},{2,3},{3,2},{4,5},{5,4},{6,7},{7,6},{8,9},{9,8},{10,11... | collective-permute-start | bytes 2312 | tf_op jit(solution)/shard_map/ppermute | solution.py:17
  14.0 0.8 fusion.41
  14.7 0.0 copy-start.1
  14.7 0.9 collective-permute-done
  15.6 0.0 copy-start.4
  15.6 0.2 fusion.19
  15.8 0.0 copy-start.3
  15.9 0.0 copy-start.5
  15.9 2.1 %collective-permute-start.2 = (f32[24,8]{1,0:T(8,128)S(1)}, f32[24,8]{1,0:T(8,128)S(1)}, u32[]{:S(2)}, u32[]{:S(2)}) collective-permute-start(f32[24,8]{1,0:T(8,128)S(1)} %fusion.19), channel_id=1, source_target_pairs={{0,1},{1,0},{2,3},{3,2},{4,5},{5,4},{6,7},{7,6},{8,9},{9,8},{10,11... | collective-permute-start | bytes 2312 | tf_op jit(solution)/shard_map/ppermute | solution.py:17
  18.0 2.2 %fusion.4 = f32[24,8,128]{2,1,0:T(8,128)S(1)} fusion(bf16[24,1,384,256]{3,2,0,1:T(8,128)(2,1)} %bitcast.69, f32[24,8,384]{2,1,0:T(8,128)S(1)} %get-tuple-element.8, f32[24,8]{1,0:T(8,128)S(1)} %max.3, pred[24,384]{1,0:T(8,128)(4,1)S(1)} %broadcast_compare_fusion), kind=kOutput, calls=%fused_computation.5 | convolution fusion | flops 19095552 | bytes 2762496 | tf_op jit(solution)/shard_map/rgp,rpd->rgd/dot_general | solution.py:68
  20.2 0.1 collective-permute-start.1
  20.2 0.0 collective-permute-done.2
  20.3 0.1 constant_dynamic-slice_fusion
  20.3 4.5 %collective-permute-done.1 = f32[24,8,128]{2,1,0:T(8,128)S(1)} collective-permute-done((f32[24,8,128]{2,1,0:T(8,128)S(1)}, f32[24,8,128]{2,1,0:T(8,128)S(1)}, u32[]{:S(2)}, u32[]{:S(2)}) %collective-permute-start.1) | collective-permute-done | bytes 98336 | tf_op jit(solution)/shard_map/ppermute | solution.py:17
  24.8 0.1 fusion.34
  25.0 0.0 copy-done.1
  25.0 1.1 fusion.38
  26.0 0.0 all-reduce.3.cloned.1.call-update
  26.1 0.1 copy.33
  26.2 0.1 copy.35
  26.3 54.8 %all-reduce.3.cloned.1.call-done = f32[24,2048]{1,0:T(8,128)} async-done(((f32[24,2048]{1,0:T(8,128)}), f32[24,2048]{1,0:T(8,128)}) %all-reduce.3.cloned.1.call-update) | async-done | bytes 196624 | tf_op jit(solution)/shard_map/psum | solution.py:80
  81.0 1.1 multiply_reduce_fusion
  82.2 0.0 copy-start.2
  82.2 0.7 copy-done.2
  82.9 0.0 copy-done.4
  82.9 1.0 fusion.12
  83.8 3.6 %all-to-all-start = ((bf16[4,1,12,2048]{3,2,1,0:T(8,128)(2,1)}), bf16[4,1,12,2048]{3,2,1,0:T(8,128)(2,1)S(1)}, u32[]{:S(2)}, u32[]{:S(2)}) async-start(bf16[4,1,12,2048]{3,2,1,0:T(8,128)(2,1)} %fusion.12), calls=%async_computation | async-start | bytes 524288 | tf_op jit(solution)/shard_map/all_to_all | solution.py:106
  87.5 0.0 copy-done.3
  87.5 0.0 copy-done.5
  87.5 0.1 fusion.42
  87.6 5.3 %all-to-all-done = bf16[4,1,12,2048]{3,2,1,0:T(8,128)(2,1)S(1)} async-done(((bf16[4,1,12,2048]{3,2,1,0:T(8,128)(2,1)}), bf16[4,1,12,2048]{3,2,1,0:T(8,128)(2,1)S(1)}, u32[]{:S(2)}, u32[]{:S(2)}) %all-to-all-start) | async-done | bytes 196640 | tf_op jit(solution)/shard_map/all_to_all | solution.py:106
  92.9 3.9 %fusion.6 = f32[4,1,12,1536]{3,2,0,1:T(8,128)S(1)} fusion(bf16[1,2048,1536]{2,1,0:T(8,128)(2,1)} %param.18, bf16[4,1,12,2048]{3,2,1,0:T(8,128)(2,1)S(1)} %all-to-all-done), kind=kOutput, calls=%fused_computation.8 | convolution fusion | flops 301989888 | bytes 6782976 | tf_op jit(solution)/shard_map/gjcd,jdf->gjcf/dot_general | solution.py:104
  96.8 0.0 copy-done
  96.8 1.4 fusion.13
  98.2 3.4 %all-to-all-start.1 = ((bf16[4,1,12,2048]{3,2,1,0:T(8,128)(2,1)}), bf16[4,1,12,2048]{3,2,1,0:T(8,128)(2,1)S(1)}, u32[]{:S(2)}, u32[]{:S(2)}) async-start(bf16[4,1,12,2048]{3,2,1,0:T(8,128)(2,1)} %fusion.13), calls=%async_computation.1 | async-start | bytes 524288 | tf_op jit(solution)/shard_map/all_to_all | solution.py:117
  101.6 0.0 all-reduce.5.cloned.1.call-start
  101.7 5.3 %all-to-all-done.1 = bf16[4,1,12,2048]{3,2,1,0:T(8,128)(2,1)S(1)} async-done(((bf16[4,1,12,2048]{3,2,1,0:T(8,128)(2,1)}), bf16[4,1,12,2048]{3,2,1,0:T(8,128)(2,1)S(1)}, u32[]{:S(2)}, u32[]{:S(2)}) %all-to-all-start.1) | async-done | bytes 196640 | tf_op jit(solution)/shard_map/all_to_all | solution.py:117
  107.0 0.7 reshape.139
  107.7 1.9 %fusion.49 = f32[24,2048]{1,0:T(8,128)} fusion(f32[24,48]{0,1:T(8,128)S(1)} %mul.79, bf16[48,2048]{1,0:T(8,128)(2,1)} %reshape.139), kind=kOutput, calls=%fused_computation.59 | convolution fusion | flops 28311552 | bytes 397824 | tf_op jit(solution)/shard_map/dot_general | solution.py:119
  109.6 0.0 all-reduce.5.cloned.1.call-update
  109.6 52.7 %all-reduce.5.cloned.1.call-done = f32[24,2048]{1,0:T(8,128)} async-done(((f32[24,2048]{1,0:T(8,128)}), f32[24,2048]{1,0:T(8,128)}) %all-reduce.5.cloned.1.call-update) | async-done | bytes 196624 | tf_op jit(solution)/shard_map/psum | solution.py:125
  162.3 1.4 add_convert_fusion.1
  (11 shorter events, 0.1 us)
Async XLA Ops:
  6.5 90.3 %copy-start = (bf16[1,768,2048]{2,1,0:T(8,128)(2,1)S(1)}, bf16[1,768,2048]{2,1,0:T(8,128)(2,1)}, u32[]{:S(2)}) copy-start(bf16[1,768,2048]{2,1,0:T(8,128)(2,1)} %param.19) | copy-start | bytes 9437188
  6.5 74.5 %all-reduce.3.cloned.1.call-start = ((), (), s32[]{:S(2)}) async-start(), calls=%async_computation.2 | async-start | bytes 393216 | tf_op jit(solution)/shard_map/psum | solution.py:80
  10.9 4.7 %collective-permute-start = (f32[24,8]{1,0:T(8,128)S(1)}, f32[24,8]{1,0:T(8,128)S(1)}, u32[]{:S(2)}, u32[]{:S(2)}) collective-permute-start(f32[24,8]{1,0:T(8,128)S(1)} %get-tuple-element.7), channel_id=1, source_target_pairs={{0,1},{1,0},{2,3},{3,2},{4,5},{5,4},{6,7},{7,6},{8,9},{9,8},{10,11... | collective-permute-start | bytes 2312 | tf_op jit(solution)/shard_map/ppermute | solution.py:17
  14.7 10.2 %copy-start.1 = (bf16[512,2048]{1,0:T(8,128)(2,1)S(1)}, bf16[512,2048]{1,0:T(8,128)(2,1)}, u32[]{:S(2)}) copy-start(bf16[512,2048]{1,0:T(8,128)(2,1)} %param.13) | copy-start | bytes 6291460
  15.6 67.2 %copy-start.4 = (f32[2048]{0:T(1024)S(1)}, f32[2048]{0:T(1024)}, u32[]{:S(2)}) copy-start(f32[2048]{0:T(1024)} %param.15) | copy-start | bytes 24580
  15.8 71.6 %copy-start.3 = (s32[24,8]{0,1:T(8,128)S(1)}, s32[24,8]{0,1:T(8,128)}, u32[]{:S(2)}) copy-start(s32[24,8]{0,1:T(8,128)} %param.16) | copy-start | bytes 2308
  15.9 71.6 %copy-start.5 = (f32[24,8]{0,1:T(8,128)S(1)}, f32[24,8]{0,1:T(8,128)}, u32[]{:S(2)}) copy-start(f32[24,8]{0,1:T(8,128)} %param.17) | copy-start | bytes 2308
  15.9 4.4 %collective-permute-start.2 = (f32[24,8]{1,0:T(8,128)S(1)}, f32[24,8]{1,0:T(8,128)S(1)}, u32[]{:S(2)}, u32[]{:S(2)}) collective-permute-start(f32[24,8]{1,0:T(8,128)S(1)} %fusion.19), channel_id=1, source_target_pairs={{0,1},{1,0},{2,3},{3,2},{4,5},{5,4},{6,7},{7,6},{8,9},{9,8},{10,11... | collective-permute-start | bytes 2312 | tf_op jit(solution)/shard_map/ppermute | solution.py:17
  20.2 4.7 %collective-permute-start.1 = (f32[24,8,128]{2,1,0:T(8,128)S(1)}, f32[24,8,128]{2,1,0:T(8,128)S(1)}, u32[]{:S(2)}, u32[]{:S(2)}) collective-permute-start(f32[24,8,128]{2,1,0:T(8,128)S(1)} %fusion.4), channel_id=1, source_target_pairs={{0,1},{1,0},{2,3},{3,2},{4,5},{5,4},{6,7},{7,6},{8,9},{9,8},{10,11... | collective-permute-start | bytes 294920 | tf_op jit(solution)/shard_map/ppermute | solution.py:17
  82.2 0.7 copy-start.2
  83.8 9.0 %all-to-all-start = ((bf16[4,1,12,2048]{3,2,1,0:T(8,128)(2,1)}), bf16[4,1,12,2048]{3,2,1,0:T(8,128)(2,1)S(1)}, u32[]{:S(2)}, u32[]{:S(2)}) async-start(bf16[4,1,12,2048]{3,2,1,0:T(8,128)(2,1)} %fusion.12), calls=%async_computation | async-start | bytes 524288 | tf_op jit(solution)/shard_map/all_to_all | solution.py:106
  98.2 8.8 %all-to-all-start.1 = ((bf16[4,1,12,2048]{3,2,1,0:T(8,128)(2,1)}), bf16[4,1,12,2048]{3,2,1,0:T(8,128)(2,1)S(1)}, u32[]{:S(2)}, u32[]{:S(2)}) async-start(bf16[4,1,12,2048]{3,2,1,0:T(8,128)(2,1)} %fusion.13), calls=%async_computation.1 | async-start | bytes 524288 | tf_op jit(solution)/shard_map/all_to_all | solution.py:117
  101.6 60.6 %all-reduce.5.cloned.1.call-start = ((), (), s32[]{:S(2)}) async-start(), calls=%async_computation.3 | async-start | bytes 393216 | tf_op jit(solution)/shard_map/psum | solution.py:125
Sparse Core Ops, SparseCore 0:
  26.2 54.8 all-reduce.2
  109.7 52.5 all-reduce.4
where the time goes:
time: 171 us; the launch traced here: 170 us
  waiting for transfers between devices  123 us (72%)
  matrix products  14.2 us (8%)
  between operations  13.5 us (8%)
  starting transfers between devices  12.3 us (7%)
  other arithmetic  4.48 us (3%)
  local copies, waits for them, and re-layouts  2.62 us (2%)
    psum x1, waiting for transfers between devices, body(): summed = lax.psum(projected, ('side', 'tp'))  54.8 us
    psum x1, waiting for transfers between devices, body(): moe_whole = lax.psum(moe_part, ('side', 'tp'))  52.7 us
    ppermute x3, waiting for transfers between devices, swapped(): return lax.ppermute(value, axis, pairs)  5.38 us
    all_to_all x1, waiting for transfers between devices, body(): lax.all_to_all(outgoing, 'grp', split_axis=0, concat_axis=0, tiled=True)  5.28 us
    all_to_all x1, waiting for transfers between devices, body(): lax.all_to_all(produced, 'grp', split_axis=0, concat_axis=0, tiled=True)  5.26 us
    ppermute x3, starting transfers between devices, swapped(): return lax.ppermute(value, axis, pairs)  5.19 us
    dot_general x1, matrix products, body(): jnp.einsum('gjcd,jdf->gjcf', lax.all_to_all(outgoing, 'grp', split_axis=0...  3.95 us
    all_to_all x1, starting transfers between devices, body(): lax.all_to_all(outgoing, 'grp', split_axis=0, concat_axis=0, tiled=True)  3.65 us
  transfers between devices with their start and end apart: 7, of which 6 were waited for; matrix products, arithmetic and copies ran while one was open for 2% of the time, Pallas kernels for 0%

commit v1 on v0

v1 whole, which is shorter than its diff:
```python
import math

import jax
import jax.numpy as jnp
from jax import lax
from jax.sharding import PartitionSpec as P

QH = 32
KVH = 4
HD = 128


def swapped(value, axis, mask):
    pairs = [(source, source ^ mask) for source in range(lax.axis_size(axis))]
    return lax.ppermute(value, axis, pairs)


def body(
    queries,
    kv_cache,
    lengths,
    out_weight,
    resid,
    norm_gain,
    expert_ids,
    expert_gates,
    w_gate_up,
    w_down,
):
    f32, bf16 = jnp.float32, jnp.bfloat16
    tp = lax.axis_size("tp")
    grp = lax.axis_size("grp")
    sides = lax.axis_size("side")
    tp_index = lax.axis_index("tp")
    grp_index = lax.axis_index("grp")
    section = lax.axis_index("side")
    group_size = sides * tp
    kv_parts = group_size // KVH
    group_heads = QH // KVH
    per_member = QH // group_size
    part_span = kv_cache.shape[2]
    model_width = out_weight.shape[1]
    half = model_width // sides
    piece = model_width // group_size
    rows = lengths.shape[0]
    part_index = tp_index % kv_parts
    head_start = tp_index // kv_parts * group_heads * HD
    query_rows = lax.dynamic_slice_in_dim(queries, head_start, group_heads * HD, 1).reshape(
        rows, group_heads, HD
    )
    key_rows = kv_cache[:, 0, :, :HD]
    value_rows = kv_cache[:, 0, :, HD:]
    positions = part_index * part_span + jnp.arange(part_span, dtype=jnp.int32)
    valid_mask = (positions[None, :] < lengths[:, None])[:, None, :]
    scores = jnp.einsum(
        "rgd,rpd->rgp", query_rows, key_rows, preferred_element_type=f32
    ) / math.sqrt(HD)
    scores = jnp.where(valid_mask, scores, -1e30)
    row_max = jnp.max(scores, axis=-1)
    weights = jnp.where(valid_mask, jnp.exp(scores - row_max[..., None]), 0.0)
    weight_sum = jnp.sum(weights, axis=-1)
    numerator = jnp.einsum(
        "rgp,rpd->rgd", weights.astype(bf16), value_rows, preferred_element_type=f32
    )
    stats = jnp.stack([row_max, weight_sum], -1)
    packed = jnp.concatenate(
        [numerator, jnp.pad(stats, ((0, 0), (0, 0), (0, HD - 2)))], -1
    )

    def chunk_of(part):
        return lax.dynamic_slice_in_dim(packed, part * per_member, per_member, 1)

    parts = [chunk_of(part_index)]
    for mask in range(1, kv_parts):
        parts.append(swapped(chunk_of(part_index ^ mask), "tp", mask))
    whole_max = parts[0][..., HD]
    for part in parts[1:]:
        whole_max = jnp.maximum(whole_max, part[..., HD])
    total, total_sum = 0.0, 0.0
    for part in parts:
        factor = jnp.exp(part[..., HD] - whole_max)
        total = total + part[..., :HD] * factor[..., None]
        total_sum = total_sum + part[..., HD + 1] * factor
    mine = (total / total_sum[..., None]).astype(bf16).reshape(rows, per_member * HD)
    projected = jnp.dot(mine, out_weight, preferred_element_type=f32)
    away = lax.dynamic_slice_in_dim(projected, (1 - section) * half, half, 1).astype(bf16)
    kept = lax.dynamic_slice_in_dim(projected, section * half, half, 1)
    kept = kept + swapped(away, "side", 1).astype(f32)
    outgoing = kept.astype(bf16)
    arrived = [swapped(outgoing, "tp", mask) for mask in range(1, tp)]
    for other in arrived:
        kept = kept + other.astype(f32)
    resid_half = lax.dynamic_slice_in_dim(resid, section * half, half, 1)
    middle = (resid_half.astype(f32) + kept).astype(bf16)
    experts_all = sides * grp * tp
    dest = (section * grp + jnp.arange(grp, dtype=jnp.int32)) * tp + tp_index
    gate_cols = []
    for s in range(sides):
        dest = (s * grp + jnp.arange(grp, dtype=jnp.int32)) * tp + tp_index
        matches = expert_ids[:, :, None] == dest[None, None, :]
        gate_cols.append(jnp.sum(jnp.where(matches, expert_gates[:, :, None], 0.0), axis=1))
    my_gates = jnp.where(section == 0, gate_cols[0], gate_cols[1])
    gates_hi = my_gates.astype(bf16)
    gates_lo = (my_gates - gates_hi.astype(f32)).astype(bf16)
    gate_pairs = jnp.stack([gates_hi, gates_lo], -1)

    def packet(target):
        pair = lax.dynamic_index_in_dim(gate_pairs, target, 1, keepdims=False)
        return jnp.concatenate([middle, jnp.pad(pair, ((0, 0), (0, HD - 2)))], -1)

    groups = [packet(grp_index)]
    for mask in range(1, grp):
        groups.append(swapped(packet(grp_index ^ mask), "grp", mask))
    gathered = jnp.concatenate(groups, 0)
    own_half = gathered[:, :half]
    gate = gathered[:, half].astype(f32) + gathered[:, half + 1].astype(f32)
    other_half = swapped(own_half, "side", 1)
    left = jnp.where(section == 0, own_half, other_half)
    right = jnp.where(section == 0, other_half, own_half)
    rows_all = jnp.concatenate([left, right], 1).astype(f32)
    inv_rms = lax.rsqrt(jnp.mean(rows_all * rows_all, axis=-1, keepdims=True) + 1e-06)
    normed = (rows_all * inv_rms * norm_gain).astype(bf16)
    hidden = jnp.dot(normed, w_gate_up[0], preferred_element_type=f32)
    inner = hidden.shape[-1] // 2
    act = (jax.nn.silu(hidden[:, :inner]) * hidden[:, inner:]).astype(bf16)
    produced = jnp.dot(act, w_down[0], preferred_element_type=f32) * gate[:, None]
    sent = lax.dynamic_slice_in_dim(produced, (1 - section) * half, half, 1).astype(bf16)
    mine_out = lax.dynamic_slice_in_dim(produced, section * half, half, 1)
    mine_out = mine_out + swapped(sent, "side", 1).astype(f32)
    blocks = mine_out.reshape(grp, rows, half)
    back = blocks[0]
    for mask in range(1, grp):
        back = back + swapped(blocks[mask].astype(bf16), "grp", mask).astype(f32)

    def columns(index):
        return lax.dynamic_slice_in_dim(back, index * piece, piece, 1)

    final = lax.dynamic_slice_in_dim(middle, tp_index * piece, piece, 1).astype(f32)
    final = final + columns(tp_index)
    for mask in range(1, tp):
        final = final + swapped(columns(tp_index ^ mask).astype(bf16), "tp", mask).astype(f32)
    return final.astype(bf16)


def solution(mesh):
    in_specs = (
        P("grp", "side"),
        P("grp", ("side", "tp"), None, None),
        P("grp"),
        P(("side", "tp"), None),
        P("grp", None),
        P(),
        P("grp", None),
        P("grp", None),
        P(("side", "grp", "tp"), None, None),
        P(("side", "grp", "tp"), None, None),
    )
    out_specs = P("grp", ("side", "tp"))
    return jax.shard_map(body, mesh=mesh, in_specs=in_specs, out_specs=out_specs, check_vma=False)
```

time: 171 us -> 80.2 us (0.47)
  waiting for transfers between devices: 123 us -> 27.7 us
  between operations: 13.5 us -> 0.21 us
  other arithmetic: 4.48 us -> 13.5 us
  starting transfers between devices: 12.3 us -> 19.2 us
  local copies, waits for them, and re-layouts: 2.62 us -> 7.29 us
  matrix products: 14.2 us -> 11.5 us
    psum x2 -> x0, waiting for transfers between devices: 107 us -> none  [the longest x1 54.8 us: body(): summed = lax.psum(projected, ('side', 'tp'))]
    ppermute x3 -> x16, waiting for transfers between devices: 5.38 us -> 27.7 us  [swapped(): return lax.ppermute(value, axis, pairs)]
    ppermute x3 -> x16, starting transfers between devices: 5.19 us -> 19.2 us  [swapped(): return lax.ppermute(value, axis, pairs)]
    all_to_all x2 -> x0, waiting for transfers between devices: 10.5 us -> none  [the longest x1 5.28 us: body(): lax.all_to_all(outgoing, 'grp', split_axis=0, concat_axis=0, tiled=True)]
    all_to_all x2 -> x0, starting transfers between devices: 7.05 us -> none  [the longest x1 3.65 us: body(): lax.all_to_all(outgoing, 'grp', split_axis=0, concat_axis=0, tiled=True)]
    concatenate x0 -> x3, other arithmetic: none -> 4.31 us  [the longest x1 2.75 us: body(): jnp.concatenate([numerator, jnp.pad(stats, ((0, 0), (0, 0), (0, HD - 2)))...]
    squeeze x0 -> x4, local copies, waits for them, and re-layouts: none -> 2.97 us  [packet(): pair = lax.dynamic_index_in_dim(gate_pairs, target, 1, keepdims=False)]
    dot_general x7 -> x5, matrix products: 14.2 us -> 11.5 us  [the longest x1 3.99 us: body(): hidden = jnp.dot(normed, w_gate_up[0], preferred_element_type=f32)]
  transfers between devices with their start and end apart: 7 -> 16, of which waited for: 6 -> 14; matrix products, arithmetic and copies ran while one was open for 2% -> 6% of each run, Pallas kernels for 0% -> 0%
where the time goes in v1:
time: 80.2 us; the launch traced here: 79.4 us
  waiting for transfers between devices  27.7 us (35%)
  starting transfers between devices  19.2 us (24%)
  other arithmetic  13.5 us (17%)
  matrix products  11.5 us (14%)
  local copies, waits for them, and re-layouts  7.29 us (9%)
    ppermute x16, waiting for transfers between devices, swapped(): return lax.ppermute(value, axis, pairs)  27.7 us
    ppermute x16, starting transfers between devices, swapped(): return lax.ppermute(value, axis, pairs)  19.2 us
    dot_general x1, matrix products, body(): hidden = jnp.dot(normed, w_gate_up[0], preferred_element_type=f32)  3.99 us
    squeeze x4, local copies, waits for them, and re-layouts, packet(): pair = lax.dynamic_index_in_dim(gate_pairs, target, 1, keepdims=False)  2.97 us
    concatenate x1, other arithmetic, body(): jnp.concatenate([numerator, jnp.pad(stats, ((0, 0), (0, 0), (0, HD - 2)))...  2.75 us
    dot_general x1, matrix products, body(): jnp.einsum('rgd,rpd->rgp', query_rows, key_rows, preferred_element_type=f32)  2.66 us
    dot_general x1, matrix products, body(): jnp.einsum('rgp,rpd->rgd', weights.astype(bf16), value_rows, preferred_el...  2.24 us
    dot_general x1, matrix products, body(): projected = jnp.dot(mine, out_weight, preferred_element_type=f32)  1.98 us
  transfers between devices with their start and end apart: 16, of which 14 were waited for; matrix products, arithmetic and copies ran while one was open for 6% of the time, Pallas kernels for 0%

profile of v1, /device:TPU:0, one launch (start us, length us, event | category | flops | bytes accessed | tf_op | source)
XLA Modules:
  0.0 79.4 jit_solution(17717278332633982769)
XLA Ops:
  0.0 1.0 %dynamic-slice_bitcast_fusion = bf16[3,8,8,128]{3,1,2,0:T(8,128)(2,1)S(1)} fusion(bf16[24,2048]{1,0:T(8,128)(2,1)} %param.10, s32[]{:T(128)S(6)} %select_n.106), kind=kLoop, calls=%fused_computation.69 | loop fusion | bytes 98308
  1.0 0.7 broadcast_compare_fusion
  1.7 2.7 %fusion.66 = (f32[24,8]{1,0:T(8,128)S(1)}, f32[24,8,384]{2,1,0:T(8,128)S(1)}) fusion(bf16[24,8,128]{2,1,0:T(8,128)(2,1)S(1)} %bitcast.52, bf16[24,1,384,256]{3,2,0,1:T(8,128)(2,1)} %bitcast.50, pred[24,384]{1,0:T(8,128)(4,1)S(1)} %broadcast_compare_fusion), kind=kOutput, calls=%fused_computation.115 | convolution fusion | flops 19095360 | bytes 2713344 | tf_op jit(solution)/shard_map/rgd,rpd->rgp/dot_general | solution.py:55
  4.4 0.1 copy.107
  4.5 0.8 %fusion.26 = f32[24,8]{1,0:T(8,128)} fusion(f32[24,8,384]{2,1,0:T(8,128)S(1)} %get-tuple-element.30, f32[24,8]{1,0:T(8,128)S(1)} %get-tuple-element.29, pred[24,384]{1,0:T(8,128)(4,1)S(1)} %broadcast_compare_fusion), kind=kLoop, calls=%fused_computation.42 | loop fusion | flops 220992 | bytes 305664 | tf_op jit(solution)/shard_map/reduce_sum | solution.py:61
  5.3 2.2 %fusion.7 = f32[24,8,128]{2,1,0:T(8,128)S(1)} fusion(bf16[24,1,384,256]{3,2,0,1:T(8,128)(2,1)} %bitcast.51, f32[24,8,384]{2,1,0:T(8,128)S(1)} %get-tuple-element.30, f32[24,8]{1,0:T(8,128)S(1)} %get-tuple-element.29, pred[24,384]{1,0:T(8,128)(4,1)} %copy-done.3), kind=kOutput, calls=%fused_computation.6 | convolution fusion | flops 19095552 | bytes 2762496 | tf_op jit(solution)/shard_map/rgp,rpd->rgd/dot_general | solution.py:62
  7.5 0.8 copy.108
  8.3 1.0 %copy.109 = f32[24,8,128]{0,1,2:T(8,128)} copy(f32[24,8,128]{2,1,0:T(8,128)S(1)} %fusion.7) | data formatting | bytes 196608 | tf_op jit(solution)/shard_map/rgp,rpd->rgd/dot_general | solution.py:62
  9.4 0.8 %select_maximum_fusion = f32[24,8,128]{0,1,2:T(8,128)} fusion(f32[24,8,1]{0,1,2:T(8,128)S(1)} %bitcast.59, f32[24,8,1]{0,1,2:T(8,128)S(1)} %bitcast.58), kind=kLoop, calls=%fused_computation.22 | loop fusion | flops 98304 | bytes 99840 | tf_op jit(solution)/shard_map/stack | solution.py:65
  10.2 2.8 %fusion.15 = (f32[24,4,256]{0,1,2:T(4,128)}, f32[24,4,256]{0,1,2:T(4,128)}) fusion(s32[]{:T(128)S(6)} %select_n.109, f32[24,8,128]{0,1,2:T(8,128)} %copy.109, f32[24,8,128]{0,1,2:T(8,128)} %select_maximum_fusion, s32[]{:T(128)S(6)} %select_n.110), kind=kLoop, calls=%fused_computation.21 | loop fusion | flops 49152 | bytes 393224 | tf_op jit(solution)/shard_map/concatenate | solution.py:66
  13.0 3.0 %collective-permute-start = (f32[24,4,256]{0,1,2:T(4,128)}, f32[24,4,256]{0,1,2:T(4,128)}, u32[]{:S(2)}, u32[]{:S(2)}) collective-permute-start(f32[24,4,256]{0,1,2:T(4,128)} %get-tuple-element.13), channel_id=1, source_target_pairs={{0,1},{1,0},{2,3},{3,2},{4,5},{5,4},{6,7},{7,6},{8,9},{9,8},{10,11... | collective-permute-start | bytes 294920 | tf_op jit(solution)/shard_map/ppermute | solution.py:15
  16.0 0.8 select_reduce_fusion
  16.8 11.4 %collective-permute-done = f32[24,4,256]{0,1,2:T(4,128)} collective-permute-done((f32[24,4,256]{0,1,2:T(4,128)}, f32[24,4,256]{0,1,2:T(4,128)}, u32[]{:S(2)}, u32[]{:S(2)}) %collective-permute-start) | collective-permute-done | bytes 98336 | tf_op jit(solution)/shard_map/ppermute | solution.py:15
  28.2 0.7 fusion.63
  28.9 1.1 %fusion.25 = bf16[24,4,128]{0,1,2:T(4,128)(2,1)S(1)} fusion(f32[24,4,256]{0,1,2:T(4,128)} %collective-permute-done, f32[24,4,256]{0,1,2:T(4,128)} %get-tuple-element.12, f32[24,4]{0,1:T(4,128)S(1)} %get-tuple-element.11, f32[24,4]{0,1:T(4,128)S(1)} %get-tuple-element.10, f32[24,4]{0,1:T(4,128)S(1)} %get-tuple-element.9), kind=kLoop, calls=%fused_computation.41 | loop fusion | flops 61440 | bytes 124032 | tf_op jit(solution)/shard_map/convert_element_type | solution.py:84
  30.0 0.1 copy.110
  30.2 2.0 %fusion.47 = f32[24,2048]{1,0:T(8,128)S(1)} fusion(bf16[512,2048]{1,0:T(8,128)(2,1)} %param.13, bf16[3,8,4,128]{3,2,1,0:T(4,128)(2,1)S(1)} %bitcast.53), kind=kOutput, calls=%fused_computation.70 | convolution fusion | flops 50331648 | bytes 2318336 | tf_op jit(solution)/shard_map/dot_general | solution.py:85
  32.2 0.1 collective-permute-start.1
  32.3 1.2 %collective-permute-done.1 = bf16[24,1024]{1,0:T(8,128)(2,1)S(1)} collective-permute-done((bf16[24,1024]{1,0:T(8,128)(2,1)S(1)}, bf16[24,1024]{1,0:T(8,128)(2,1)S(1)}, u32[]{:S(2)}, u32[]{:S(2)}) %collective-permute-start.1) | collective-permute-done | bytes 49184 | tf_op jit(solution)/shard_map/ppermute | solution.py:15
  33.5 1.8 %collective-permute-start.2 = (bf16[24,1024]{1,0:T(8,128)(2,1)S(1)}, bf16[24,1024]{1,0:T(8,128)(2,1)S(1)}, u32[]{:S(2)}, u32[]{:S(2)}) collective-permute-start(bf16[24,1024]{1,0:T(8,128)(2,1)S(1)} %fusion.43), channel_id=1, source_target_pairs={{0,1},{1,0},{2,3},{3,2},{4,5},{5,4},{6,7},{7,6},{8,9},{9,8},{10,11... | collective-permute-start | bytes 147464 | tf_op jit(solution)/shard_map/ppermute | solution.py:15
  35.3 2.6 %collective-permute-start.3 = (bf16[24,1024]{1,0:T(8,128)(2,1)S(1)}, bf16[24,1024]{1,0:T(8,128)(2,1)S(1)}, u32[]{:S(2)}, u32[]{:S(2)}) collective-permute-start(bf16[24,1024]{1,0:T(8,128)(2,1)S(1)} %fusion.43), channel_id=1, source_target_pairs={{0,2},{1,3},{2,0},{3,1},{4,6},{5,7},{6,4},{7,5},{8,10},{9,11},{10,... | collective-permute-start | bytes 147464 | tf_op jit(solution)/shard_map/ppermute | solution.py:15
  37.9 0.1 collective-permute-start.4
  37.9 0.6 fusion.57
  38.5 0.1 copy.116
  38.6 0.8 copy.117
  39.4 1.4 %copy.118 = bf16[24,1,2]{2,0,1:T(8,128)(2,1)} copy(bf16[24,1,2]{0,1,2:T(2,128)(2,1)} %get-tuple-element.27) | data formatting | bytes 192 | tf_op jit(solution)/shard_map/jit(dynamic_index_in_dim)/squeeze | solution.py:108
  40.7 0.0 collective-permute-done.2
  40.7 0.4 collective-permute-done.3
  41.2 2.7 %collective-permute-done.4 = bf16[24,1024]{1,0:T(8,128)(2,1)} collective-permute-done((bf16[24,1024]{1,0:T(8,128)(2,1)S(1)}, bf16[24,1024]{1,0:T(8,128)(2,1)}, u32[]{:S(2)}, u32[]{:S(2)}) %collective-permute-start.4) | collective-permute-done | bytes 49184 | tf_op jit(solution)/shard_map/ppermute | solution.py:15
  43.9 0.9 %add_convert_fusion = bf16[24,1024]{1,0:T(8,128)(2,1)S(1)} fusion(bf16[24,1024]{1,0:T(8,128)(2,1)} %collective-permute-done.4, bf16[24,1024]{1,0:T(8,128)(2,1)S(1)} %collective-permute-done.3, bf16[24,1024]{1,0:T(8,128)(2,1)S(1)} %collective-permute-done.2, bf16[24,1024]{1,0:T(8,128)(2,1)S(1)} %collective-permute-done.1, f32[24,2048]{1,0:T(8,128)S(1)} %fusion.47, ...), kind=kLoop, calls=%fused_computation.61 | loop fusion | flops 270336 | bytes 393220 | tf_op jit(solution)/shard_map/convert_element_type | solution.py:94
  44.7 0.7 fusion.44
  45.5 1.6 %collective-permute-start.5 = (bf16[24,1152]{1,0:T(8,128)(2,1)S(1)}, bf16[24,1152]{1,0:T(8,128)(2,1)S(1)}, u32[]{:S(2)}, u32[]{:S(2)}) collective-permute-start(bf16[24,1152]{1,0:T(8,128)(2,1)S(1)} %get-tuple-element.22), channel_id=1, source_target_pairs={{0,4},{4,0},{8,12},{12,8},{1,5},{5,1},{9,13},{13,9},{2,6},{6,2},{1... | collective-permute-start | bytes 165896 | tf_op jit(solution)/shard_map/ppermute | solution.py:15
  47.0 1.5 %collective-permute-start.6 = (bf16[24,1152]{1,0:T(8,128)(2,1)S(1)}, bf16[24,1152]{1,0:T(8,128)(2,1)S(1)}, u32[]{:S(2)}, u32[]{:S(2)}) collective-permute-start(bf16[24,1152]{1,0:T(8,128)(2,1)S(1)} %get-tuple-element.23), channel_id=1, source_target_pairs={{0,8},{4,12},{8,0},{12,4},{1,9},{5,13},{9,1},{13,5},{2,10},{6,14},... | collective-permute-start | bytes 165896 | tf_op jit(solution)/shard_map/ppermute | solution.py:15
  48.5 0.5 collective-permute-start.7
  49.0 0.8 copy.115
  49.8 0.4 collective-permute-done.5
  50.2 1.2 %collective-permute-done.6 = bf16[24,1152]{1,0:T(8,128)(2,1)S(1)} collective-permute-done((bf16[24,1152]{1,0:T(8,128)(2,1)S(1)}, bf16[24,1152]{1,0:T(8,128)(2,1)S(1)}, u32[]{:S(2)}, u32[]{:S(2)}) %collective-permute-start.6) | collective-permute-done | bytes 55328 | tf_op jit(solution)/shard_map/ppermute | solution.py:15
  51.4 2.3 %collective-permute-done.7 = bf16[24,1152]{1,0:T(8,128)(2,1)} collective-permute-done((bf16[24,1152]{1,0:T(8,128)(2,1)S(1)}, bf16[24,1152]{1,0:T(8,128)(2,1)}, u32[]{:S(2)}, u32[]{:S(2)}) %collective-permute-start.7) | collective-permute-done | bytes 55328 | tf_op jit(solution)/shard_map/ppermute | solution.py:15
  53.7 0.8 %fusion.31 = bf16[96,1152]{1,0:T(8,128)(2,1)S(1)} fusion(bf16[24,2]{1,0:T(8,128)(2,1)S(1)} %bitcast.54, bf16[24,1152]{1,0:T(8,128)(2,1)} %collective-permute-done.7, bf16[24,1152]{1,0:T(8,128)(2,1)S(1)} %collective-permute-done.6, bf16[24,1152]{1,0:T(8,128)(2,1)S(1)} %collective-permute-done.5, bf16[24,1024]{1,0:T(8,128)(2,1)S(1)} %add_convert_fusion), kind=kLoop, calls=%fused_computation.47 | loop fusion | flops 1658880 | bytes 436320 | tf_op jit(solution)/shard_map/concatenate | solution.py:114
  54.6 0.1 collective-permute-start.8
  54.6 0.2 add_reduce_fusion
  54.8 1.3 %collective-permute-done.8 = bf16[96,1024]{1,0:T(8,128)(2,1)S(1)} collective-permute-done((bf16[96,1024]{1,0:T(8,128)(2,1)S(1)}, bf16[96,1024]{1,0:T(8,128)(2,1)S(1)}, u32[]{:S(2)}, u32[]{:S(2)}) %collective-permute-start.8) | collective-permute-done | bytes 196640 | tf_op jit(solution)/shard_map/ppermute | solution.py:15
  56.1 0.2 fusion.11
  56.3 4.0 %fusion = f32[96,1536]{1,0:T(8,128)S(1)} fusion(bf16[1,2048,1536]{2,1,0:T(8,128)(2,1)} %param.18, f32[2048]{0:T(1024)} %param.15, f32[96]{0:T(128)S(1)} %add_rsqrt_fusion, bf16[96,1024]{1,0:T(8,128)(2,1)S(1)} %get-tuple-element.15, bf16[96,1024]{1,0:T(8,128)(2,1)S(1)} %get-tuple-element.14), kind=kOutput, calls=%fused_computation | convolution fusion | flops 605356032 | bytes 7283072 | tf_op jit(solution)/shard_map/dot_general | solution.py:123
  60.3 0.7 fusion.4
  61.0 0.2 collective-permute-start.9
  61.2 1.3 %collective-permute-done.9 = bf16[96,1024]{1,0:T(8,128)(2,1)S(1)} collective-permute-done((bf16[96,1024]{1,0:T(8,128)(2,1)S(1)}, bf16[96,1024]{1,0:T(8,128)(2,1)S(1)}, u32[]{:S(2)}, u32[]{:S(2)}) %collective-permute-start.9) | collective-permute-done | bytes 196640 | tf_op jit(solution)/shard_map/ppermute | solution.py:15
  62.5 0.1 fusion.64
  62.6 0.7 fusion.65
  63.2 0.5 collective-permute-start.10
  63.8 0.5 collective-permute-start.11
  64.3 2.4 %collective-permute-start.12 = (bf16[24,1024]{1,0:T(8,128)(2,1)}, bf16[24,1024]{1,0:T(8,128)(2,1)}, u32[]{:S(2)}, u32[]{:S(2)}) collective-permute-start(bf16[24,1024]{1,0:T(8,128)(2,1)} %get-tuple-element.17), channel_id=1, source_target_pairs={{0,12},{4,8},{8,4},{12,0},{1,13},{5,9},{9,5},{13,1},{2,14},{6,10},... | collective-permute-start | bytes 147464 | tf_op jit(solution)/shard_map/ppermute | solution.py:15
  66.7 0.9 %collective-permute-done.10 = bf16[24,1024]{1,0:T(8,128)(2,1)} collective-permute-done((bf16[24,1024]{1,0:T(8,128)(2,1)}, bf16[24,1024]{1,0:T(8,128)(2,1)}, u32[]{:S(2)}, u32[]{:S(2)}) %collective-permute-start.10) | collective-permute-done | bytes 49184 | tf_op jit(solution)/shard_map/ppermute | solution.py:15
  67.6 1.1 %collective-permute-done.11 = bf16[24,1024]{1,0:T(8,128)(2,1)} collective-permute-done((bf16[24,1024]{1,0:T(8,128)(2,1)}, bf16[24,1024]{1,0:T(8,128)(2,1)}, u32[]{:S(2)}, u32[]{:S(2)}) %collective-permute-start.11) | collective-permute-done | bytes 49184 | tf_op jit(solution)/shard_map/ppermute | solution.py:15
  68.7 0.9 %collective-permute-done.12 = bf16[24,1024]{1,0:T(8,128)(2,1)} collective-permute-done((bf16[24,1024]{1,0:T(8,128)(2,1)}, bf16[24,1024]{1,0:T(8,128)(2,1)}, u32[]{:S(2)}, u32[]{:S(2)}) %collective-permute-start.12) | collective-permute-done | bytes 49184 | tf_op jit(solution)/shard_map/ppermute | solution.py:15
  69.6 0.9 %fusion.42 = f32[24,1024]{1,0:T(8,128)S(1)} fusion(f32[96,1024]{1,0:T(8,128)S(1)} %get-tuple-element.8, bf16[24,1024]{1,0:T(8,128)(2,1)} %collective-permute-done.12, bf16[24,1024]{1,0:T(8,128)(2,1)} %collective-permute-done.11, bf16[24,1024]{1,0:T(8,128)(2,1)} %collective-permute-done.10), kind=kLoop, calls=%fused_computation.60 | loop fusion | flops 147456 | bytes 344064 | tf_op jit(solution)/shard_map/add | solution.py:133
  70.4 0.6 copy-done.2
  71.1 0.0 collective-permute-start.13
  71.1 1.5 %collective-permute-start.14 = (bf16[24,256]{1,0:T(8,128)(2,1)S(1)}, bf16[24,256]{1,0:T(8,128)(2,1)S(1)}, u32[]{:S(2)}, u32[]{:S(2)}) collective-permute-start(bf16[24,256]{1,0:T(8,128)(2,1)S(1)} %get-tuple-element.21), channel_id=1, source_target_pairs={{0,2},{1,3},{2,0},{3,1},{4,6},{5,7},{6,4},{7,5},{8,10},{9,11},{10,... | collective-permute-start | bytes 36872 | tf_op jit(solution)/shard_map/ppermute | solution.py:15
  72.6 2.9 %collective-permute-start.15 = (bf16[24,256]{1,0:T(8,128)(2,1)S(1)}, bf16[24,256]{1,0:T(8,128)(2,1)S(1)}, u32[]{:S(2)}, u32[]{:S(2)}) collective-permute-start(bf16[24,256]{1,0:T(8,128)(2,1)S(1)} %get-tuple-element.20), channel_id=1, source_target_pairs={{0,3},{1,2},{2,1},{3,0},{4,7},{5,6},{6,5},{7,4},{8,11},{9,10},{10,... | collective-permute-start | bytes 36872 | tf_op jit(solution)/shard_map/ppermute | solution.py:15
  75.5 0.0 collective-permute-done.13
  75.5 0.3 collective-permute-done.14
  75.7 2.3 %collective-permute-done.15 = bf16[24,256]{1,0:T(8,128)(2,1)S(1)} collective-permute-done((bf16[24,256]{1,0:T(8,128)(2,1)S(1)}, bf16[24,256]{1,0:T(8,128)(2,1)S(1)}, u32[]{:S(2)}, u32[]{:S(2)}) %collective-permute-start.15) | collective-permute-done | bytes 12320 | tf_op jit(solution)/shard_map/ppermute | solution.py:15
  78.1 1.4 %add_convert_fusion.1 = bf16[24,256]{1,0:T(8,128)(2,1)} fusion(bf16[24,256]{1,0:T(8,128)(2,1)S(1)} %collective-permute-done.15, bf16[24,256]{1,0:T(8,128)(2,1)S(1)} %collective-permute-done.14, bf16[24,256]{1,0:T(8,128)(2,1)S(1)} %collective-permute-done.13, f32[24,1024]{1,0:T(8,128)} %copy-done.2, s32[]{:T(128)S(6)} %select_n.112, bf16[24,1024]{1,0:T(8,128)(2,1)} %copy-done.1), kind=kLoop, calls=%fused_computation.73 | loop fusion | flops 55296 | bytes 86020 | tf_op jit(solution)/shard_map/convert_element_type | solution.py:142
  (19 shorter events, 0.2 us)
Async XLA Ops:
  0.0 60.3 %copy-start = (bf16[1,768,2048]{2,1,0:T(8,128)(2,1)S(1)}, bf16[1,768,2048]{2,1,0:T(8,128)(2,1)}, u32[]{:S(2)}) copy-start(bf16[1,768,2048]{2,1,0:T(8,128)(2,1)} %param.19) | copy-start | bytes 9437188
  1.7 2.7 %copy-start.3 = (pred[24,384]{1,0:T(8,128)(4,1)}, pred[24,384]{1,0:T(8,128)(4,1)S(1)}, u32[]{:S(2)}) copy-start(pred[24,384]{1,0:T(8,128)(4,1)S(1)} %broadcast_compare_fusion) | copy-start | bytes 27652
  13.0 15.3 %collective-permute-start = (f32[24,4,256]{0,1,2:T(4,128)}, f32[24,4,256]{0,1,2:T(4,128)}, u32[]{:S(2)}, u32[]{:S(2)}) collective-permute-start(f32[24,4,256]{0,1,2:T(4,128)} %get-tuple-element.13), channel_id=1, source_target_pairs={{0,1},{1,0},{2,3},{3,2},{4,5},{5,4},{6,7},{7,6},{8,9},{9,8},{10,11... | collective-permute-start | bytes 294920 | tf_op jit(solution)/shard_map/ppermute | solution.py:15
  32.2 1.3 %collective-permute-start.1 = (bf16[24,1024]{1,0:T(8,128)(2,1)S(1)}, bf16[24,1024]{1,0:T(8,128)(2,1)S(1)}, u32[]{:S(2)}, u32[]{:S(2)}) collective-permute-start(bf16[24,1024]{1,0:T(8,128)(2,1)S(1)} %dynamic-slice_convert_fusion.1), channel_id=1, source_target_pairs={{0,16},{16,0},{1,17},{17,1},{2,18},{18,2},{3,19},{19,3},{4,20},{20... | collective-permute-start | bytes 147464 | tf_op jit(solution)/shard_map/ppermute | solution.py:15
  33.5 7.3 %collective-permute-start.2 = (bf16[24,1024]{1,0:T(8,128)(2,1)S(1)}, bf16[24,1024]{1,0:T(8,128)(2,1)S(1)}, u32[]{:S(2)}, u32[]{:S(2)}) collective-permute-start(bf16[24,1024]{1,0:T(8,128)(2,1)S(1)} %fusion.43), channel_id=1, source_target_pairs={{0,1},{1,0},{2,3},{3,2},{4,5},{5,4},{6,7},{7,6},{8,9},{9,8},{10,11... | collective-permute-start | bytes 147464 | tf_op jit(solution)/shard_map/ppermute | solution.py:15
  35.3 5.9 %collective-permute-start.3 = (bf16[24,1024]{1,0:T(8,128)(2,1)S(1)}, bf16[24,1024]{1,0:T(8,128)(2,1)S(1)}, u32[]{:S(2)}, u32[]{:S(2)}) collective-permute-start(bf16[24,1024]{1,0:T(8,128)(2,1)S(1)} %fusion.43), channel_id=1, source_target_pairs={{0,2},{1,3},{2,0},{3,1},{4,6},{5,7},{6,4},{7,5},{8,10},{9,11},{10,... | collective-permute-start | bytes 147464 | tf_op jit(solution)/shard_map/ppermute | solution.py:15
  37.9 6.0 %collective-permute-start.4 = (bf16[24,1024]{1,0:T(8,128)(2,1)S(1)}, bf16[24,1024]{1,0:T(8,128)(2,1)}, u32[]{:S(2)}, u32[]{:S(2)}) collective-permute-start(bf16[24,1024]{1,0:T(8,128)(2,1)S(1)} %fusion.43), channel_id=1, source_target_pairs={{0,3},{1,2},{2,1},{3,0},{4,7},{5,6},{6,5},{7,4},{8,11},{9,10},{10,... | collective-permute-start | bytes 147464 | tf_op jit(solution)/shard_map/ppermute | solution.py:15
  44.7 15.6 %copy-start.1 = (bf16[24,1024]{1,0:T(8,128)(2,1)}, bf16[24,1024]{1,0:T(8,128)(2,1)S(1)}, u32[]{:S(2)}) copy-start(bf16[24,1024]{1,0:T(8,128)(2,1)S(1)} %add_convert_fusion) | copy-start | bytes 147460
  45.5 4.7 %collective-permute-start.5 = (bf16[24,1152]{1,0:T(8,128)(2,1)S(1)}, bf16[24,1152]{1,0:T(8,128)(2,1)S(1)}, u32[]{:S(2)}, u32[]{:S(2)}) collective-permute-start(bf16[24,1152]{1,0:T(8,128)(2,1)S(1)} %get-tuple-element.22), channel_id=1, source_target_pairs={{0,4},{4,0},{8,12},{12,8},{1,5},{5,1},{9,13},{13,9},{2,6},{6,2},{1... | collective-permute-start | bytes 165896 | tf_op jit(solution)/shard_map/ppermute | solution.py:15
  47.0 4.4 %collective-permute-start.6 = (bf16[24,1152]{1,0:T(8,128)(2,1)S(1)}, bf16[24,1152]{1,0:T(8,128)(2,1)S(1)}, u32[]{:S(2)}, u32[]{:S(2)}) collective-permute-start(bf16[24,1152]{1,0:T(8,128)(2,1)S(1)} %get-tuple-element.23), channel_id=1, source_target_pairs={{0,8},{4,12},{8,0},{12,4},{1,9},{5,13},{9,1},{13,5},{2,10},{6,14},... | collective-permute-start | bytes 165896 | tf_op jit(solution)/shard_map/ppermute | solution.py:15
  48.5 5.2 %collective-permute-start.7 = (bf16[24,1152]{1,0:T(8,128)(2,1)S(1)}, bf16[24,1152]{1,0:T(8,128)(2,1)}, u32[]{:S(2)}, u32[]{:S(2)}) collective-permute-start(bf16[24,1152]{1,0:T(8,128)(2,1)S(1)} %get-tuple-element.24), channel_id=1, source_target_pairs={{0,12},{4,8},{8,4},{12,0},{1,13},{5,9},{9,5},{13,1},{2,14},{6,10},... | collective-permute-start | bytes 165896 | tf_op jit(solution)/shard_map/ppermute | solution.py:15
  54.6 1.5 %collective-permute-start.8 = (bf16[96,1024]{1,0:T(8,128)(2,1)S(1)}, bf16[96,1024]{1,0:T(8,128)(2,1)S(1)}, u32[]{:S(2)}, u32[]{:S(2)}) collective-permute-start(bf16[96,1024]{1,0:T(8,128)(2,1)S(1)} %slice.85), channel_id=1, source_target_pairs={{0,16},{16,0},{1,17},{17,1},{2,18},{18,2},{3,19},{19,3},{4,20},{20... | collective-permute-start | bytes 589832 | tf_op jit(solution)/shard_map/ppermute | solution.py:15
  61.0 1.5 %collective-permute-start.9 = (bf16[96,1024]{1,0:T(8,128)(2,1)S(1)}, bf16[96,1024]{1,0:T(8,128)(2,1)S(1)}, u32[]{:S(2)}, u32[]{:S(2)}) collective-permute-start(bf16[96,1024]{1,0:T(8,128)(2,1)S(1)} %dynamic-slice_convert_fusion), channel_id=1, source_target_pairs={{0,16},{16,0},{1,17},{17,1},{2,18},{18,2},{3,19},{19,3},{4,20},{20... | collective-permute-start | bytes 589832 | tf_op jit(solution)/shard_map/ppermute | solution.py:15
  63.2 4.4 %collective-permute-start.10 = (bf16[24,1024]{1,0:T(8,128)(2,1)}, bf16[24,1024]{1,0:T(8,128)(2,1)}, u32[]{:S(2)}, u32[]{:S(2)}) collective-permute-start(bf16[24,1024]{1,0:T(8,128)(2,1)} %get-tuple-element.16), channel_id=1, source_target_pairs={{0,4},{4,0},{8,12},{12,8},{1,5},{5,1},{9,13},{13,9},{2,6},{6,2},{1... | collective-permute-start | bytes 147464 | tf_op jit(solution)/shard_map/ppermute | solution.py:15
  63.8 4.9 %collective-permute-start.11 = (bf16[24,1024]{1,0:T(8,128)(2,1)}, bf16[24,1024]{1,0:T(8,128)(2,1)}, u32[]{:S(2)}, u32[]{:S(2)}) collective-permute-start(bf16[24,1024]{1,0:T(8,128)(2,1)} %get-tuple-element.18), channel_id=1, source_target_pairs={{0,8},{4,12},{8,0},{12,4},{1,9},{5,13},{9,1},{13,5},{2,10},{6,14},... | collective-permute-start | bytes 147464 | tf_op jit(solution)/shard_map/ppermute | solution.py:15
  64.3 5.3 %collective-permute-start.12 = (bf16[24,1024]{1,0:T(8,128)(2,1)}, bf16[24,1024]{1,0:T(8,128)(2,1)}, u32[]{:S(2)}, u32[]{:S(2)}) collective-permute-start(bf16[24,1024]{1,0:T(8,128)(2,1)} %get-tuple-element.17), channel_id=1, source_target_pairs={{0,12},{4,8},{8,4},{12,0},{1,13},{5,9},{9,5},{13,1},{2,14},{6,10},... | collective-permute-start | bytes 147464 | tf_op jit(solution)/shard_map/ppermute | solution.py:15
  70.4 0.6 copy-start.2
  71.1 4.4 %collective-permute-start.13 = (bf16[24,256]{1,0:T(8,128)(2,1)S(1)}, bf16[24,256]{1,0:T(8,128)(2,1)S(1)}, u32[]{:S(2)}, u32[]{:S(2)}) collective-permute-start(bf16[24,256]{1,0:T(8,128)(2,1)S(1)} %get-tuple-element.19), channel_id=1, source_target_pairs={{0,1},{1,0},{2,3},{3,2},{4,5},{5,4},{6,7},{7,6},{8,9},{9,8},{10,11... | collective-permute-start | bytes 36872 | tf_op jit(solution)/shard_map/ppermute | solution.py:15
  71.1 4.7 %collective-permute-start.14 = (bf16[24,256]{1,0:T(8,128)(2,1)S(1)}, bf16[24,256]{1,0:T(8,128)(2,1)S(1)}, u32[]{:S(2)}, u32[]{:S(2)}) collective-permute-start(bf16[24,256]{1,0:T(8,128)(2,1)S(1)} %get-tuple-element.21), channel_id=1, source_target_pairs={{0,2},{1,3},{2,0},{3,1},{4,6},{5,7},{6,4},{7,5},{8,10},{9,11},{10,... | collective-permute-start | bytes 36872 | tf_op jit(solution)/shard_map/ppermute | solution.py:15
  72.6 5.5 %collective-permute-start.15 = (bf16[24,256]{1,0:T(8,128)(2,1)S(1)}, bf16[24,256]{1,0:T(8,128)(2,1)S(1)}, u32[]{:S(2)}, u32[]{:S(2)}) collective-permute-start(bf16[24,256]{1,0:T(8,128)(2,1)S(1)} %get-tuple-element.20), channel_id=1, source_target_pairs={{0,3},{1,2},{2,1},{3,0},{4,7},{5,6},{6,5},{7,4},{8,11},{9,10},{10,... | collective-permute-start | bytes 36872 | tf_op jit(solution)/shard_map/ppermute | solution.py:15

commit v2 on v0

v2 whole, which is shorter than its diff:
```python
import functools
import math

import jax
import jax.numpy as jnp
from jax import lax
from jax.experimental import pallas as pl
from jax.experimental.pallas import tpu as pltpu
from jax.sharding import PartitionSpec as P

QH = 32
KVH = 4
HD = 128
LOW = -1e30
F32 = jnp.float32
BF16 = jnp.bfloat16
MIB = 1024 * 1024
VMEM_SPEC = pl.BlockSpec(memory_space=pltpu.VMEM)


def swapped(value, axis, mask):
    pairs = [(source, source ^ mask) for source in range(lax.axis_size(axis))]
    return lax.ppermute(value, axis, pairs)


def crossed(value, mask):
    grp, tp = lax.axis_size("grp"), lax.axis_size("tp")
    pairs = [
        ((s * grp + g) * tp + t, ((1 - s) * grp + (g ^ mask)) * tp + t)
        for s in range(2)
        for g in range(grp)
        for t in range(tp)
    ]
    return lax.ppermute(value, ("side", "grp", "tp"), pairs)


def near(value, space=pltpu.VMEM):
    return pltpu.with_memory_space_constraint(value, space)


def call(kernel, ins, outs, scratch=(), far=(), limit=8, name=None, cost=None):
    spaces = [pltpu.HBM if i in far else pltpu.VMEM for i in range(len(ins))]
    return pl.pallas_call(
        kernel,
        out_shape=[pltpu.VMEM(shape, dtype) for shape, dtype in outs],
        in_specs=[pl.BlockSpec(memory_space=s) for s in spaces],
        out_specs=[VMEM_SPEC] * len(outs),
        scratch_shapes=list(scratch),
        compiler_params=pltpu.CompilerParams(vmem_limit_bytes=limit * MIB),
        name=name,
        cost_estimate=cost,
    )(*[near(a, s) for a, s in zip(ins, spaces)])


def attention_kernel(sizes, *refs):
    tp, grp, sides, kv_parts, group_heads, per_member, rows, span, top, half = sizes
    q_hbm, len_hbm, ids_hbm, gates_hbm, kv_hbm, out_w_hbm, resid_hbm, gain_hbm = refs[:8]
    own_ref, *send_refs = refs[8 : 8 + kv_parts]
    lanes_ref, out_w_ref, resid_ref, gain_ref = refs[8 + kv_parts : 12 + kv_parts]
    kv, q_in, len_ref, ids_ref, gates_ref, turn_s, q_s, score_s, num_s, max_s, sum_s, sems = refs[
        12 + kv_parts :
    ]
    chunks = 4
    step = rows // chunks
    section = lax.axis_index("side")
    tp_index = lax.axis_index("tp")
    part = tp_index % kv_parts
    q_cols = pl.ds(
        pl.multiple_of(tp_index // kv_parts * (group_heads * HD), group_heads * HD), group_heads * HD
    )
    half_cols = pl.ds(pl.multiple_of(section * half, half), half)
    pairs = [
        (q_hbm.at[:, q_cols], q_in),
        (len_hbm, len_ref),
        *[(kv_hbm.at[pl.ds(c * step, step), 0], kv.at[pl.ds(c * step, step)]) for c in range(chunks)],
        (ids_hbm, ids_ref),
        (gates_hbm, gates_ref),
        (out_w_hbm, out_w_ref),
        (resid_hbm.at[:, half_cols], resid_ref),
        (gain_hbm, gain_ref),
    ]
    copies = [pltpu.make_async_copy(a, b, sems.at[i]) for i, (a, b) in enumerate(pairs)]
    for copy in copies:
        copy.start()
    copies[0].wait()
    for g in range(group_heads):
        q_s[pl.ds(g, rows, stride=group_heads), :] = q_in[:, g * HD : (g + 1) * HD].astype(F32)
    copies[1].wait()

    for c in range(chunks):
        copies[2 + c].wait()
        for r in range(c * step, (c + 1) * step):
            at = pl.ds(r * group_heads, group_heads)
            score_s[at, :] = lax.dot_general(
                q_s[at, :].astype(BF16),
                kv[r, :, :HD],
                (((1,), (1,)), ((), ())),
                preferred_element_type=F32,
            )
    scale = math.log2(math.e) / math.sqrt(HD)
    place = part * span + lax.broadcasted_iota(jnp.int32, (group_heads, span), 1)
    for r in range(rows):
        at = pl.ds(r * group_heads, group_heads)
        valid = place < len_ref[r]
        score = jnp.where(valid, score_s[at, :], LOW)
        top_score = jnp.max(score, axis=-1, keepdims=True)
        weight = jnp.where(valid, jnp.exp2((score - top_score) * scale), 0.0)
        max_s[at, :] = jnp.broadcast_to(top_score, (group_heads, HD))
        sum_s[at, :] = jnp.broadcast_to(jnp.sum(weight, axis=-1, keepdims=True), (group_heads, HD))
        num_s[at, :] = jnp.dot(weight.astype(BF16), kv[r, :, HD:], preferred_element_type=F32)
    lane = lax.broadcasted_iota(jnp.int32, (rows, HD), 1)
    for mask, out in enumerate([own_ref, *send_refs]):
        first = (part ^ mask) * per_member
        stats = jnp.zeros((rows, HD), F32)
        for i in range(per_member):
            pick = pl.ds(first + i, rows, stride=group_heads)
            out[:, i * HD : (i + 1) * HD] = num_s[pick, :]
            stats = jnp.where(lane == 2 * i, max_s[pick, :], stats)
            stats = jnp.where(lane == 2 * i + 1, sum_s[pick, :], stats)
        out[:, per_member * HD :] = stats
    for copy in copies[2 + chunks :]:
        copy.wait()
    place = lax.broadcasted_iota(jnp.int32, (HD, rows), 0)
    target = place % (HD // 2)
    expert = jnp.where(target < grp, ((1 - section) * grp + target) * tp + tp_index, -1)
    gate = jnp.zeros((HD, rows), F32)
    for k in range(top):
        gate = gate + jnp.where(ids_ref[k : k + 1, :] == expert, gates_ref[k : k + 1, :], 0.0)
    high = gate.astype(BF16).astype(F32)
    turn_s[...] = jnp.zeros((HD, HD), F32)
    turn_s[:, :rows] = jnp.where(place < HD // 2, high, gate - high)
    lanes_ref[...] = turn_s[...].T[:rows].astype(BF16)


def fetch_kernel(after_ref, source, target, token_ref, sems):
    parts = sems.shape[0]
    step = source.shape[1] // parts
    copies = []
    for j in range(parts):
        at = pl.ds(j * step, step)
        copies.append(pltpu.make_async_copy(source.at[:, at], target.at[:, at], sems.at[j]))
        copies[-1].start()
    token_ref[...] = after_ref[:, :HD]
    for copy in copies:
        copy.wait()


def fetched(after, weight):
    rows = after.shape[0]
    return call(
        fetch_kernel,
        [after, weight],
        [(weight.shape, BF16), ((rows, HD), BF16)],
        [pltpu.SemaphoreType.DMA((8,))],
        far=(1,),
        name="fetch",
        cost=pl.CostEstimate(flops=0, transcendentals=0, bytes_accessed=2 * weight.size),
    )


def project_kernel(sizes, token_ref, weight_ref, *rest):
    kv_parts, per_member, half, sides = sizes
    packets = rest[:kv_parts]
    away_ref, kept_ref = rest[kv_parts:]
    scale = math.log2(math.e) / math.sqrt(HD)
    heads = []
    for i in range(per_member):
        at = per_member * HD + 2 * i
        tops = [p[:, at : at + 1] for p in packets]
        whole = functools.reduce(jnp.maximum, tops)
        total, total_sum = 0.0, 0.0
        for p, top in zip(packets, tops):
            factor = jnp.exp2((top - whole) * scale)
            total = total + p[:, i * HD : (i + 1) * HD] * factor
            total_sum = total_sum + p[:, at + 1 : at + 2] * factor
        heads.append((total / total_sum).astype(BF16))
    heads = jnp.concatenate(heads, axis=1)
    section = lax.axis_index("side")
    for ref, side in ((away_ref, 1 - section), (kept_ref, section)):
        cols = pl.ds(pl.multiple_of(side * half, half), half)
        ref[...] = jnp.dot(
            heads, weight_ref[:, cols], preferred_element_type=F32
        ).astype(ref.dtype)


def add_kernel(kept_ref, came_ref, out_ref):
    out_ref[...] = (kept_ref[...] + came_ref[...].astype(F32)).astype(BF16)


def middle_kernel(half, token_ref, resid_ref, lanes_ref, *rest):
    *parts, out_ref = rest
    total = parts[0][...].astype(F32)
    for part in parts[1:]:
        total = total + part[...].astype(F32)
    out_ref[:, :half] = (resid_ref[...].astype(F32) + total).astype(BF16)
    out_ref[:, half:] = lanes_ref[...]


def gather_kernel(half, *rest):
    *packets, x_ref, gate_ref = rest
    me = lax.axis_index("grp")
    for mask, packet in enumerate(packets):
        x_ref[me ^ mask] = packet[:, :half]
        lane = lax.broadcasted_iota(jnp.int32, (packet.shape[0], HD), 1)
        picked = jnp.where(lane % (HD // 2) == me, packet[:, half:].astype(F32), 0.0)
        gate_ref[me ^ mask] = jnp.broadcast_to(
            jnp.sum(picked, axis=1, keepdims=True), (packet.shape[0], HD)
        )


def scaled_rows(x_ref, gain_ref, side, half):
    groups, rows, _ = x_ref.shape
    x = x_ref[...].astype(F32).reshape(groups * rows, half)
    gain = gain_ref[:, pl.ds(pl.multiple_of(side * half, half), half)]
    return (x * gain).astype(BF16), jnp.sum(x * x, axis=1, keepdims=True)


def first_half_kernel(tile, x_ref, gain_ref, w_ref, hidden_ref, square_ref):
    half = x_ref.shape[2]
    section = lax.axis_index("side")
    x, square = scaled_rows(x_ref, gain_ref, 1 - section, half)
    square_ref[...] = jnp.broadcast_to(square, square_ref.shape)
    rows = pl.ds(pl.multiple_of((1 - section) * half, half), half)

    def column(j, carry):
        cols = pl.ds(pl.multiple_of(j * tile, tile), tile)
        hidden_ref[:, cols] = jnp.dot(x, w_ref[0, rows, cols], preferred_element_type=F32)
        return carry

    lax.fori_loop(0, hidden_ref.shape[1] // tile, column, 0)


def second_half_kernel(
    tile, x_ref, gain_ref, w_ref, hidden_ref, square_ref, gate_ref, down_ref, act_ref, away_ref
):
    half = x_ref.shape[2]
    inner = act_ref.shape[1]
    section = lax.axis_index("side")
    x, square = scaled_rows(x_ref, gain_ref, section, half)
    square = square + square_ref[:, :1]
    inv = lax.rsqrt(square / (half * lax.axis_size("side")) + 1e-6)
    rows = pl.ds(pl.multiple_of(section * half, half), half)

    def column(j, carry):
        both = []
        for base in (0, inner):
            cols = pl.ds(pl.multiple_of(base + j * tile, tile), tile)
            part = jnp.dot(x, w_ref[0, rows, cols], preferred_element_type=F32)
            both.append((hidden_ref[:, cols] + part) * inv)
        act = both[0] / (1.0 + jnp.exp(-both[0])) * both[1]
        act_ref[:, pl.ds(pl.multiple_of(j * tile, tile), tile)] = act.astype(BF16)
        return carry

    lax.fori_loop(0, inner // tile, column, 0)
    down(tile, act_ref, gate_ref, down_ref, away_ref, 1 - section)


def down(tile, act_ref, gate_ref, down_ref, out_ref, side):
    half = out_ref.shape[1]
    gate = gate_ref[...].reshape(act_ref.shape[0], HD)[:, :1]

    def column(j, carry):
        at = pl.ds(pl.multiple_of(side * half + j * tile, tile), tile)
        part = jnp.dot(act_ref[...], down_ref[0, :, at], preferred_element_type=F32)
        out_ref[:, pl.ds(pl.multiple_of(j * tile, tile), tile)] = (part * gate).astype(
            out_ref.dtype
        )
        return carry

    lax.fori_loop(0, half // tile, column, 0)


def keep_kernel(tile, act_ref, gate_ref, down_ref, kept_ref):
    down(tile, act_ref, gate_ref, down_ref, kept_ref, lax.axis_index("side"))


def blocks_kernel(kept_ref, came_ref, out_ref):
    blocks, rows, piece = out_ref.shape
    tp = kept_ref.shape[1] // piece
    for b in range(blocks):
        at = (slice(b // tp * rows, (b // tp + 1) * rows), slice(b % tp * piece, (b % tp + 1) * piece))
        out_ref[b] = (kept_ref[at] + came_ref[at].astype(F32)).astype(BF16)


def final_kernel(blocks_ref, middle_ref, out_ref):
    blocks, rows, piece = blocks_ref.shape
    at = pl.ds(pl.multiple_of(lax.axis_index("tp") * piece, piece), piece)
    total = middle_ref[:, at].astype(F32)
    for b in range(blocks):
        total = total + blocks_ref[b].astype(F32)
    out_ref[...] = total.astype(BF16)


def body(
    queries,
    kv_cache,
    lengths,
    out_weight,
    resid,
    norm_gain,
    expert_ids,
    expert_gates,
    w_gate_up,
    w_down,
):
    tp = lax.axis_size("tp")
    grp = lax.axis_size("grp")
    sides = lax.axis_size("side")
    group_size = sides * tp
    kv_parts = group_size // KVH
    group_heads = QH // KVH
    per_member = QH // group_size
    span = kv_cache.shape[2]
    width = out_weight.shape[1]
    half = width // sides
    piece = width // group_size
    rows, top = expert_ids.shape
    inner = w_down.shape[1]
    packet = (rows, (per_member + 1) * HD)
    sizes = (tp, grp, sides, kv_parts, group_heads, per_member, rows, span, top, half)
    many = rows * group_heads
    results = call(
        functools.partial(attention_kernel, sizes),
        [
            queries,
            lengths,
            expert_ids.T,
            expert_gates.T,
            kv_cache,
            out_weight,
            resid,
            norm_gain.reshape(1, width),
        ],
        [(packet, F32)] * kv_parts
        + [
            ((rows, HD), BF16),
            (out_weight.shape, BF16),
            ((rows, half), BF16),
            ((1, width), F32),
        ],
        [
            pltpu.VMEM((rows, span, 2 * HD), BF16),
            pltpu.VMEM((rows, group_heads * HD), BF16),
            pltpu.SMEM((rows,), jnp.int32),
            pltpu.VMEM((top, rows), jnp.int32),
            pltpu.VMEM((top, rows), F32),
            pltpu.VMEM((HD, HD), F32),
            pltpu.VMEM((many, HD), F32),
            pltpu.VMEM((many, span), F32),
            pltpu.VMEM((many, HD), F32),
            pltpu.VMEM((many, HD), F32),
            pltpu.VMEM((many, HD), F32),
            pltpu.SemaphoreType.DMA((11,)),
        ],
        far=range(8),
        limit=16,
        name="attention",
    )
    own, *rest = results[:kv_parts]
    gate_lanes, out_weight, resid, gain = results[kv_parts:]
    w_down, token = fetched(gate_lanes, w_down)
    came = [swapped(rest[mask - 1], "tp", mask) for mask in range(1, kv_parts)]
    away, kept = call(
        functools.partial(project_kernel, (kv_parts, per_member, half, sides)),
        [token, out_weight, own, *came],
        [((rows, half), BF16), ((rows, half), F32)],
        name="project",
    )
    outgoing = call(add_kernel, [kept, swapped(away, "side", 1)], [((rows, half), BF16)], name="pair")[0]
    w_gate_up, token = fetched(outgoing, w_gate_up)
    parts = [outgoing] + [swapped(outgoing, "tp", mask) for mask in range(1, tp)]
    middle = call(
        functools.partial(middle_kernel, half),
        [token, resid, gate_lanes, *parts],
        [((rows, half + HD), BF16)],
        name="middle",
    )[0]
    packets = [crossed(middle, mask) for mask in range(grp)]
    far_half, gate = call(
        functools.partial(gather_kernel, half),
        packets,
        [((grp, rows, half), BF16), ((grp, rows, HD), F32)],
        name="gather",
    )
    near_half = swapped(far_half, "side", 1)
    total = grp * rows
    tile = 256
    hidden, square = call(
        functools.partial(first_half_kernel, tile),
        [far_half, gain, w_gate_up],
        [((total, 2 * inner), F32), ((total, HD), F32)],
        name="first_half",
    )
    act, sent = call(
        functools.partial(second_half_kernel, tile),
        [near_half, gain, w_gate_up, hidden, square, gate, w_down],
        [((total, inner), BF16), ((total, half), BF16)],
        name="second_half",
    )
    back = swapped(sent, "side", 1)
    mine = call(
        functools.partial(keep_kernel, tile),
        [act, gate, w_down],
        [((total, half), F32)],
        name="keep",
    )[0]
    blocks = call(
        blocks_kernel, [mine, back], [((grp * tp, rows, piece), BF16)], name="blocks"
    )[0]
    returned = lax.all_to_all(blocks, ("grp", "tp"), 0, 0, tiled=True)
    return pl.pallas_call(
        final_kernel,
        out_shape=jax.ShapeDtypeStruct((rows, piece), BF16),
        in_specs=[VMEM_SPEC] * 2,
        out_specs=VMEM_SPEC,
        name="final",
    )(near(returned), near(middle))


def solution(mesh):
    in_specs = (
        P("grp", "side"),
        P("grp", ("side", "tp"), None, None),
        P("grp"),
        P(("side", "tp"), None),
        P("grp", None),
        P(),
        P("grp", None),
        P("grp", None),
        P(("side", "grp", "tp"), None, None),
        P(("side", "grp", "tp"), None, None),
    )
    out_specs = P("grp", ("side", "tp"))
    return jax.shard_map(body, mesh=mesh, in_specs=in_specs, out_specs=out_specs, check_vma=False)
```

time: 171 us -> 46.7 us (0.27)
  waiting for transfers between devices: 123 us -> 6.66 us
  matrix products: 14.2 us -> 0 us
  blocking collectives: 0 us -> 14.1 us
  Pallas kernels: 0 us -> 13.9 us
  between operations: 13.5 us -> 0.09 us
  other arithmetic: 4.48 us -> 0 us
  local copies, waits for them, and re-layouts: 2.62 us -> 0 us
    psum x2 -> x0, waiting for transfers between devices: 107 us -> none  [the longest x1 54.8 us: body(): summed = lax.psum(projected, ('side', 'tp'))]
    dot_general x7 -> x0, matrix products: 14.2 us -> none  [the longest x1 3.95 us: body(): jnp.einsum('gjcd,jdf->gjcf', lax.all_to_all(outgoing, 'grp', split_axis=0...]
    all_to_all x0 -> x1, blocking collectives: none -> 14.1 us  [body(): returned = lax.all_to_all(blocks, ('grp', 'tp'), 0, 0, tiled=True)]
    pallas_call x0 -> x12, Pallas kernels: none -> 13.9 us  [the longest x11 13.2 us: call(): pl.pallas_call(kernel, out_shape=[pltpu.VMEM(shape, dtype) for shape, dty...]
    all_to_all x2 -> x0, waiting for transfers between devices: 10.5 us -> none  [the longest x1 5.28 us: body(): lax.all_to_all(outgoing, 'grp', split_axis=0, concat_axis=0, tiled=True)]
    all_to_all x2 -> x0, starting transfers between devices: 7.05 us -> none  [the longest x1 3.65 us: body(): lax.all_to_all(outgoing, 'grp', split_axis=0, concat_axis=0, tiled=True)]
    ppermute x0 -> x4, waiting for transfers between devices: none -> 3.45 us  [crossed(): return lax.ppermute(value, ('side', 'grp', 'tp'), pairs)]
    ppermute x0 -> x4, starting transfers between devices: none -> 3.39 us  [crossed(): return lax.ppermute(value, ('side', 'grp', 'tp'), pairs)]
  transfers between devices with their start and end apart: 7 -> 11, of which waited for: 6 -> 7; matrix products, arithmetic and copies ran while one was open for 2% -> 0% of each run, Pallas kernels for 0% -> 15%
where the time goes in v2:
time: 46.7 us; the launch traced here: 46.6 us
  blocking collectives  14.1 us (30%)
  Pallas kernels  13.9 us (30%)
  starting transfers between devices  11.8 us (25%)
  waiting for transfers between devices  6.66 us (14%)
    all_to_all x1, blocking collectives, body(): returned = lax.all_to_all(blocks, ('grp', 'tp'), 0, 0, tiled=True)  14.1 us
    pallas_call x11, Pallas kernels, call(): pl.pallas_call(kernel, out_shape=[pltpu.VMEM(shape, dtype) for shape, dty...  13.2 us
    ppermute x7, starting transfers between devices, swapped(): return lax.ppermute(value, axis, pairs)  8.43 us
    ppermute x4, waiting for transfers between devices, crossed(): return lax.ppermute(value, ('side', 'grp', 'tp'), pairs)  3.45 us
    ppermute x4, starting transfers between devices, crossed(): return lax.ppermute(value, ('side', 'grp', 'tp'), pairs)  3.39 us
    ppermute x7, waiting for transfers between devices, swapped(): return lax.ppermute(value, axis, pairs)  3.21 us
  transfers between devices with their start and end apart: 11, of which 7 were waited for; matrix products, arithmetic and copies ran while one was open for 0% of the time, Pallas kernels for 15%

profile of v2, /device:TPU:0, one launch (start us, length us, event | category | flops | bytes accessed | tf_op | source)
XLA Modules:
  0.0 46.6 jit_solution(6897118449073357117)
XLA Ops:
  0.0 3.3 %attention.1 = (f32[24,640]{1,0:T(8,128)S(1)}, f32[24,640]{1,0:T(8,128)S(1)}, bf16[24,128]{1,0:T(8,128)(2,1)S(1)}, bf16[512,2048]{1,0:T(8,128)(2,1)S(1)}, bf16[2...) custom-call(bf16[24,2048]{1,0:T(8,128)(2,1)} %refs_0_.1, s32[24]{0:T(128)} %refs_1_.1, s32[8,24]{1,0:T(8,128)} %bitcast.4, ...), custom_call_target="tpu_custom_call" | custom-call | tf_op jit(solution)/shard_map/attention/pallas_call | solution.py:43
  3.3 3.1 %collective-permute-start = (f32[24,640]{1,0:T(8,128)S(1)}, f32[24,640]{1,0:T(8,128)S(1)}, u32[]{:S(2)}, u32[]{:S(2)}) collective-permute-start(f32[24,640]{1,0:T(8,128)S(1)} %get-tuple-element.27), channel_id=1, source_target_pairs={{0,1},{1,0},{2,3},{3,2},{4,5},{5,4},{6,7},{7,6},{8,9},{9,8},{10,11... | collective-permute-start | bytes 184328 | tf_op jit(solution)/shard_map/ppermute | solution.py:23
  6.4 1.9 %fetch.2 = (bf16[1,768,2048]{2,1,0:T(8,128)(2,1)S(1)}, bf16[24,128]{1,0:T(8,128)(2,1)S(1)}) custom-call(bf16[24,128]{1,0:T(8,128)(2,1)S(1)} %get-tuple-element.23.after_ref.lanes_ref, bf16[1,768,2048]{2,1,0:T(8,128)(2,1)} %source.2), custom_call_target="tpu_custom_call" | custom-call | bytes 3145728 | tf_op jit(solution)/shard_map/fetch/pallas_call | solution.py:43
  8.3 0.3 collective-permute-done.rest_1_
  8.6 0.6 %project.1 = (bf16[24,1024]{1,0:T(8,128)(2,1)S(1)}, f32[24,1024]{1,0:T(8,128)S(1)}) custom-call(bf16[24,128]{1,0:T(8,128)(2,1)S(1)} %get-tuple-element.24.token_ref, bf16[512,2048]{1,0:T(8,128)(2,1)S(1)} %get-tuple-element.25.weight_ref, f32[24,640]{1,0:T(8,128)S(1)} %get-tuple-element.26.rest_0_, f32[24,640]{1,0:T(8,128)S(1)} %collective-permute-done.rest_1_), custom_call_target="tpu_custom_call" | custom-call | tf_op jit(solution)/shard_map/project/pallas_call | solution.py:43
  9.2 0.0 collective-permute-start.1
  9.2 1.2 %collective-permute-done.1.came_ref = bf16[24,1024]{1,0:T(8,128)(2,1)S(1)} collective-permute-done((bf16[24,1024]{1,0:T(8,128)(2,1)S(1)}, bf16[24,1024]{1,0:T(8,128)(2,1)S(1)}, u32[]{:S(2)}, u32[]{:S(2)}) %collective-permute-start.1) | collective-permute-done | bytes 49184 | tf_op jit(solution)/shard_map/ppermute | solution.py:23
  10.5 4.1 %collective-permute-start.4 = (bf16[24,1024]{1,0:T(8,128)(2,1)S(1)}, bf16[24,1024]{1,0:T(8,128)(2,1)S(1)}, u32[]{:S(2)}, u32[]{:S(2)}) collective-permute-start(bf16[24,1024]{1,0:T(8,128)(2,1)S(1)} %pair.1.after_ref.rest_0_), channel_id=1, source_target_pairs={{0,3},{1,2},{2,1},{3,0},{4,7},{5,6},{6,5},{7,4},{8,11},{9,10},{10,... | collective-permute-start | bytes 147464 | tf_op jit(solution)/shard_map/ppermute | solution.py:23
  14.6 0.0 collective-permute-start.3
  14.6 0.6 %collective-permute-start.2 = (bf16[24,1024]{1,0:T(8,128)(2,1)S(1)}, bf16[24,1024]{1,0:T(8,128)(2,1)S(1)}, u32[]{:S(2)}, u32[]{:S(2)}) collective-permute-start(bf16[24,1024]{1,0:T(8,128)(2,1)S(1)} %pair.1.after_ref.rest_0_), channel_id=1, source_target_pairs={{0,1},{1,0},{2,3},{3,2},{4,5},{5,4},{6,7},{7,6},{8,9},{9,8},{10,11... | collective-permute-start | bytes 147464 | tf_op jit(solution)/shard_map/ppermute | solution.py:23
  15.2 2.9 %fetch.3 = (bf16[1,2048,1536]{2,1,0:T(8,128)(2,1)S(1)}, bf16[24,128]{1,0:T(8,128)(2,1)S(1)}) custom-call(bf16[24,1024]{1,0:T(8,128)(2,1)S(1)} %pair.1.after_ref.rest_0_, bf16[1,2048,1536]{2,1,0:T(8,128)(2,1)} %source.3), custom_call_target="tpu_custom_call" | custom-call | bytes 6291456 | tf_op jit(solution)/shard_map/fetch/pallas_call | solution.py:43
  18.1 0.0 collective-permute-done.4.rest_3_
  18.1 1.5 %collective-permute-done.3.rest_2_ = bf16[24,1024]{1,0:T(8,128)(2,1)S(1)} collective-permute-done((bf16[24,1024]{1,0:T(8,128)(2,1)S(1)}, bf16[24,1024]{1,0:T(8,128)(2,1)S(1)}, u32[]{:S(2)}, u32[]{:S(2)}) %collective-permute-start.3) | collective-permute-done | bytes 49184 | tf_op jit(solution)/shard_map/ppermute | solution.py:23
  19.6 0.0 collective-permute-done.2.rest_1_
  19.6 1.4 %collective-permute-start.8 = (bf16[24,1152]{1,0:T(8,128)(2,1)S(1)}, bf16[24,1152]{1,0:T(8,128)(2,1)S(1)}, u32[]{:S(2)}, u32[]{:S(2)}) collective-permute-start(bf16[24,1152]{1,0:T(8,128)(2,1)S(1)} %middle.1.middle_ref), channel_id=1, source_target_pairs={{0,28},{1,29},{2,30},{3,31},{4,24},{5,25},{6,26},{7,27},{8,20},{9,... | collective-permute-start | bytes 165896 | tf_op jit(solution)/shard_map/ppermute | solution.py:34
  21.0 1.4 %collective-permute-start.7 = (bf16[24,1152]{1,0:T(8,128)(2,1)S(1)}, bf16[24,1152]{1,0:T(8,128)(2,1)S(1)}, u32[]{:S(2)}, u32[]{:S(2)}) collective-permute-start(bf16[24,1152]{1,0:T(8,128)(2,1)S(1)} %middle.1.middle_ref), channel_id=1, source_target_pairs={{0,24},{1,25},{2,26},{3,27},{4,28},{5,29},{6,30},{7,31},{8,16},{9,... | collective-permute-start | bytes 165896 | tf_op jit(solution)/shard_map/ppermute | solution.py:34
  22.3 0.1 collective-permute-start.6
  22.5 0.5 %collective-permute-start.5 = (bf16[24,1152]{1,0:T(8,128)(2,1)S(1)}, bf16[24,1152]{1,0:T(8,128)(2,1)S(1)}, u32[]{:S(2)}, u32[]{:S(2)}) collective-permute-start(bf16[24,1152]{1,0:T(8,128)(2,1)S(1)} %middle.1.middle_ref), channel_id=1, source_target_pairs={{0,16},{1,17},{2,18},{3,19},{4,20},{5,21},{6,22},{7,23},{8,24},{9,... | collective-permute-start | bytes 165896 | tf_op jit(solution)/shard_map/ppermute | solution.py:34
  23.0 1.7 %collective-permute-done.8.rest_3_ = bf16[24,1152]{1,0:T(8,128)(2,1)S(1)} collective-permute-done((bf16[24,1152]{1,0:T(8,128)(2,1)S(1)}, bf16[24,1152]{1,0:T(8,128)(2,1)S(1)}, u32[]{:S(2)}, u32[]{:S(2)}) %collective-permute-start.8) | collective-permute-done | bytes 55328 | tf_op jit(solution)/shard_map/ppermute | solution.py:34
  24.7 0.6 %collective-permute-done.7.rest_2_ = bf16[24,1152]{1,0:T(8,128)(2,1)S(1)} collective-permute-done((bf16[24,1152]{1,0:T(8,128)(2,1)S(1)}, bf16[24,1152]{1,0:T(8,128)(2,1)S(1)}, u32[]{:S(2)}, u32[]{:S(2)}) %collective-permute-start.7) | collective-permute-done | bytes 55328 | tf_op jit(solution)/shard_map/ppermute | solution.py:34
  25.3 1.1 %collective-permute-done.6.rest_1_ = bf16[24,1152]{1,0:T(8,128)(2,1)S(1)} collective-permute-done((bf16[24,1152]{1,0:T(8,128)(2,1)S(1)}, bf16[24,1152]{1,0:T(8,128)(2,1)S(1)}, u32[]{:S(2)}, u32[]{:S(2)}) %collective-permute-start.6) | collective-permute-done | bytes 55328 | tf_op jit(solution)/shard_map/ppermute | solution.py:34
  26.4 0.0 collective-permute-done.5.rest_0_
  26.4 0.1 gather.1
  26.5 0.1 collective-permute-start.9
  26.7 1.5 %first_half.1 = (f32[96,1536]{1,0:T(8,128)S(1)}, f32[96,128]{1,0:T(8,128)S(1)}) custom-call(bf16[4,24,1024]{2,1,0:T(8,128)(2,1)S(1)} %get-tuple-element.32.x_ref, f32[1,2048]{1,0:T(1,128)S(1)} %get-tuple-element.33.gain_ref, bf16[1,2048,1536]{2,1,0:T(8,128)(2,1)S(1)} %get-tuple-element.34.w_ref), custom_call_target="tpu_custom_call" | custom-call | tf_op jit(solution)/shard_map/first_half/pallas_call | solution.py:43
  28.2 0.0 collective-permute-done.9.x_ref
  28.2 2.0 %second_half.1 = (bf16[96,768]{1,0:T(8,128)(2,1)S(1)}, bf16[96,1024]{1,0:T(8,128)(2,1)S(1)}) custom-call(bf16[4,24,1024]{2,1,0:T(8,128)(2,1)S(1)} %collective-permute-done.9.x_ref, f32[1,2048]{1,0:T(1,128)S(1)} %get-tuple-element.33.gain_ref, bf16[1,2048,1536]{2,1,0:T(8,128)(2,1)S(1)} %get-tuple-element.34.w_ref, ...), custom_call_target="tpu_custom_call" | custom-call | tf_op jit(solution)/shard_map/second_half/pallas_call | solution.py:43
  30.2 0.5 collective-permute-start.10
  30.7 0.9 %keep.1.kept_ref = f32[96,1024]{1,0:T(8,128)S(1)} custom-call(bf16[96,768]{1,0:T(8,128)(2,1)S(1)} %get-tuple-element.39.act_ref, f32[4,24,128]{2,1,0:T(8,128)S(1)} %get-tuple-element.37.gate_ref, bf16[1,768,2048]{2,1,0:T(8,128)(2,1)S(1)} %get-tuple-element.38.down_ref), custom_call_target="tpu_custom_call" | custom-call | tf_op jit(solution)/shard_map/keep/pallas_call | solution.py:43
  31.6 0.2 collective-permute-done.10.came_ref
  31.8 14.1 %all_to_all.5.blocks_ref = bf16[16,24,256]{2,1,0:T(8,128)(2,1)S(1)} all-to-all(bf16[16,24,256]{2,1,0:T(8,128)(2,1)S(1)} %blocks.1), channel_id=1, replica_groups=mesh['side'=2,'grp'=4,'tp'=4] {'grp','tp'}, dimensions={0} | all-to-all | bytes 393216 | tf_op jit(solution)/shard_map/all_to_all | solution.py:410
  45.9 0.6 %final.1 = bf16[24,256]{1,0:T(8,128)(2,1)} custom-call(bf16[16,24,256]{2,1,0:T(8,128)(2,1)S(1)} %all_to_all.5.blocks_ref, bf16[24,1152]{1,0:T(8,128)(2,1)S(1)} %middle.1.middle_ref), custom_call_target="tpu_custom_call" | custom-call | tf_op jit(solution)/shard_map/final/pallas_call | solution.py:411
  (3 shorter events, 0.1 us)
Async XLA Ops:
  3.3 5.3 %collective-permute-start = (f32[24,640]{1,0:T(8,128)S(1)}, f32[24,640]{1,0:T(8,128)S(1)}, u32[]{:S(2)}, u32[]{:S(2)}) collective-permute-start(f32[24,640]{1,0:T(8,128)S(1)} %get-tuple-element.27), channel_id=1, source_target_pairs={{0,1},{1,0},{2,3},{3,2},{4,5},{5,4},{6,7},{7,6},{8,9},{9,8},{10,11... | collective-permute-start | bytes 184328 | tf_op jit(solution)/shard_map/ppermute | solution.py:23
  9.2 1.2 %collective-permute-start.1 = (bf16[24,1024]{1,0:T(8,128)(2,1)S(1)}, bf16[24,1024]{1,0:T(8,128)(2,1)S(1)}, u32[]{:S(2)}, u32[]{:S(2)}) collective-permute-start(bf16[24,1024]{1,0:T(8,128)(2,1)S(1)} %get-tuple-element.29), channel_id=1, source_target_pairs={{0,16},{16,0},{1,17},{17,1},{2,18},{18,2},{3,19},{19,3},{4,20},{20... | collective-permute-start | bytes 147464 | tf_op jit(solution)/shard_map/ppermute | solution.py:23
  10.5 7.6 %collective-permute-start.4 = (bf16[24,1024]{1,0:T(8,128)(2,1)S(1)}, bf16[24,1024]{1,0:T(8,128)(2,1)S(1)}, u32[]{:S(2)}, u32[]{:S(2)}) collective-permute-start(bf16[24,1024]{1,0:T(8,128)(2,1)S(1)} %pair.1.after_ref.rest_0_), channel_id=1, source_target_pairs={{0,3},{1,2},{2,1},{3,0},{4,7},{5,6},{6,5},{7,4},{8,11},{9,10},{10,... | collective-permute-start | bytes 147464 | tf_op jit(solution)/shard_map/ppermute | solution.py:23
  14.6 5.0 %collective-permute-start.3 = (bf16[24,1024]{1,0:T(8,128)(2,1)S(1)}, bf16[24,1024]{1,0:T(8,128)(2,1)S(1)}, u32[]{:S(2)}, u32[]{:S(2)}) collective-permute-start(bf16[24,1024]{1,0:T(8,128)(2,1)S(1)} %pair.1.after_ref.rest_0_), channel_id=1, source_target_pairs={{0,2},{1,3},{2,0},{3,1},{4,6},{5,7},{6,4},{7,5},{8,10},{9,11},{10,... | collective-permute-start | bytes 147464 | tf_op jit(solution)/shard_map/ppermute | solution.py:23
  14.6 5.0 %collective-permute-start.2 = (bf16[24,1024]{1,0:T(8,128)(2,1)S(1)}, bf16[24,1024]{1,0:T(8,128)(2,1)S(1)}, u32[]{:S(2)}, u32[]{:S(2)}) collective-permute-start(bf16[24,1024]{1,0:T(8,128)(2,1)S(1)} %pair.1.after_ref.rest_0_), channel_id=1, source_target_pairs={{0,1},{1,0},{2,3},{3,2},{4,5},{5,4},{6,7},{7,6},{8,9},{9,8},{10,11... | collective-permute-start | bytes 147464 | tf_op jit(solution)/shard_map/ppermute | solution.py:23
  19.6 5.1 %collective-permute-start.8 = (bf16[24,1152]{1,0:T(8,128)(2,1)S(1)}, bf16[24,1152]{1,0:T(8,128)(2,1)S(1)}, u32[]{:S(2)}, u32[]{:S(2)}) collective-permute-start(bf16[24,1152]{1,0:T(8,128)(2,1)S(1)} %middle.1.middle_ref), channel_id=1, source_target_pairs={{0,28},{1,29},{2,30},{3,31},{4,24},{5,25},{6,26},{7,27},{8,20},{9,... | collective-permute-start | bytes 165896 | tf_op jit(solution)/shard_map/ppermute | solution.py:34
  21.0 4.3 %collective-permute-start.7 = (bf16[24,1152]{1,0:T(8,128)(2,1)S(1)}, bf16[24,1152]{1,0:T(8,128)(2,1)S(1)}, u32[]{:S(2)}, u32[]{:S(2)}) collective-permute-start(bf16[24,1152]{1,0:T(8,128)(2,1)S(1)} %middle.1.middle_ref), channel_id=1, source_target_pairs={{0,24},{1,25},{2,26},{3,27},{4,28},{5,29},{6,30},{7,31},{8,16},{9,... | collective-permute-start | bytes 165896 | tf_op jit(solution)/shard_map/ppermute | solution.py:34
  22.3 4.1 %collective-permute-start.6 = (bf16[24,1152]{1,0:T(8,128)(2,1)S(1)}, bf16[24,1152]{1,0:T(8,128)(2,1)S(1)}, u32[]{:S(2)}, u32[]{:S(2)}) collective-permute-start(bf16[24,1152]{1,0:T(8,128)(2,1)S(1)} %middle.1.middle_ref), channel_id=1, source_target_pairs={{0,20},{1,21},{2,22},{3,23},{4,16},{5,17},{6,18},{7,19},{8,28},{9,... | collective-permute-start | bytes 165896 | tf_op jit(solution)/shard_map/ppermute | solution.py:34
  22.5 4.0 %collective-permute-start.5 = (bf16[24,1152]{1,0:T(8,128)(2,1)S(1)}, bf16[24,1152]{1,0:T(8,128)(2,1)S(1)}, u32[]{:S(2)}, u32[]{:S(2)}) collective-permute-start(bf16[24,1152]{1,0:T(8,128)(2,1)S(1)} %middle.1.middle_ref), channel_id=1, source_target_pairs={{0,16},{1,17},{2,18},{3,19},{4,20},{5,21},{6,22},{7,23},{8,24},{9,... | collective-permute-start | bytes 165896 | tf_op jit(solution)/shard_map/ppermute | solution.py:34
  26.5 1.6 %collective-permute-start.9 = (bf16[4,24,1024]{2,1,0:T(8,128)(2,1)S(1)}, bf16[4,24,1024]{2,1,0:T(8,128)(2,1)S(1)}, u32[]{:S(2)}, u32[]{:S(2)}) collective-permute-start(bf16[4,24,1024]{2,1,0:T(8,128)(2,1)S(1)} %get-tuple-element.32.x_ref), channel_id=1, source_target_pairs={{0,16},{16,0},{1,17},{17,1},{2,18},{18,2},{3,19},{19,3},{4,20},{20... | collective-permute-start | bytes 589832 | tf_op jit(solution)/shard_map/ppermute | solution.py:23
  30.2 1.5 %collective-permute-start.10 = (bf16[96,1024]{1,0:T(8,128)(2,1)S(1)}, bf16[96,1024]{1,0:T(8,128)(2,1)S(1)}, u32[]{:S(2)}, u32[]{:S(2)}) collective-permute-start(bf16[96,1024]{1,0:T(8,128)(2,1)S(1)} %get-tuple-element.40), channel_id=1, source_target_pairs={{0,16},{16,0},{1,17},{17,1},{2,18},{18,2},{3,19},{19,3},{4,20},{20... | collective-permute-start | bytes 589832 | tf_op jit(solution)/shard_map/ppermute | solution.py:23

commit v3 on v2

--- a/solution.py
+++ b/solution.py
@@ -12,6 +12,8 @@
 KVH = 4
 HD = 128
 LOW = -1e30
+CHUNKS = 4
+LAG = 1
 F32 = jnp.float32
 BF16 = jnp.bfloat16
 MIB = 1024 * 1024
@@ -53,73 +55,34 @@
 
 
 def attention_kernel(sizes, *refs):
-    tp, grp, sides, kv_parts, group_heads, per_member, rows, span, top, half = sizes
-    q_hbm, len_hbm, ids_hbm, gates_hbm, kv_hbm, out_w_hbm, resid_hbm, gain_hbm = refs[:8]
-    own_ref, *send_refs = refs[8 : 8 + kv_parts]
-    lanes_ref, out_w_ref, resid_ref, gain_ref = refs[8 + kv_parts : 12 + kv_parts]
+    tp, grp, sides, kv_parts, group_heads, per_member, rows, span, top = sizes
+    q_hbm, len_hbm, ids_hbm, gates_hbm, kv_hbm = refs[:5]
+    own_ref, *send_refs = refs[5 : 5 + kv_parts]
+    lanes_ref = refs[5 + kv_parts]
     kv, q_in, len_ref, ids_ref, gates_ref, turn_s, q_s, score_s, num_s, max_s, sum_s, sems = refs[
-        12 + kv_parts :
+        6 + kv_parts :
     ]
-    chunks = 4
-    step = rows // chunks
+    step = rows // CHUNKS
     section = lax.axis_index("side")
     tp_index = lax.axis_index("tp")
     part = tp_index % kv_parts
     q_cols = pl.ds(
         pl.multiple_of(tp_index // kv_parts * (group_heads * HD), group_heads * HD), group_heads * HD
     )
-    half_cols = pl.ds(pl.multiple_of(section * half, half), half)
     pairs = [
         (q_hbm.at[:, q_cols], q_in),
         (len_hbm, len_ref),
-        *[(kv_hbm.at[pl.ds(c * step, step), 0], kv.at[pl.ds(c * step, step)]) for c in range(chunks)],
         (ids_hbm, ids_ref),
         (gates_hbm, gates_ref),
-        (out_w_hbm, out_w_ref),
-        (resid_hbm.at[:, half_cols], resid_ref),
-        (gain_hbm, gain_ref),
+        *[(kv_hbm.at[pl.ds(c * step, step), 0], kv.at[pl.ds(c * step, step)]) for c in range(CHUNKS)],
     ]
     copies = [pltpu.make_async_copy(a, b, sems.at[i]) for i, (a, b) in enumerate(pairs)]
     for copy in copies:
         copy.start()
-    copies[0].wait()
+    for copy in copies[:4]:
+        copy.wait()
     for g in range(group_heads):
         q_s[pl.ds(g, rows, stride=group_heads), :] = q_in[:, g * HD : (g + 1) * HD].astype(F32)
-    copies[1].wait()
-
-    for c in range(chunks):
-        copies[2 + c].wait()
-        for r in range(c * step, (c + 1) * step):
-            at = pl.ds(r * group_heads, group_heads)
-            score_s[at, :] = lax.dot_general(
-                q_s[at, :].astype(BF16),
-                kv[r, :, :HD],
-                (((1,), (1,)), ((), ())),
-                preferred_element_type=F32,
-            )
-    scale = math.log2(math.e) / math.sqrt(HD)
-    place = part * span + lax.broadcasted_iota(jnp.int32, (group_heads, span), 1)
-    for r in range(rows):
-        at = pl.ds(r * group_heads, group_heads)
-        valid = place < len_ref[r]
-        score = jnp.where(valid, score_s[at, :], LOW)
-        top_score = jnp.max(score, axis=-1, keepdims=True)
-        weight = jnp.where(valid, jnp.exp2((score - top_score) * scale), 0.0)
-        max_s[at, :] = jnp.broadcast_to(top_score, (group_heads, HD))
-        sum_s[at, :] = jnp.broadcast_to(jnp.sum(weight, axis=-1, keepdims=True), (group_heads, HD))
-        num_s[at, :] = jnp.dot(weight.astype(BF16), kv[r, :, HD:], preferred_element_type=F32)
-    lane = lax.broadcasted_iota(jnp.int32, (rows, HD), 1)
-    for mask, out in enumerate([own_ref, *send_refs]):
-        first = (part ^ mask) * per_member
-        stats = jnp.zeros((rows, HD), F32)
-        for i in range(per_member):
-            pick = pl.ds(first + i, rows, stride=group_heads)
-            out[:, i * HD : (i + 1) * HD] = num_s[pick, :]
-            stats = jnp.where(lane == 2 * i, max_s[pick, :], stats)
-            stats = jnp.where(lane == 2 * i + 1, sum_s[pick, :], stats)
-        out[:, per_member * HD :] = stats
-    for copy in copies[2 + chunks :]:
-        copy.wait()
     place = lax.broadcasted_iota(jnp.int32, (HD, rows), 0)
     target = place % (HD // 2)
     expert = jnp.where(target < grp, ((1 - section) * grp + target) * tp + tp_index, -1)
@@ -130,57 +93,115 @@
     turn_s[...] = jnp.zeros((HD, HD), F32)
     turn_s[:, :rows] = jnp.where(place < HD // 2, high, gate - high)
     lanes_ref[...] = turn_s[...].T[:rows].astype(BF16)
-
-
-def fetch_kernel(after_ref, source, target, token_ref, sems):
-    parts = sems.shape[0]
-    step = source.shape[1] // parts
+    scale = math.log2(math.e) / math.sqrt(HD)
+    place = part * span + lax.broadcasted_iota(jnp.int32, (group_heads, span), 1)
+    def spot(r):
+        return pl.ds(r * group_heads, group_heads)
+
+    def values(some):
+        for r in some:
+            valid = place < len_ref[r]
+            score = jnp.where(valid, score_s[spot(r), :], LOW)
+            top_score = jnp.max(score, axis=-1, keepdims=True)
+            weight = jnp.where(valid, jnp.exp2((score - top_score) * scale), 0.0)
+            max_s[spot(r), :] = jnp.broadcast_to(top_score, (group_heads, HD))
+            sum_s[spot(r), :] = jnp.broadcast_to(
+                jnp.sum(weight, axis=-1, keepdims=True), (group_heads, HD)
+            )
+            num_s[spot(r), :] = jnp.dot(
+                weight.astype(BF16), kv[r, :, HD:], preferred_element_type=F32
+            )
+
+    for c in range(CHUNKS):
+        copies[4 + c].wait()
+        for r in range(c * step, (c + 1) * step):
+            score_s[spot(r), :] = lax.dot_general(
+                q_s[spot(r), :].astype(BF16),
+                kv[r, :, :HD],
+                (((1,), (1,)), ((), ())),
+                preferred_element_type=F32,
+            )
+        if c >= LAG:
+            values(range((c - LAG) * step, (c - LAG + 1) * step))
+    values(range((CHUNKS - LAG) * step, rows))
+    lane = lax.broadcasted_iota(jnp.int32, (rows, HD), 1)
+    for mask, out in enumerate([own_ref, *send_refs]):
+        first = (part ^ mask) * per_member
+        stats = jnp.zeros((rows, HD), F32)
+        for i in range(per_member):
+            pick = pl.ds(first + i, rows, stride=group_heads)
+            out[:, i * HD : (i + 1) * HD] = num_s[pick, :].astype(out.dtype)
+            for j, value in enumerate((max_s[pick, :], sum_s[pick, :])):
+                for k in range(3):
+                    term = value.astype(out.dtype).astype(F32)
+                    stats = jnp.where(lane == 6 * i + 3 * j + k, term, stats)
+                    value = value - term
+        out[:, per_member * HD :] = stats.astype(out.dtype)
+
+
+def fetch_kernel(parts, after_ref, *refs):
+    count = (len(refs) - 2) // 2
+    sources, targets, token_ref, sems = refs[:count], refs[count:-2], refs[-2], refs[-1]
     copies = []
-    for j in range(parts):
-        at = pl.ds(j * step, step)
-        copies.append(pltpu.make_async_copy(source.at[:, at], target.at[:, at], sems.at[j]))
-        copies[-1].start()
+    for source, target, number in zip(sources, targets, parts):
+        axis = source.ndim - 2
+        step = source.shape[axis] // number
+        for j in range(number):
+            at = (slice(None),) * axis + (pl.ds(j * step, step),)
+            copies.append(
+                pltpu.make_async_copy(source.at[at], target.at[at], sems.at[len(copies)])
+            )
+            copies[-1].start()
     token_ref[...] = after_ref[:, :HD]
     for copy in copies:
         copy.wait()
 
 
-def fetched(after, weight):
+def fetched(after, *arrays):
     rows = after.shape[0]
+    parts = [4 if a.size > MIB // 2 else 1 for a in arrays]
     return call(
-        fetch_kernel,
-        [after, weight],
-        [(weight.shape, BF16), ((rows, HD), BF16)],
-        [pltpu.SemaphoreType.DMA((8,))],
-        far=(1,),
+        functools.partial(fetch_kernel, parts),
+        [after, *arrays],
+        [(a.shape, a.dtype) for a in arrays] + [((rows, HD), BF16)],
+        [pltpu.SemaphoreType.DMA((sum(parts),))],
+        far=range(1, len(arrays) + 1),
         name="fetch",
-        cost=pl.CostEstimate(flops=0, transcendentals=0, bytes_accessed=2 * weight.size),
+        cost=pl.CostEstimate(
+            flops=0, transcendentals=0, bytes_accessed=sum(2 * a.size * a.dtype.itemsize for a in arrays)
+        ),
     )
 
 
 def project_kernel(sizes, token_ref, weight_ref, *rest):
-    kv_parts, per_member, half, sides = sizes
+    kv_parts, per_member, half = sizes
     packets = rest[:kv_parts]
-    away_ref, kept_ref = rest[kv_parts:]
+    heads_ref, away_ref = rest[kv_parts:]
     scale = math.log2(math.e) / math.sqrt(HD)
-    heads = []
+    stats = [p[:, per_member * HD :].astype(F32) for p in packets]
+
+    def whole(stat, at):
+        return stat[:, at : at + 1] + stat[:, at + 1 : at + 2] + stat[:, at + 2 : at + 3]
+
     for i in range(per_member):
-        at = per_member * HD + 2 * i
-        tops = [p[:, at : at + 1] for p in packets]
-        whole = functools.reduce(jnp.maximum, tops)
+        tops = [whole(stat, 6 * i) for stat in stats]
+        highest = functools.reduce(jnp.maximum, tops)
         total, total_sum = 0.0, 0.0
-        for p, top in zip(packets, tops):
-            factor = jnp.exp2((top - whole) * scale)
-            total = total + p[:, i * HD : (i + 1) * HD] * factor
-            total_sum = total_sum + p[:, at + 1 : at + 2] * factor
-        heads.append((total / total_sum).astype(BF16))
-    heads = jnp.concatenate(heads, axis=1)
+        for p, stat, top in zip(packets, stats, tops):
+            factor = jnp.exp2((top - highest) * scale)
+            total = total + p[:, i * HD : (i + 1) * HD].astype(F32) * factor
+            total_sum = total_sum + whole(stat, 6 * i + 3) * factor
+        heads_ref[:, i * HD : (i + 1) * HD] = (total / total_sum).astype(BF16)
+    part_kernel(False, heads_ref, weight_ref, away_ref)
+
+
+def part_kernel(mine, heads_ref, weight_ref, out_ref):
+    half = out_ref.shape[1]
     section = lax.axis_index("side")
-    for ref, side in ((away_ref, 1 - section), (kept_ref, section)):
-        cols = pl.ds(pl.multiple_of(side * half, half), half)
-        ref[...] = jnp.dot(
-            heads, weight_ref[:, cols], preferred_element_type=F32
-        ).astype(ref.dtype)
+    cols = pl.ds(pl.multiple_of((section if mine else 1 - section) * half, half), half)
+    out_ref[...] = jnp.dot(
+        heads_ref[...], weight_ref[:, cols], preferred_element_type=F32
+    ).astype(out_ref.dtype)
 
 
 def add_kernel(kept_ref, came_ref, out_ref):
@@ -189,14 +210,15 @@
 
 def middle_kernel(half, token_ref, resid_ref, lanes_ref, *rest):
     *parts, out_ref = rest
+    cols = pl.ds(pl.multiple_of(lax.axis_index("side") * half, half), half)
     total = parts[0][...].astype(F32)
     for part in parts[1:]:
         total = total + part[...].astype(F32)
-    out_ref[:, :half] = (resid_ref[...].astype(F32) + total).astype(BF16)
+    out_ref[:, :half] = (resid_ref[:, cols].astype(F32) + total).astype(BF16)
     out_ref[:, half:] = lanes_ref[...]
 
 
-def gather_kernel(half, *rest):
+def gather_kernel(half, token_ref, *rest):
     *packets, x_ref, gate_ref = rest
     me = lax.axis_index("grp")
     for mask, packet in enumerate(packets):
@@ -223,11 +245,12 @@
     rows = pl.ds(pl.multiple_of((1 - section) * half, half), half)
 
     def column(j, carry):
-        cols = pl.ds(pl.multiple_of(j * tile, tile), tile)
+        cols = pl.ds(j * tile, tile)
         hidden_ref[:, cols] = jnp.dot(x, w_ref[0, rows, cols], preferred_element_type=F32)
         return carry
 
-    lax.fori_loop(0, hidden_ref.shape[1] // tile, column, 0)
+    for j in range(hidden_ref.shape[1] // tile):
+        column(j, 0)
 
 
 def second_half_kernel(
@@ -244,14 +267,15 @@
     def column(j, carry):
         both = []
         for base in (0, inner):
-            cols = pl.ds(pl.multiple_of(base + j * tile, tile), tile)
+            cols = pl.ds(base + j * tile, tile)
             part = jnp.dot(x, w_ref[0, rows, cols], preferred_element_type=F32)
             both.append((hidden_ref[:, cols] + part) * inv)
         act = both[0] / (1.0 + jnp.exp(-both[0])) * both[1]
-        act_ref[:, pl.ds(pl.multiple_of(j * tile, tile), tile)] = act.astype(BF16)
+        act_ref[:, pl.ds(j * tile, tile)] = act.astype(BF16)
         return carry
 
-    lax.fori_loop(0, inner // tile, column, 0)
+    for j in range(inner // tile):
+        column(j, 0)
     down(tile, act_ref, gate_ref, down_ref, away_ref, 1 - section)
 
 
@@ -260,14 +284,15 @@
     gate = gate_ref[...].reshape(act_ref.shape[0], HD)[:, :1]
 
     def column(j, carry):
-        at = pl.ds(pl.multiple_of(side * half + j * tile, tile), tile)
+        at = pl.ds(pl.multiple_of(side * half + j * tile, HD), tile)
         part = jnp.dot(act_ref[...], down_ref[0, :, at], preferred_element_type=F32)
-        out_ref[:, pl.ds(pl.multiple_of(j * tile, tile), tile)] = (part * gate).astype(
+        out_ref[:, pl.ds(j * tile, tile)] = (part * gate).astype(
             out_ref.dtype
         )
         return carry
 
-    lax.fori_loop(0, half // tile, column, 0)
+    for j in range(half // tile):
+        column(j, 0)
 
 
 def keep_kernel(tile, act_ref, gate_ref, down_ref, kept_ref):
@@ -317,7 +342,7 @@
     rows, top = expert_ids.shape
     inner = w_down.shape[1]
     packet = (rows, (per_member + 1) * HD)
-    sizes = (tp, grp, sides, kv_parts, group_heads, per_member, rows, span, top, half)
+    sizes = (tp, grp, sides, kv_parts, group_heads, per_member, rows, span, top)
     many = rows * group_heads
     results = call(
         functools.partial(attention_kernel, sizes),
@@ -327,17 +352,9 @@
             expert_ids.T,
             expert_gates.T,
             kv_cache,
-            out_weight,
-            resid,
-            norm_gain.reshape(1, width),
         ],
-        [(packet, F32)] * kv_parts
-        + [
-            ((rows, HD), BF16),
-            (out_weight.shape, BF16),
-            ((rows, half), BF16),
-            ((1, width), F32),
-        ],
+        [(packet, F32)] + [(packet, BF16)] * (kv_parts - 1)
+        + [((rows, HD), BF16)],
         [
             pltpu.VMEM((rows, span, 2 * HD), BF16),
             pltpu.VMEM((rows, group_heads * HD), BF16),
@@ -350,23 +367,29 @@
             pltpu.VMEM((many, HD), F32),
             pltpu.VMEM((many, HD), F32),
             pltpu.VMEM((many, HD), F32),
-            pltpu.SemaphoreType.DMA((11,)),
+            pltpu.SemaphoreType.DMA((4 + CHUNKS,)),
         ],
-        far=range(8),
+        far=range(5),
         limit=16,
         name="attention",
     )
     own, *rest = results[:kv_parts]
-    gate_lanes, out_weight, resid, gain = results[kv_parts:]
-    w_down, token = fetched(gate_lanes, w_down)
+    gate_lanes = results[kv_parts]
+    out_weight, resid, gain, token = fetched(
+        gate_lanes, out_weight, resid, norm_gain.reshape(1, width)
+    )
     came = [swapped(rest[mask - 1], "tp", mask) for mask in range(1, kv_parts)]
-    away, kept = call(
-        functools.partial(project_kernel, (kv_parts, per_member, half, sides)),
+    heads, away = call(
+        functools.partial(project_kernel, (kv_parts, per_member, half)),
         [token, out_weight, own, *came],
-        [((rows, half), BF16), ((rows, half), F32)],
+        [((rows, per_member * HD), BF16), ((rows, half), BF16)],
         name="project",
     )
-    outgoing = call(add_kernel, [kept, swapped(away, "side", 1)], [((rows, half), BF16)], name="pair")[0]
+    away = swapped(away, "side", 1)
+    kept = call(
+        functools.partial(part_kernel, True), [heads, out_weight], [((rows, half), F32)], name="kept"
+    )[0]
+    outgoing = call(add_kernel, [kept, away], [((rows, half), BF16)], name="pair")[0]
     w_gate_up, token = fetched(outgoing, w_gate_up)
     parts = [outgoing] + [swapped(outgoing, "tp", mask) for mask in range(1, tp)]
     middle = call(
@@ -375,10 +398,12 @@
         [((rows, half + HD), BF16)],
         name="middle",
     )[0]
-    packets = [crossed(middle, mask) for mask in range(grp)]
+    w_down, token = fetched(middle, w_down)
+    packets = [crossed(middle, mask) for mask in [*range(1, grp), 0]]
+    packets = [packets[-1], *packets[:-1]]
     far_half, gate = call(
         functools.partial(gather_kernel, half),
-        packets,
+        [token, *packets],
         [((grp, rows, half), BF16), ((grp, rows, HD), F32)],
         name="gather",
     )

time: 46.7 us -> 44.6 us (0.955)
  waiting for transfers between devices: 6.66 us -> 5.83 us
  Pallas kernels: 13.9 us -> 13.1 us
    ppermute x4, waiting for transfers between devices: 3.45 us -> 1.56 us  [crossed(): return lax.ppermute(value, ('side', 'grp', 'tp'), pairs)]
    ppermute x7, waiting for transfers between devices: 3.21 us -> 4.27 us  [swapped(): return lax.ppermute(value, axis, pairs)]
    pallas_call x11 -> x13, Pallas kernels: 13.2 us -> 12.4 us  [call(): pl.pallas_call(kernel, out_shape=[pltpu.VMEM(shape, dtype) for shape, dty...]
  transfers between devices with their start and end apart: 11 -> 11, of which waited for: 7 -> 7; matrix products, arithmetic and copies ran while one was open for 0% -> 0% of each run, Pallas kernels for 15% -> 17%
where the time goes in v3:
time: 44.6 us; the launch traced here: 44.5 us
  blocking collectives  13.9 us (31%)
  Pallas kernels  13.1 us (29%)
  starting transfers between devices  11.6 us (26%)
  waiting for transfers between devices  5.83 us (13%)
    all_to_all x1, blocking collectives, body(): returned = lax.all_to_all(blocks, ('grp', 'tp'), 0, 0, tiled=True)  13.9 us
    pallas_call x13, Pallas kernels, call(): pl.pallas_call(kernel, out_shape=[pltpu.VMEM(shape, dtype) for shape, dty...  12.4 us
    ppermute x7, starting transfers between devices, swapped(): return lax.ppermute(value, axis, pairs)  8.19 us
    ppermute x7, waiting for transfers between devices, swapped(): return lax.ppermute(value, axis, pairs)  4.27 us
    ppermute x4, starting transfers between devices, crossed(): return lax.ppermute(value, ('side', 'grp', 'tp'), pairs)  3.39 us
    ppermute x4, waiting for transfers between devices, crossed(): return lax.ppermute(value, ('side', 'grp', 'tp'), pairs)  1.56 us
  transfers between devices with their start and end apart: 11, of which 7 were waited for; matrix products, arithmetic and copies ran while one was open for 0% of the time, Pallas kernels for 17%

profile of v3, /device:TPU:0, one launch (start us, length us, event | category | flops | bytes accessed | tf_op | source)
XLA Modules:
  0.0 44.5 jit_solution(5083907593395053965)
XLA Ops:
  0.0 3.1 %attention.1 = (f32[24,640]{1,0:T(8,128)S(1)}, bf16[24,640]{1,0:T(8,128)(2,1)S(1)}, bf16[24,128]{1,0:T(8,128)(2,1)S(1)}) custom-call(bf16[24,2048]{1,0:T(8,128)(2,1)} %refs_0_.4, s32[24]{0:T(128)} %refs_1_.2, s32[8,24]{1,0:T(8,128)} %bitcast.4, f32[8,24]{1,0:T(8,128)} %bitcast.5, bf16[24,1,384,256]{3,2,1,0:T(8,128)(2,1)} %refs_4_.1), custom_call_target="tpu_custom_call" | custom-call | tf_op jit(solution)/shard_map/attention/pallas_call | solution.py:45
  3.2 3.1 %collective-permute-start = (bf16[24,640]{1,0:T(8,128)(2,1)S(1)}, bf16[24,640]{1,0:T(8,128)(2,1)S(1)}, u32[]{:S(2)}, u32[]{:S(2)}) collective-permute-start(bf16[24,640]{1,0:T(8,128)(2,1)S(1)} %get-tuple-element.28), channel_id=1, source_target_pairs={{0,1},{1,0},{2,3},{3,2},{4,5},{5,4},{6,7},{7,6},{8,9},{9,8},{10,11... | collective-permute-start | bytes 92168 | tf_op jit(solution)/shard_map/ppermute | solution.py:25
  6.2 1.6 %fetch.3 = (bf16[512,2048]{1,0:T(8,128)(2,1)S(1)}, bf16[24,2048]{1,0:T(8,128)(2,1)S(1)}, f32[1,2048]{1,0:T(1,128)S(1)}, bf16[24,128]{1,0:T(8,128)(2,1)S(1)}) custom-call(bf16[24,128]{1,0:T(8,128)(2,1)S(1)} %get-tuple-element.24.after_ref.lanes_ref, bf16[512,2048]{1,0:T(8,128)(2,1)} %refs_0_.5, bf16[24,2048]{1,0:T(8,128)(2,1)} %refs_1_.3, f32[1,2048]{1,0:T(1,128)} %bitcast.3), custom_call_target="tpu_custom_call" | custom-call | bytes 4407296 | tf_op jit(solution)/shard_map/fetch/pallas_call | solution.py:45
  7.8 0.3 collective-permute-done.rest_1_
  8.1 0.5 %project.1 = (bf16[24,512]{1,0:T(8,128)(2,1)S(1)}, bf16[24,1024]{1,0:T(8,128)(2,1)S(1)}) custom-call(bf16[24,128]{1,0:T(8,128)(2,1)S(1)} %get-tuple-element.25.token_ref, bf16[512,2048]{1,0:T(8,128)(2,1)S(1)} %get-tuple-element.26.weight_ref, f32[24,640]{1,0:T(8,128)S(1)} %get-tuple-element.27.rest_0_, bf16[24,640]{1,0:T(8,128)(2,1)S(1)} %collective-permute-done.rest_1_), custom_call_target="tpu_custom_call" | custom-call | tf_op jit(solution)/shard_map/project/pallas_call | solution.py:45
  8.6 0.0 collective-permute-start.1
  8.6 0.3 kept.1.kept_ref
  8.9 0.9 %collective-permute-done.1.came_ref = bf16[24,1024]{1,0:T(8,128)(2,1)S(1)} collective-permute-done((bf16[24,1024]{1,0:T(8,128)(2,1)S(1)}, bf16[24,1024]{1,0:T(8,128)(2,1)S(1)}, u32[]{:S(2)}, u32[]{:S(2)}) %collective-permute-start.1) | collective-permute-done | bytes 49184 | tf_op jit(solution)/shard_map/ppermute | solution.py:25
  9.9 4.1 %collective-permute-start.4 = (bf16[24,1024]{1,0:T(8,128)(2,1)S(1)}, bf16[24,1024]{1,0:T(8,128)(2,1)S(1)}, u32[]{:S(2)}, u32[]{:S(2)}) collective-permute-start(bf16[24,1024]{1,0:T(8,128)(2,1)S(1)} %pair.1.after_ref.rest_0_), channel_id=1, source_target_pairs={{0,3},{1,2},{2,1},{3,0},{4,7},{5,6},{6,5},{7,4},{8,11},{9,10},{10,... | collective-permute-start | bytes 147464 | tf_op jit(solution)/shard_map/ppermute | solution.py:25
  14.0 0.0 collective-permute-start.3
  14.0 0.6 %collective-permute-start.2 = (bf16[24,1024]{1,0:T(8,128)(2,1)S(1)}, bf16[24,1024]{1,0:T(8,128)(2,1)S(1)}, u32[]{:S(2)}, u32[]{:S(2)}) collective-permute-start(bf16[24,1024]{1,0:T(8,128)(2,1)S(1)} %pair.1.after_ref.rest_0_), channel_id=1, source_target_pairs={{0,1},{1,0},{2,3},{3,2},{4,5},{5,4},{6,7},{7,6},{8,9},{9,8},{10,11... | collective-permute-start | bytes 147464 | tf_op jit(solution)/shard_map/ppermute | solution.py:25
  14.6 2.9 %fetch.4 = (bf16[1,2048,1536]{2,1,0:T(8,128)(2,1)S(1)}, bf16[24,128]{1,0:T(8,128)(2,1)S(1)}) custom-call(bf16[24,1024]{1,0:T(8,128)(2,1)S(1)} %pair.1.after_ref.rest_0_, bf16[1,2048,1536]{2,1,0:T(8,128)(2,1)} %refs_0_.6), custom_call_target="tpu_custom_call" | custom-call | bytes 12582912 | tf_op jit(solution)/shard_map/fetch/pallas_call | solution.py:45
  17.5 0.0 collective-permute-done.4.rest_3_
  17.5 1.5 %collective-permute-done.3.rest_2_ = bf16[24,1024]{1,0:T(8,128)(2,1)S(1)} collective-permute-done((bf16[24,1024]{1,0:T(8,128)(2,1)S(1)}, bf16[24,1024]{1,0:T(8,128)(2,1)S(1)}, u32[]{:S(2)}, u32[]{:S(2)}) %collective-permute-start.3) | collective-permute-done | bytes 49184 | tf_op jit(solution)/shard_map/ppermute | solution.py:25
  19.0 0.0 collective-permute-done.2.rest_1_
  19.0 1.4 %collective-permute-start.8 = (bf16[24,1152]{1,0:T(8,128)(2,1)S(1)}, bf16[24,1152]{1,0:T(8,128)(2,1)S(1)}, u32[]{:S(2)}, u32[]{:S(2)}) collective-permute-start(bf16[24,1152]{1,0:T(8,128)(2,1)S(1)} %middle.1.after_ref.middle_ref), channel_id=1, source_target_pairs={{0,28},{1,29},{2,30},{3,31},{4,24},{5,25},{6,26},{7,27},{8,20},{9,... | collective-permute-start | bytes 165896 | tf_op jit(solution)/shard_map/ppermute | solution.py:36
  20.4 1.3 %collective-permute-start.7 = (bf16[24,1152]{1,0:T(8,128)(2,1)S(1)}, bf16[24,1152]{1,0:T(8,128)(2,1)S(1)}, u32[]{:S(2)}, u32[]{:S(2)}) collective-permute-start(bf16[24,1152]{1,0:T(8,128)(2,1)S(1)} %middle.1.after_ref.middle_ref), channel_id=1, source_target_pairs={{0,24},{1,25},{2,26},{3,27},{4,28},{5,29},{6,30},{7,31},{8,16},{9,... | collective-permute-start | bytes 165896 | tf_op jit(solution)/shard_map/ppermute | solution.py:36
  21.7 0.1 collective-permute-start.6
  21.9 0.5 %collective-permute-start.5 = (bf16[24,1152]{1,0:T(8,128)(2,1)S(1)}, bf16[24,1152]{1,0:T(8,128)(2,1)S(1)}, u32[]{:S(2)}, u32[]{:S(2)}) collective-permute-start(bf16[24,1152]{1,0:T(8,128)(2,1)S(1)} %middle.1.after_ref.middle_ref), channel_id=1, source_target_pairs={{0,16},{1,17},{2,18},{3,19},{4,20},{5,21},{6,22},{7,23},{8,24},{9,... | collective-permute-start | bytes 165896 | tf_op jit(solution)/shard_map/ppermute | solution.py:36
  22.4 1.9 %fetch.5 = (bf16[1,768,2048]{2,1,0:T(8,128)(2,1)S(1)}, bf16[24,128]{1,0:T(8,128)(2,1)S(1)}) custom-call(bf16[24,1152]{1,0:T(8,128)(2,1)S(1)} %middle.1.after_ref.middle_ref, bf16[1,768,2048]{2,1,0:T(8,128)(2,1)} %refs_0_.7), custom_call_target="tpu_custom_call" | custom-call | bytes 6291456 | tf_op jit(solution)/shard_map/fetch/pallas_call | solution.py:45
  24.3 0.0 collective-permute-done.8.rest_3_
  24.3 0.4 collective-permute-done.7.rest_2_
  24.7 1.1 %collective-permute-done.6.rest_1_ = bf16[24,1152]{1,0:T(8,128)(2,1)S(1)} collective-permute-done((bf16[24,1152]{1,0:T(8,128)(2,1)S(1)}, bf16[24,1152]{1,0:T(8,128)(2,1)S(1)}, u32[]{:S(2)}, u32[]{:S(2)}) %collective-permute-start.6) | collective-permute-done | bytes 55328 | tf_op jit(solution)/shard_map/ppermute | solution.py:36
  25.8 0.0 collective-permute-done.5.rest_0_
  25.8 0.1 gather.1
  25.9 0.1 collective-permute-start.9
  26.1 0.6 %first_half.1 = (f32[96,1536]{1,0:T(8,128)S(1)}, f32[96,128]{1,0:T(8,128)S(1)}) custom-call(bf16[4,24,1024]{2,1,0:T(8,128)(2,1)S(1)} %get-tuple-element.34.x_ref, f32[1,2048]{1,0:T(1,128)S(1)} %get-tuple-element.35.gain_ref, bf16[1,2048,1536]{2,1,0:T(8,128)(2,1)S(1)} %get-tuple-element.36.w_ref), custom_call_target="tpu_custom_call" | custom-call | tf_op jit(solution)/shard_map/first_half/pallas_call | solution.py:45
  26.7 0.7 %collective-permute-done.9.x_ref = bf16[4,24,1024]{2,1,0:T(8,128)(2,1)S(1)} collective-permute-done((bf16[4,24,1024]{2,1,0:T(8,128)(2,1)S(1)}, bf16[4,24,1024]{2,1,0:T(8,128)(2,1)S(1)}, u32[]{:S(2)}, u32[]{:S(2)}) %collective-permute-start.9) | collective-permute-done | bytes 196640 | tf_op jit(solution)/shard_map/ppermute | solution.py:25
  27.4 1.0 %second_half.1 = (bf16[96,768]{1,0:T(8,128)(2,1)S(1)}, bf16[96,1024]{1,0:T(8,128)(2,1)S(1)}) custom-call(bf16[4,24,1024]{2,1,0:T(8,128)(2,1)S(1)} %collective-permute-done.9.x_ref, f32[1,2048]{1,0:T(1,128)S(1)} %get-tuple-element.35.gain_ref, bf16[1,2048,1536]{2,1,0:T(8,128)(2,1)S(1)} %get-tuple-element.36.w_ref, ...), custom_call_target="tpu_custom_call" | custom-call | tf_op jit(solution)/shard_map/second_half/pallas_call | solution.py:45
  28.4 0.2 collective-permute-start.10
  28.6 0.4 keep.1.kept_ref
  29.0 0.9 %collective-permute-done.10.came_ref = bf16[96,1024]{1,0:T(8,128)(2,1)S(1)} collective-permute-done((bf16[96,1024]{1,0:T(8,128)(2,1)S(1)}, bf16[96,1024]{1,0:T(8,128)(2,1)S(1)}, u32[]{:S(2)}, u32[]{:S(2)}) %collective-permute-start.10) | collective-permute-done | bytes 196640 | tf_op jit(solution)/shard_map/ppermute | solution.py:25
  29.9 13.9 %all_to_all.5.blocks_ref = bf16[16,24,256]{2,1,0:T(8,128)(2,1)S(1)} all-to-all(bf16[16,24,256]{2,1,0:T(8,128)(2,1)S(1)} %blocks.1), channel_id=1, replica_groups=mesh['side'=2,'grp'=4,'tp'=4] {'grp','tp'}, dimensions={0} | all-to-all | bytes 393216 | tf_op jit(solution)/shard_map/all_to_all | solution.py:435
  43.8 0.6 %final.1 = bf16[24,256]{1,0:T(8,128)(2,1)} custom-call(bf16[16,24,256]{2,1,0:T(8,128)(2,1)S(1)} %all_to_all.5.blocks_ref, bf16[24,1152]{1,0:T(8,128)(2,1)S(1)} %middle.1.after_ref.middle_ref), custom_call_target="tpu_custom_call" | custom-call | tf_op jit(solution)/shard_map/final/pallas_call | solution.py:436
  (3 shorter events, 0.1 us)
Async XLA Ops:
  3.2 5.0 %collective-permute-start = (bf16[24,640]{1,0:T(8,128)(2,1)S(1)}, bf16[24,640]{1,0:T(8,128)(2,1)S(1)}, u32[]{:S(2)}, u32[]{:S(2)}) collective-permute-start(bf16[24,640]{1,0:T(8,128)(2,1)S(1)} %get-tuple-element.28), channel_id=1, source_target_pairs={{0,1},{1,0},{2,3},{3,2},{4,5},{5,4},{6,7},{7,6},{8,9},{9,8},{10,11... | collective-permute-start | bytes 92168 | tf_op jit(solution)/shard_map/ppermute | solution.py:25
  8.6 1.2 %collective-permute-start.1 = (bf16[24,1024]{1,0:T(8,128)(2,1)S(1)}, bf16[24,1024]{1,0:T(8,128)(2,1)S(1)}, u32[]{:S(2)}, u32[]{:S(2)}) collective-permute-start(bf16[24,1024]{1,0:T(8,128)(2,1)S(1)} %get-tuple-element.30), channel_id=1, source_target_pairs={{0,16},{16,0},{1,17},{17,1},{2,18},{18,2},{3,19},{19,3},{4,20},{20... | collective-permute-start | bytes 147464 | tf_op jit(solution)/shard_map/ppermute | solution.py:25
  9.9 7.6 %collective-permute-start.4 = (bf16[24,1024]{1,0:T(8,128)(2,1)S(1)}, bf16[24,1024]{1,0:T(8,128)(2,1)S(1)}, u32[]{:S(2)}, u32[]{:S(2)}) collective-permute-start(bf16[24,1024]{1,0:T(8,128)(2,1)S(1)} %pair.1.after_ref.rest_0_), channel_id=1, source_target_pairs={{0,3},{1,2},{2,1},{3,0},{4,7},{5,6},{6,5},{7,4},{8,11},{9,10},{10,... | collective-permute-start | bytes 147464 | tf_op jit(solution)/shard_map/ppermute | solution.py:25
  14.0 5.0 %collective-permute-start.3 = (bf16[24,1024]{1,0:T(8,128)(2,1)S(1)}, bf16[24,1024]{1,0:T(8,128)(2,1)S(1)}, u32[]{:S(2)}, u32[]{:S(2)}) collective-permute-start(bf16[24,1024]{1,0:T(8,128)(2,1)S(1)} %pair.1.after_ref.rest_0_), channel_id=1, source_target_pairs={{0,2},{1,3},{2,0},{3,1},{4,6},{5,7},{6,4},{7,5},{8,10},{9,11},{10,... | collective-permute-start | bytes 147464 | tf_op jit(solution)/shard_map/ppermute | solution.py:25
  14.0 5.0 %collective-permute-start.2 = (bf16[24,1024]{1,0:T(8,128)(2,1)S(1)}, bf16[24,1024]{1,0:T(8,128)(2,1)S(1)}, u32[]{:S(2)}, u32[]{:S(2)}) collective-permute-start(bf16[24,1024]{1,0:T(8,128)(2,1)S(1)} %pair.1.after_ref.rest_0_), channel_id=1, source_target_pairs={{0,1},{1,0},{2,3},{3,2},{4,5},{5,4},{6,7},{7,6},{8,9},{9,8},{10,11... | collective-permute-start | bytes 147464 | tf_op jit(solution)/shard_map/ppermute | solution.py:25
  19.0 5.3 %collective-permute-start.8 = (bf16[24,1152]{1,0:T(8,128)(2,1)S(1)}, bf16[24,1152]{1,0:T(8,128)(2,1)S(1)}, u32[]{:S(2)}, u32[]{:S(2)}) collective-permute-start(bf16[24,1152]{1,0:T(8,128)(2,1)S(1)} %middle.1.after_ref.middle_ref), channel_id=1, source_target_pairs={{0,28},{1,29},{2,30},{3,31},{4,24},{5,25},{6,26},{7,27},{8,20},{9,... | collective-permute-start | bytes 165896 | tf_op jit(solution)/shard_map/ppermute | solution.py:36
  20.4 4.3 %collective-permute-start.7 = (bf16[24,1152]{1,0:T(8,128)(2,1)S(1)}, bf16[24,1152]{1,0:T(8,128)(2,1)S(1)}, u32[]{:S(2)}, u32[]{:S(2)}) collective-permute-start(bf16[24,1152]{1,0:T(8,128)(2,1)S(1)} %middle.1.after_ref.middle_ref), channel_id=1, source_target_pairs={{0,24},{1,25},{2,26},{3,27},{4,28},{5,29},{6,30},{7,31},{8,16},{9,... | collective-permute-start | bytes 165896 | tf_op jit(solution)/shard_map/ppermute | solution.py:36
  21.7 4.1 %collective-permute-start.6 = (bf16[24,1152]{1,0:T(8,128)(2,1)S(1)}, bf16[24,1152]{1,0:T(8,128)(2,1)S(1)}, u32[]{:S(2)}, u32[]{:S(2)}) collective-permute-start(bf16[24,1152]{1,0:T(8,128)(2,1)S(1)} %middle.1.after_ref.middle_ref), channel_id=1, source_target_pairs={{0,20},{1,21},{2,22},{3,23},{4,16},{5,17},{6,18},{7,19},{8,28},{9,... | collective-permute-start | bytes 165896 | tf_op jit(solution)/shard_map/ppermute | solution.py:36
  21.9 4.0 %collective-permute-start.5 = (bf16[24,1152]{1,0:T(8,128)(2,1)S(1)}, bf16[24,1152]{1,0:T(8,128)(2,1)S(1)}, u32[]{:S(2)}, u32[]{:S(2)}) collective-permute-start(bf16[24,1152]{1,0:T(8,128)(2,1)S(1)} %middle.1.after_ref.middle_ref), channel_id=1, source_target_pairs={{0,16},{1,17},{2,18},{3,19},{4,20},{5,21},{6,22},{7,23},{8,24},{9,... | collective-permute-start | bytes 165896 | tf_op jit(solution)/shard_map/ppermute | solution.py:36
  25.9 1.4 %collective-permute-start.9 = (bf16[4,24,1024]{2,1,0:T(8,128)(2,1)S(1)}, bf16[4,24,1024]{2,1,0:T(8,128)(2,1)S(1)}, u32[]{:S(2)}, u32[]{:S(2)}) collective-permute-start(bf16[4,24,1024]{2,1,0:T(8,128)(2,1)S(1)} %get-tuple-element.34.x_ref), channel_id=1, source_target_pairs={{0,16},{16,0},{1,17},{17,1},{2,18},{18,2},{3,19},{19,3},{4,20},{20... | collective-permute-start | bytes 589832 | tf_op jit(solution)/shard_map/ppermute | solution.py:25
  28.4 1.5 %collective-permute-start.10 = (bf16[96,1024]{1,0:T(8,128)(2,1)S(1)}, bf16[96,1024]{1,0:T(8,128)(2,1)S(1)}, u32[]{:S(2)}, u32[]{:S(2)}) collective-permute-start(bf16[96,1024]{1,0:T(8,128)(2,1)S(1)} %get-tuple-element.42), channel_id=1, source_target_pairs={{0,16},{16,0},{1,17},{17,1},{2,18},{18,2},{3,19},{19,3},{4,20},{20... | collective-permute-start | bytes 589832 | tf_op jit(solution)/shard_map/ppermute | solution.py:25

commit v4 on v3

--- a/solution.py
+++ b/solution.py
@@ -25,10 +25,10 @@
     return lax.ppermute(value, axis, pairs)
 
 
-def crossed(value, mask):
+def crossed(value, mask, along=0):
     grp, tp = lax.axis_size("grp"), lax.axis_size("tp")
     pairs = [
-        ((s * grp + g) * tp + t, ((1 - s) * grp + (g ^ mask)) * tp + t)
+        ((s * grp + g) * tp + t, ((1 - s) * grp + (g ^ mask)) * tp + (t ^ along))
         for s in range(2)
         for g in range(grp)
         for t in range(tp)
@@ -218,30 +218,22 @@
     out_ref[:, half:] = lanes_ref[...]
 
 
-def gather_kernel(half, token_ref, *rest):
-    *packets, x_ref, gate_ref = rest
-    me = lax.axis_index("grp")
-    for mask, packet in enumerate(packets):
-        x_ref[me ^ mask] = packet[:, :half]
-        lane = lax.broadcasted_iota(jnp.int32, (packet.shape[0], HD), 1)
-        picked = jnp.where(lane % (HD // 2) == me, packet[:, half:].astype(F32), 0.0)
-        gate_ref[me ^ mask] = jnp.broadcast_to(
-            jnp.sum(picked, axis=1, keepdims=True), (packet.shape[0], HD)
-        )
-
-
-def scaled_rows(x_ref, gain_ref, side, half):
-    groups, rows, _ = x_ref.shape
-    x = x_ref[...].astype(F32).reshape(groups * rows, half)
+def scaled_rows(packets, gain_ref, side, half):
+    x = jnp.concatenate([p[:, :half].astype(F32) for p in packets], axis=0)
     gain = gain_ref[:, pl.ds(pl.multiple_of(side * half, half), half)]
     return (x * gain).astype(BF16), jnp.sum(x * x, axis=1, keepdims=True)
 
 
-def first_half_kernel(tile, x_ref, gain_ref, w_ref, hidden_ref, square_ref):
-    half = x_ref.shape[2]
+def first_half_kernel(tile, half, gain_ref, w_ref, *rest):
+    *packets, hidden_ref, square_ref, gate_ref = rest
     section = lax.axis_index("side")
-    x, square = scaled_rows(x_ref, gain_ref, 1 - section, half)
+    me = lax.axis_index("grp")
+    x, square = scaled_rows(packets, gain_ref, 1 - section, half)
     square_ref[...] = jnp.broadcast_to(square, square_ref.shape)
+    lanes = jnp.concatenate([p[:, half:].astype(F32) for p in packets], axis=0)
+    lane = lax.broadcasted_iota(jnp.int32, lanes.shape, 1)
+    gate = jnp.sum(jnp.where(lane % (HD // 2) == me, lanes, 0.0), axis=1, keepdims=True)
+    gate_ref[...] = jnp.broadcast_to(gate, gate_ref.shape)
     rows = pl.ds(pl.multiple_of((1 - section) * half, half), half)
 
     def column(j, carry):
@@ -254,12 +246,12 @@
 
 
 def second_half_kernel(
-    tile, x_ref, gain_ref, w_ref, hidden_ref, square_ref, gate_ref, down_ref, act_ref, away_ref
+    tile, half, gain_ref, w_ref, hidden_ref, square_ref, gate_ref, down_ref, *rest
 ):
-    half = x_ref.shape[2]
+    *packets, act_ref, away_ref = rest
     inner = act_ref.shape[1]
     section = lax.axis_index("side")
-    x, square = scaled_rows(x_ref, gain_ref, section, half)
+    x, square = scaled_rows(packets, gain_ref, section, half)
     square = square + square_ref[:, :1]
     inv = lax.rsqrt(square / (half * lax.axis_size("side")) + 1e-6)
     rows = pl.ds(pl.multiple_of(section * half, half), half)
@@ -281,7 +273,7 @@
 
 def down(tile, act_ref, gate_ref, down_ref, out_ref, side):
     half = out_ref.shape[1]
-    gate = gate_ref[...].reshape(act_ref.shape[0], HD)[:, :1]
+    gate = gate_ref[:, :1]
 
     def column(j, carry):
         at = pl.ds(pl.multiple_of(side * half + j * tile, HD), tile)
@@ -299,20 +291,31 @@
     down(tile, act_ref, gate_ref, down_ref, kept_ref, lax.axis_index("side"))
 
 
-def blocks_kernel(kept_ref, came_ref, out_ref):
-    blocks, rows, piece = out_ref.shape
-    tp = kept_ref.shape[1] // piece
-    for b in range(blocks):
-        at = (slice(b // tp * rows, (b // tp + 1) * rows), slice(b % tp * piece, (b % tp + 1) * piece))
-        out_ref[b] = (kept_ref[at] + came_ref[at].astype(F32)).astype(BF16)
-
-
-def final_kernel(blocks_ref, middle_ref, out_ref):
-    blocks, rows, piece = blocks_ref.shape
+def fold_kernel(rows, kept_ref, came_ref, *sends):
+    for b, ref in enumerate(sends):
+        at = slice(b * rows, (b + 1) * rows)
+        ref[...] = (kept_ref[at, :] + came_ref[at, :].astype(F32)).astype(BF16)
+
+
+def split_kernel(count, *refs):
+    parts, sends = refs[:count], refs[count:]
+    piece = sends[0].shape[1]
+    me = lax.axis_index("tp")
+    for mask, ref in enumerate(sends):
+        at = pl.ds(pl.multiple_of((me ^ mask) * piece, piece), piece)
+        total = parts[0][:, at].astype(F32)
+        for part in parts[1:]:
+            total = total + part[:, at].astype(F32)
+        ref[...] = total.astype(BF16)
+
+
+def final_kernel(middle_ref, *rest):
+    *parts, out_ref = rest
+    piece = out_ref.shape[1]
     at = pl.ds(pl.multiple_of(lax.axis_index("tp") * piece, piece), piece)
     total = middle_ref[:, at].astype(F32)
-    for b in range(blocks):
-        total = total + blocks_ref[b].astype(F32)
+    for part in parts:
+        total = total + part[...].astype(F32)
     out_ref[...] = total.astype(BF16)
 
 
@@ -398,27 +401,20 @@
         [((rows, half + HD), BF16)],
         name="middle",
     )[0]
-    w_down, token = fetched(middle, w_down)
     packets = [crossed(middle, mask) for mask in [*range(1, grp), 0]]
     packets = [packets[-1], *packets[:-1]]
-    far_half, gate = call(
-        functools.partial(gather_kernel, half),
-        [token, *packets],
-        [((grp, rows, half), BF16), ((grp, rows, HD), F32)],
-        name="gather",
-    )
-    near_half = swapped(far_half, "side", 1)
+    near_packets = [middle] + [swapped(p, "side", 1) for p in packets[1:]]
     total = grp * rows
     tile = 256
-    hidden, square = call(
-        functools.partial(first_half_kernel, tile),
-        [far_half, gain, w_gate_up],
-        [((total, 2 * inner), F32), ((total, HD), F32)],
+    hidden, square, gate = call(
+        functools.partial(first_half_kernel, tile, half),
+        [gain, w_gate_up, *packets],
+        [((total, 2 * inner), F32), ((total, HD), F32), ((total, HD), F32)],
         name="first_half",
     )
     act, sent = call(
-        functools.partial(second_half_kernel, tile),
-        [near_half, gain, w_gate_up, hidden, square, gate, w_down],
+        functools.partial(second_half_kernel, tile, half),
+        [gain, w_gate_up, hidden, square, gate, w_down, *near_packets],
         [((total, inner), BF16), ((total, half), BF16)],
         name="second_half",
     )
@@ -429,17 +425,28 @@
         [((total, half), F32)],
         name="keep",
     )[0]
-    blocks = call(
-        blocks_kernel, [mine, back], [((grp * tp, rows, piece), BF16)], name="blocks"
-    )[0]
-    returned = lax.all_to_all(blocks, ("grp", "tp"), 0, 0, tiled=True)
+    sends = call(
+        functools.partial(fold_kernel, rows),
+        [mine, back],
+        [((rows, half), BF16)] * grp,
+        name="fold",
+    )
+    came = [crossed(sends[mask], mask) for mask in reversed(range(grp))]
+    sends = call(
+        functools.partial(split_kernel, grp),
+        came,
+        [((rows, piece), BF16)] * tp,
+        name="split",
+    )
+    came = [crossed(sends[mask], 0, mask) for mask in reversed(range(tp))]
+    ins = [middle, *came]
     return pl.pallas_call(
         final_kernel,
         out_shape=jax.ShapeDtypeStruct((rows, piece), BF16),
-        in_specs=[VMEM_SPEC] * 2,
+        in_specs=[VMEM_SPEC] * len(ins),
         out_specs=VMEM_SPEC,
         name="final",
-    )(near(returned), near(middle))
+    )(*map(near, ins))
 
 
 def solution(mesh):

time: 44.6 us -> 42.6 us (0.955)
  blocking collectives: 13.9 us -> 0 us
  starting transfers between devices: 11.6 us -> 20.1 us
  waiting for transfers between devices: 5.83 us -> 11.1 us
  Pallas kernels: 13.1 us -> 11.1 us
    all_to_all x1 -> x0, blocking collectives: 13.9 us -> none  [body(): returned = lax.all_to_all(blocks, ('grp', 'tp'), 0, 0, tiled=True)]
    ppermute x4 -> x12, starting transfers between devices: 3.39 us -> 11.1 us  [crossed(): return lax.ppermute(value, ('side', 'grp', 'tp'), pairs)]
    ppermute x4 -> x12, waiting for transfers between devices: 1.56 us -> 7.06 us  [crossed(): return lax.ppermute(value, ('side', 'grp', 'tp'), pairs)]
    pallas_call x13 -> x12, Pallas kernels: 12.4 us -> 10.5 us  [call(): pl.pallas_call(kernel, out_shape=[pltpu.VMEM(shape, dtype) for shape, dty...]
    ppermute x7 -> x9, starting transfers between devices: 8.19 us -> 9.03 us  [swapped(): return lax.ppermute(value, axis, pairs)]
    ppermute x7 -> x9, waiting for transfers between devices: 4.27 us -> 4.01 us  [swapped(): return lax.ppermute(value, axis, pairs)]
  transfers between devices with their start and end apart: 11 -> 21, of which waited for: 7 -> 12; matrix products, arithmetic and copies ran while one was open for 0% -> 0% of each run, Pallas kernels for 17% -> 14%
where the time goes in v4:
time: 42.6 us; the launch traced here: 42.4 us
  starting transfers between devices  20.1 us (47%)
  Pallas kernels  11.1 us (26%)
  waiting for transfers between devices  11.1 us (26%)
    ppermute x12, starting transfers between devices, crossed(): return lax.ppermute(value, ('side', 'grp', 'tp'), pairs)  11.1 us
    pallas_call x12, Pallas kernels, call(): pl.pallas_call(kernel, out_shape=[pltpu.VMEM(shape, dtype) for shape, dty...  10.5 us
    ppermute x9, starting transfers between devices, swapped(): return lax.ppermute(value, axis, pairs)  9.03 us
    ppermute x12, waiting for transfers between devices, crossed(): return lax.ppermute(value, ('side', 'grp', 'tp'), pairs)  7.06 us
    ppermute x9, waiting for transfers between devices, swapped(): return lax.ppermute(value, axis, pairs)  4.01 us
  transfers between devices with their start and end apart: 21, of which 12 were waited for; matrix products, arithmetic and copies ran while one was open for 0% of the time, Pallas kernels for 14%

profile of v4, /device:TPU:0, one launch (start us, length us, event | category | flops | bytes accessed | tf_op | source)
XLA Modules:
  0.0 42.4 jit_solution(7928859321464321881)
XLA Ops:
  0.0 3.1 %attention.1 = (f32[24,640]{1,0:T(8,128)S(1)}, bf16[24,640]{1,0:T(8,128)(2,1)S(1)}, bf16[24,128]{1,0:T(8,128)(2,1)S(1)}) custom-call(bf16[24,2048]{1,0:T(8,128)(2,1)} %refs_0_.3, s32[24]{0:T(128)} %refs_1_.2, s32[8,24]{1,0:T(8,128)} %bitcast.4, f32[8,24]{1,0:T(8,128)} %bitcast.5, bf16[24,1,384,256]{3,2,1,0:T(8,128)(2,1)} %refs_4_.1), custom_call_target="tpu_custom_call" | custom-call | tf_op jit(solution)/shard_map/attention/pallas_call | solution.py:45
  3.2 3.1 %collective-permute-start = (bf16[24,640]{1,0:T(8,128)(2,1)S(1)}, bf16[24,640]{1,0:T(8,128)(2,1)S(1)}, u32[]{:S(2)}, u32[]{:S(2)}) collective-permute-start(bf16[24,640]{1,0:T(8,128)(2,1)S(1)} %get-tuple-element.33), channel_id=1, source_target_pairs={{0,1},{1,0},{2,3},{3,2},{4,5},{5,4},{6,7},{7,6},{8,9},{9,8},{10,11... | collective-permute-start | bytes 92168 | tf_op jit(solution)/shard_map/ppermute | solution.py:25
  6.2 1.6 %fetch.2 = (bf16[512,2048]{1,0:T(8,128)(2,1)S(1)}, bf16[24,2048]{1,0:T(8,128)(2,1)S(1)}, f32[1,2048]{1,0:T(1,128)S(1)}, bf16[24,128]{1,0:T(8,128)(2,1)S(1)}) custom-call(bf16[24,128]{1,0:T(8,128)(2,1)S(1)} %get-tuple-element.29.after_ref.lanes_ref, bf16[512,2048]{1,0:T(8,128)(2,1)} %refs_0_.4, bf16[24,2048]{1,0:T(8,128)(2,1)} %refs_1_.3, f32[1,2048]{1,0:T(1,128)} %bitcast.3), custom_call_target="tpu_custom_call" | custom-call | bytes 4407296 | tf_op jit(solution)/shard_map/fetch/pallas_call | solution.py:45
  7.8 0.3 collective-permute-done.rest_1_
  8.1 0.5 %project.1 = (bf16[24,512]{1,0:T(8,128)(2,1)S(1)}, bf16[24,1024]{1,0:T(8,128)(2,1)S(1)}) custom-call(bf16[24,128]{1,0:T(8,128)(2,1)S(1)} %get-tuple-element.30.token_ref, bf16[512,2048]{1,0:T(8,128)(2,1)S(1)} %get-tuple-element.31.weight_ref, f32[24,640]{1,0:T(8,128)S(1)} %get-tuple-element.32.rest_0_, bf16[24,640]{1,0:T(8,128)(2,1)S(1)} %collective-permute-done.rest_1_), custom_call_target="tpu_custom_call" | custom-call | tf_op jit(solution)/shard_map/project/pallas_call | solution.py:45
  8.6 0.0 collective-permute-start.1
  8.6 0.3 kept.1.kept_ref
  8.9 0.9 %collective-permute-done.1.came_ref = bf16[24,1024]{1,0:T(8,128)(2,1)S(1)} collective-permute-done((bf16[24,1024]{1,0:T(8,128)(2,1)S(1)}, bf16[24,1024]{1,0:T(8,128)(2,1)S(1)}, u32[]{:S(2)}, u32[]{:S(2)}) %collective-permute-start.1) | collective-permute-done | bytes 49184 | tf_op jit(solution)/shard_map/ppermute | solution.py:25
  9.9 4.1 %collective-permute-start.4 = (bf16[24,1024]{1,0:T(8,128)(2,1)S(1)}, bf16[24,1024]{1,0:T(8,128)(2,1)S(1)}, u32[]{:S(2)}, u32[]{:S(2)}) collective-permute-start(bf16[24,1024]{1,0:T(8,128)(2,1)S(1)} %pair.1.after_ref.rest_0_), channel_id=1, source_target_pairs={{0,3},{1,2},{2,1},{3,0},{4,7},{5,6},{6,5},{7,4},{8,11},{9,10},{10,... | collective-permute-start | bytes 147464 | tf_op jit(solution)/shard_map/ppermute | solution.py:25
  14.0 0.0 collective-permute-start.3
  14.0 0.6 %collective-permute-start.2 = (bf16[24,1024]{1,0:T(8,128)(2,1)S(1)}, bf16[24,1024]{1,0:T(8,128)(2,1)S(1)}, u32[]{:S(2)}, u32[]{:S(2)}) collective-permute-start(bf16[24,1024]{1,0:T(8,128)(2,1)S(1)} %pair.1.after_ref.rest_0_), channel_id=1, source_target_pairs={{0,1},{1,0},{2,3},{3,2},{4,5},{5,4},{6,7},{7,6},{8,9},{9,8},{10,11... | collective-permute-start | bytes 147464 | tf_op jit(solution)/shard_map/ppermute | solution.py:25
  14.6 2.9 %fetch.3 = (bf16[1,2048,1536]{2,1,0:T(8,128)(2,1)S(1)}, bf16[24,128]{1,0:T(8,128)(2,1)S(1)}) custom-call(bf16[24,1024]{1,0:T(8,128)(2,1)S(1)} %pair.1.after_ref.rest_0_, bf16[1,2048,1536]{2,1,0:T(8,128)(2,1)} %refs_0_.5), custom_call_target="tpu_custom_call" | custom-call | bytes 12582912 | tf_op jit(solution)/shard_map/fetch/pallas_call | solution.py:45
  17.5 0.0 copy-start
  17.5 0.0 collective-permute-done.4.rest_3_
  17.5 1.4 %collective-permute-done.3.rest_2_ = bf16[24,1024]{1,0:T(8,128)(2,1)S(1)} collective-permute-done((bf16[24,1024]{1,0:T(8,128)(2,1)S(1)}, bf16[24,1024]{1,0:T(8,128)(2,1)S(1)}, u32[]{:S(2)}, u32[]{:S(2)}) %collective-permute-start.3) | collective-permute-done | bytes 49184 | tf_op jit(solution)/shard_map/ppermute | solution.py:25
  19.0 0.0 collective-permute-done.2.rest_1_
  19.0 1.4 %collective-permute-start.8 = (bf16[24,1152]{1,0:T(8,128)(2,1)S(1)}, bf16[24,1152]{1,0:T(8,128)(2,1)S(1)}, u32[]{:S(2)}, u32[]{:S(2)}) collective-permute-start(bf16[24,1152]{1,0:T(8,128)(2,1)S(1)} %middle.1.rest_0_.middle_ref), channel_id=1, source_target_pairs={{0,28},{1,29},{2,30},{3,31},{4,24},{5,25},{6,26},{7,27},{8,20},{9,... | collective-permute-start | bytes 165896 | tf_op jit(solution)/shard_map/ppermute | solution.py:36
  20.4 1.3 %collective-permute-start.7 = (bf16[24,1152]{1,0:T(8,128)(2,1)S(1)}, bf16[24,1152]{1,0:T(8,128)(2,1)S(1)}, u32[]{:S(2)}, u32[]{:S(2)}) collective-permute-start(bf16[24,1152]{1,0:T(8,128)(2,1)S(1)} %middle.1.rest_0_.middle_ref), channel_id=1, source_target_pairs={{0,24},{1,25},{2,26},{3,27},{4,28},{5,29},{6,30},{7,31},{8,16},{9,... | collective-permute-start | bytes 165896 | tf_op jit(solution)/shard_map/ppermute | solution.py:36
  21.7 0.1 collective-permute-start.6
  21.9 0.5 %collective-permute-start.5 = (bf16[24,1152]{1,0:T(8,128)(2,1)S(1)}, bf16[24,1152]{1,0:T(8,128)(2,1)S(1)}, u32[]{:S(2)}, u32[]{:S(2)}) collective-permute-start(bf16[24,1152]{1,0:T(8,128)(2,1)S(1)} %middle.1.rest_0_.middle_ref), channel_id=1, source_target_pairs={{0,16},{1,17},{2,18},{3,19},{4,20},{5,21},{6,22},{7,23},{8,24},{9,... | collective-permute-start | bytes 165896 | tf_op jit(solution)/shard_map/ppermute | solution.py:36
  22.4 1.7 %collective-permute-done.8.rest_3_ = bf16[24,1152]{1,0:T(8,128)(2,1)S(1)} collective-permute-done((bf16[24,1152]{1,0:T(8,128)(2,1)S(1)}, bf16[24,1152]{1,0:T(8,128)(2,1)S(1)}, u32[]{:S(2)}, u32[]{:S(2)}) %collective-permute-start.8) | collective-permute-done | bytes 55328 | tf_op jit(solution)/shard_map/ppermute | solution.py:36
  24.1 0.0 collective-permute-start.11
  24.2 0.6 %collective-permute-done.7.rest_2_ = bf16[24,1152]{1,0:T(8,128)(2,1)S(1)} collective-permute-done((bf16[24,1152]{1,0:T(8,128)(2,1)S(1)}, bf16[24,1152]{1,0:T(8,128)(2,1)S(1)}, u32[]{:S(2)}, u32[]{:S(2)}) %collective-permute-start.7) | collective-permute-done | bytes 55328 | tf_op jit(solution)/shard_map/ppermute | solution.py:36
  24.7 0.8 %collective-permute-start.10 = (bf16[24,1152]{1,0:T(8,128)(2,1)S(1)}, bf16[24,1152]{1,0:T(8,128)(2,1)S(1)}, u32[]{:S(2)}, u32[]{:S(2)}) collective-permute-start(bf16[24,1152]{1,0:T(8,128)(2,1)S(1)} %collective-permute-done.7.rest_2_), channel_id=1, source_target_pairs={{0,16},{16,0},{1,17},{17,1},{2,18},{18,2},{3,19},{19,3},{4,20},{20... | collective-permute-start | bytes 165896 | tf_op jit(solution)/shard_map/ppermute | solution.py:25
  25.5 0.3 collective-permute-done.6.rest_1_
  25.8 0.1 collective-permute-start.9
  26.0 0.0 collective-permute-done.5.rest_0_
  26.0 0.6 %first_half.1 = (f32[96,1536]{1,0:T(8,128)S(1)}, f32[96,128]{1,0:T(8,128)S(1)}, f32[96,128]{1,0:T(8,128)S(1)}) custom-call(f32[1,2048]{1,0:T(1,128)S(1)} %get-tuple-element.38.gain_ref, bf16[1,2048,1536]{2,1,0:T(8,128)(2,1)S(1)} %get-tuple-element.39.w_ref, bf16[24,1152]{1,0:T(8,128)(2,1)S(1)} %collective-permute-done.5.rest_0_, ...), custom_call_target="tpu_custom_call" | custom-call | tf_op jit(solution)/shard_map/first_half/pallas_call | solution.py:45
  26.6 0.0 collective-permute-done.11.rest_3_
  26.6 0.0 collective-permute-done.10.rest_2_
  26.6 0.5 %collective-permute-done.9.rest_1_ = bf16[24,1152]{1,0:T(8,128)(2,1)S(1)} collective-permute-done((bf16[24,1152]{1,0:T(8,128)(2,1)S(1)}, bf16[24,1152]{1,0:T(8,128)(2,1)S(1)}, u32[]{:S(2)}, u32[]{:S(2)}) %collective-permute-start.9) | collective-permute-done | bytes 55328 | tf_op jit(solution)/shard_map/ppermute | solution.py:25
  27.1 0.0 copy-done
  27.1 1.0 %second_half.1 = (bf16[96,768]{1,0:T(8,128)(2,1)S(1)}, bf16[96,1024]{1,0:T(8,128)(2,1)S(1)}) custom-call(f32[1,2048]{1,0:T(1,128)S(1)} %get-tuple-element.38.gain_ref, bf16[1,2048,1536]{2,1,0:T(8,128)(2,1)S(1)} %get-tuple-element.39.w_ref, f32[96,1536]{1,0:T(8,128)S(1)} %get-tuple-element.40.hidden_ref, f32[96,128]{1,0:T(8,128)S(1)} %get-tuple-element.41.square_ref, ...), custom_call_target="tpu_custom_call" | custom-call | tf_op jit(solution)/shard_map/second_half/pallas_call | solution.py:45
  28.1 0.2 collective-permute-start.12
  28.3 0.4 keep.1.kept_ref
  28.7 0.9 %collective-permute-done.12.came_ref = bf16[96,1024]{1,0:T(8,128)(2,1)S(1)} collective-permute-done((bf16[96,1024]{1,0:T(8,128)(2,1)S(1)}, bf16[96,1024]{1,0:T(8,128)(2,1)S(1)}, u32[]{:S(2)}, u32[]{:S(2)}) %collective-permute-start.12) | collective-permute-done | bytes 196640 | tf_op jit(solution)/shard_map/ppermute | solution.py:25
  29.6 1.4 %collective-permute-start.13 = (bf16[24,1024]{1,0:T(8,128)(2,1)S(1)}, bf16[24,1024]{1,0:T(8,128)(2,1)S(1)}, u32[]{:S(2)}, u32[]{:S(2)}) collective-permute-start(bf16[24,1024]{1,0:T(8,128)(2,1)S(1)} %get-tuple-element.45), channel_id=1, source_target_pairs={{0,28},{1,29},{2,30},{3,31},{4,24},{5,25},{6,26},{7,27},{8,20},{9,... | collective-permute-start | bytes 147464 | tf_op jit(solution)/shard_map/ppermute | solution.py:36
  31.0 0.4 %collective-permute-start.14 = (bf16[24,1024]{1,0:T(8,128)(2,1)S(1)}, bf16[24,1024]{1,0:T(8,128)(2,1)S(1)}, u32[]{:S(2)}, u32[]{:S(2)}) collective-permute-start(bf16[24,1024]{1,0:T(8,128)(2,1)S(1)} %get-tuple-element.46), channel_id=1, source_target_pairs={{0,24},{1,25},{2,26},{3,27},{4,28},{5,29},{6,30},{7,31},{8,16},{9,... | collective-permute-start | bytes 147464 | tf_op jit(solution)/shard_map/ppermute | solution.py:36
  31.4 1.2 %collective-permute-start.15 = (bf16[24,1024]{1,0:T(8,128)(2,1)S(1)}, bf16[24,1024]{1,0:T(8,128)(2,1)S(1)}, u32[]{:S(2)}, u32[]{:S(2)}) collective-permute-start(bf16[24,1024]{1,0:T(8,128)(2,1)S(1)} %get-tuple-element.47), channel_id=1, source_target_pairs={{0,20},{1,21},{2,22},{3,23},{4,16},{5,17},{6,18},{7,19},{8,28},{9,... | collective-permute-start | bytes 147464 | tf_op jit(solution)/shard_map/ppermute | solution.py:36
  32.6 0.3 collective-permute-start.16
  33.0 1.3 %collective-permute-done.13.refs_0_ = bf16[24,1024]{1,0:T(8,128)(2,1)S(1)} collective-permute-done((bf16[24,1024]{1,0:T(8,128)(2,1)S(1)}, bf16[24,1024]{1,0:T(8,128)(2,1)S(1)}, u32[]{:S(2)}, u32[]{:S(2)}) %collective-permute-start.13) | collective-permute-done | bytes 49184 | tf_op jit(solution)/shard_map/ppermute | solution.py:36
  34.3 1.3 %collective-permute-done.14.refs_1_ = bf16[24,1024]{1,0:T(8,128)(2,1)S(1)} collective-permute-done((bf16[24,1024]{1,0:T(8,128)(2,1)S(1)}, bf16[24,1024]{1,0:T(8,128)(2,1)S(1)}, u32[]{:S(2)}, u32[]{:S(2)}) %collective-permute-start.14) | collective-permute-done | bytes 49184 | tf_op jit(solution)/shard_map/ppermute | solution.py:36
  35.6 0.0 collective-permute-done.15.refs_2_
  35.6 0.0 collective-permute-done.16.refs_3_
  35.7 2.1 %collective-permute-start.17 = (bf16[24,256]{1,0:T(8,128)(2,1)S(1)}, bf16[24,256]{1,0:T(8,128)(2,1)S(1)}, u32[]{:S(2)}, u32[]{:S(2)}) collective-permute-start(bf16[24,256]{1,0:T(8,128)(2,1)S(1)} %get-tuple-element.49), channel_id=1, source_target_pairs={{0,19},{1,18},{2,17},{3,16},{4,23},{5,22},{6,21},{7,20},{8,27},{9,... | collective-permute-start | bytes 36872 | tf_op jit(solution)/shard_map/ppermute | solution.py:36
  37.8 0.1 collective-permute-start.18
  37.9 1.7 %collective-permute-start.19 = (bf16[24,256]{1,0:T(8,128)(2,1)S(1)}, bf16[24,256]{1,0:T(8,128)(2,1)S(1)}, u32[]{:S(2)}, u32[]{:S(2)}) collective-permute-start(bf16[24,256]{1,0:T(8,128)(2,1)S(1)} %get-tuple-element.51), channel_id=1, source_target_pairs={{0,17},{1,16},{2,19},{3,18},{4,21},{5,20},{6,23},{7,22},{8,25},{9,... | collective-permute-start | bytes 36872 | tf_op jit(solution)/shard_map/ppermute | solution.py:36
  39.5 0.4 %collective-permute-start.20 = (bf16[24,256]{1,0:T(8,128)(2,1)S(1)}, bf16[24,256]{1,0:T(8,128)(2,1)S(1)}, u32[]{:S(2)}, u32[]{:S(2)}) collective-permute-start(bf16[24,256]{1,0:T(8,128)(2,1)S(1)} %get-tuple-element.52), channel_id=1, source_target_pairs={{0,16},{1,17},{2,18},{3,19},{4,20},{5,21},{6,22},{7,23},{8,24},{9,... | collective-permute-start | bytes 36872 | tf_op jit(solution)/shard_map/ppermute | solution.py:36
  40.0 0.7 %collective-permute-done.17.rest_0_ = bf16[24,256]{1,0:T(8,128)(2,1)S(1)} collective-permute-done((bf16[24,256]{1,0:T(8,128)(2,1)S(1)}, bf16[24,256]{1,0:T(8,128)(2,1)S(1)}, u32[]{:S(2)}, u32[]{:S(2)}) %collective-permute-start.17) | collective-permute-done | bytes 12320 | tf_op jit(solution)/shard_map/ppermute | solution.py:36
  40.6 1.1 %collective-permute-done.18.rest_1_ = bf16[24,256]{1,0:T(8,128)(2,1)S(1)} collective-permute-done((bf16[24,256]{1,0:T(8,128)(2,1)S(1)}, bf16[24,256]{1,0:T(8,128)(2,1)S(1)}, u32[]{:S(2)}, u32[]{:S(2)}) %collective-permute-start.18) | collective-permute-done | bytes 12320 | tf_op jit(solution)/shard_map/ppermute | solution.py:36
  41.8 0.0 collective-permute-done.19.rest_2_
  41.8 0.0 collective-permute-done.20.rest_3_
  41.8 0.6 %final.1 = bf16[24,256]{1,0:T(8,128)(2,1)} custom-call(bf16[24,1152]{1,0:T(8,128)(2,1)S(1)} %middle.1.rest_0_.middle_ref, bf16[24,256]{1,0:T(8,128)(2,1)S(1)} %collective-permute-done.17.rest_0_, bf16[24,256]{1,0:T(8,128)(2,1)S(1)} %collective-permute-done.18.rest_1_, bf16[24,256]{1,0:T(8,128)(2,1)S(1)} %collective-permute-done.19.rest_2_, ...), custom_call_target="tpu_custom_call" | custom-call | tf_op jit(solution)/shard_map/final/pallas_call | solution.py:443
  (4 shorter events, 0.1 us)
Async XLA Ops:
  3.2 5.0 %collective-permute-start = (bf16[24,640]{1,0:T(8,128)(2,1)S(1)}, bf16[24,640]{1,0:T(8,128)(2,1)S(1)}, u32[]{:S(2)}, u32[]{:S(2)}) collective-permute-start(bf16[24,640]{1,0:T(8,128)(2,1)S(1)} %get-tuple-element.33), channel_id=1, source_target_pairs={{0,1},{1,0},{2,3},{3,2},{4,5},{5,4},{6,7},{7,6},{8,9},{9,8},{10,11... | collective-permute-start | bytes 92168 | tf_op jit(solution)/shard_map/ppermute | solution.py:25
  8.6 1.2 %collective-permute-start.1 = (bf16[24,1024]{1,0:T(8,128)(2,1)S(1)}, bf16[24,1024]{1,0:T(8,128)(2,1)S(1)}, u32[]{:S(2)}, u32[]{:S(2)}) collective-permute-start(bf16[24,1024]{1,0:T(8,128)(2,1)S(1)} %get-tuple-element.35), channel_id=1, source_target_pairs={{0,16},{16,0},{1,17},{17,1},{2,18},{18,2},{3,19},{19,3},{4,20},{20... | collective-permute-start | bytes 147464 | tf_op jit(solution)/shard_map/ppermute | solution.py:25
  9.9 7.6 %collective-permute-start.4 = (bf16[24,1024]{1,0:T(8,128)(2,1)S(1)}, bf16[24,1024]{1,0:T(8,128)(2,1)S(1)}, u32[]{:S(2)}, u32[]{:S(2)}) collective-permute-start(bf16[24,1024]{1,0:T(8,128)(2,1)S(1)} %pair.1.after_ref.rest_0_), channel_id=1, source_target_pairs={{0,3},{1,2},{2,1},{3,0},{4,7},{5,6},{6,5},{7,4},{8,11},{9,10},{10,... | collective-permute-start | bytes 147464 | tf_op jit(solution)/shard_map/ppermute | solution.py:25
  14.0 5.0 %collective-permute-start.3 = (bf16[24,1024]{1,0:T(8,128)(2,1)S(1)}, bf16[24,1024]{1,0:T(8,128)(2,1)S(1)}, u32[]{:S(2)}, u32[]{:S(2)}) collective-permute-start(bf16[24,1024]{1,0:T(8,128)(2,1)S(1)} %pair.1.after_ref.rest_0_), channel_id=1, source_target_pairs={{0,2},{1,3},{2,0},{3,1},{4,6},{5,7},{6,4},{7,5},{8,10},{9,11},{10,... | collective-permute-start | bytes 147464 | tf_op jit(solution)/shard_map/ppermute | solution.py:25
  14.0 5.0 %collective-permute-start.2 = (bf16[24,1024]{1,0:T(8,128)(2,1)S(1)}, bf16[24,1024]{1,0:T(8,128)(2,1)S(1)}, u32[]{:S(2)}, u32[]{:S(2)}) collective-permute-start(bf16[24,1024]{1,0:T(8,128)(2,1)S(1)} %pair.1.after_ref.rest_0_), channel_id=1, source_target_pairs={{0,1},{1,0},{2,3},{3,2},{4,5},{5,4},{6,7},{7,6},{8,9},{9,8},{10,11... | collective-permute-start | bytes 147464 | tf_op jit(solution)/shard_map/ppermute | solution.py:25
  17.5 9.6 %copy-start = (bf16[1,768,2048]{2,1,0:T(8,128)(2,1)S(1)}, bf16[1,768,2048]{2,1,0:T(8,128)(2,1)}, u32[]{:S(2)}) copy-start(bf16[1,768,2048]{2,1,0:T(8,128)(2,1)} %down_ref.3) | copy-start | bytes 9437188
  19.0 5.1 %collective-permute-start.8 = (bf16[24,1152]{1,0:T(8,128)(2,1)S(1)}, bf16[24,1152]{1,0:T(8,128)(2,1)S(1)}, u32[]{:S(2)}, u32[]{:S(2)}) collective-permute-start(bf16[24,1152]{1,0:T(8,128)(2,1)S(1)} %middle.1.rest_0_.middle_ref), channel_id=1, source_target_pairs={{0,28},{1,29},{2,30},{3,31},{4,24},{5,25},{6,26},{7,27},{8,20},{9,... | collective-permute-start | bytes 165896 | tf_op jit(solution)/shard_map/ppermute | solution.py:36
  20.4 4.3 %collective-permute-start.7 = (bf16[24,1152]{1,0:T(8,128)(2,1)S(1)}, bf16[24,1152]{1,0:T(8,128)(2,1)S(1)}, u32[]{:S(2)}, u32[]{:S(2)}) collective-permute-start(bf16[24,1152]{1,0:T(8,128)(2,1)S(1)} %middle.1.rest_0_.middle_ref), channel_id=1, source_target_pairs={{0,24},{1,25},{2,26},{3,27},{4,28},{5,29},{6,30},{7,31},{8,16},{9,... | collective-permute-start | bytes 165896 | tf_op jit(solution)/shard_map/ppermute | solution.py:36
  21.7 4.1 %collective-permute-start.6 = (bf16[24,1152]{1,0:T(8,128)(2,1)S(1)}, bf16[24,1152]{1,0:T(8,128)(2,1)S(1)}, u32[]{:S(2)}, u32[]{:S(2)}) collective-permute-start(bf16[24,1152]{1,0:T(8,128)(2,1)S(1)} %middle.1.rest_0_.middle_ref), channel_id=1, source_target_pairs={{0,20},{1,21},{2,22},{3,23},{4,16},{5,17},{6,18},{7,19},{8,28},{9,... | collective-permute-start | bytes 165896 | tf_op jit(solution)/shard_map/ppermute | solution.py:36
  21.9 4.1 %collective-permute-start.5 = (bf16[24,1152]{1,0:T(8,128)(2,1)S(1)}, bf16[24,1152]{1,0:T(8,128)(2,1)S(1)}, u32[]{:S(2)}, u32[]{:S(2)}) collective-permute-start(bf16[24,1152]{1,0:T(8,128)(2,1)S(1)} %middle.1.rest_0_.middle_ref), channel_id=1, source_target_pairs={{0,16},{1,17},{2,18},{3,19},{4,20},{5,21},{6,22},{7,23},{8,24},{9,... | collective-permute-start | bytes 165896 | tf_op jit(solution)/shard_map/ppermute | solution.py:36
  24.1 2.5 %collective-permute-start.11 = (bf16[24,1152]{1,0:T(8,128)(2,1)S(1)}, bf16[24,1152]{1,0:T(8,128)(2,1)S(1)}, u32[]{:S(2)}, u32[]{:S(2)}) collective-permute-start(bf16[24,1152]{1,0:T(8,128)(2,1)S(1)} %collective-permute-done.8.rest_3_), channel_id=1, source_target_pairs={{0,16},{16,0},{1,17},{17,1},{2,18},{18,2},{3,19},{19,3},{4,20},{20... | collective-permute-start | bytes 165896 | tf_op jit(solution)/shard_map/ppermute | solution.py:25
  24.7 1.9 %collective-permute-start.10 = (bf16[24,1152]{1,0:T(8,128)(2,1)S(1)}, bf16[24,1152]{1,0:T(8,128)(2,1)S(1)}, u32[]{:S(2)}, u32[]{:S(2)}) collective-permute-start(bf16[24,1152]{1,0:T(8,128)(2,1)S(1)} %collective-permute-done.7.rest_2_), channel_id=1, source_target_pairs={{0,16},{16,0},{1,17},{17,1},{2,18},{18,2},{3,19},{19,3},{4,20},{20... | collective-permute-start | bytes 165896 | tf_op jit(solution)/shard_map/ppermute | solution.py:25
  25.8 1.2 %collective-permute-start.9 = (bf16[24,1152]{1,0:T(8,128)(2,1)S(1)}, bf16[24,1152]{1,0:T(8,128)(2,1)S(1)}, u32[]{:S(2)}, u32[]{:S(2)}) collective-permute-start(bf16[24,1152]{1,0:T(8,128)(2,1)S(1)} %collective-permute-done.6.rest_1_), channel_id=1, source_target_pairs={{0,16},{16,0},{1,17},{17,1},{2,18},{18,2},{3,19},{19,3},{4,20},{20... | collective-permute-start | bytes 165896 | tf_op jit(solution)/shard_map/ppermute | solution.py:25
  28.1 1.5 %collective-permute-start.12 = (bf16[96,1024]{1,0:T(8,128)(2,1)S(1)}, bf16[96,1024]{1,0:T(8,128)(2,1)S(1)}, u32[]{:S(2)}, u32[]{:S(2)}) collective-permute-start(bf16[96,1024]{1,0:T(8,128)(2,1)S(1)} %get-tuple-element.44), channel_id=1, source_target_pairs={{0,16},{16,0},{1,17},{17,1},{2,18},{18,2},{3,19},{19,3},{4,20},{20... | collective-permute-start | bytes 589832 | tf_op jit(solution)/shard_map/ppermute | solution.py:25
  29.6 4.7 %collective-permute-start.13 = (bf16[24,1024]{1,0:T(8,128)(2,1)S(1)}, bf16[24,1024]{1,0:T(8,128)(2,1)S(1)}, u32[]{:S(2)}, u32[]{:S(2)}) collective-permute-start(bf16[24,1024]{1,0:T(8,128)(2,1)S(1)} %get-tuple-element.45), channel_id=1, source_target_pairs={{0,28},{1,29},{2,30},{3,31},{4,24},{5,25},{6,26},{7,27},{8,20},{9,... | collective-permute-start | bytes 147464 | tf_op jit(solution)/shard_map/ppermute | solution.py:36
  31.0 4.7 %collective-permute-start.14 = (bf16[24,1024]{1,0:T(8,128)(2,1)S(1)}, bf16[24,1024]{1,0:T(8,128)(2,1)S(1)}, u32[]{:S(2)}, u32[]{:S(2)}) collective-permute-start(bf16[24,1024]{1,0:T(8,128)(2,1)S(1)} %get-tuple-element.46), channel_id=1, source_target_pairs={{0,24},{1,25},{2,26},{3,27},{4,28},{5,29},{6,30},{7,31},{8,16},{9,... | collective-permute-start | bytes 147464 | tf_op jit(solution)/shard_map/ppermute | solution.py:36
  31.4 4.2 %collective-permute-start.15 = (bf16[24,1024]{1,0:T(8,128)(2,1)S(1)}, bf16[24,1024]{1,0:T(8,128)(2,1)S(1)}, u32[]{:S(2)}, u32[]{:S(2)}) collective-permute-start(bf16[24,1024]{1,0:T(8,128)(2,1)S(1)} %get-tuple-element.47), channel_id=1, source_target_pairs={{0,20},{1,21},{2,22},{3,23},{4,16},{5,17},{6,18},{7,19},{8,28},{9,... | collective-permute-start | bytes 147464 | tf_op jit(solution)/shard_map/ppermute | solution.py:36
  32.6 3.0 %collective-permute-start.16 = (bf16[24,1024]{1,0:T(8,128)(2,1)S(1)}, bf16[24,1024]{1,0:T(8,128)(2,1)S(1)}, u32[]{:S(2)}, u32[]{:S(2)}) collective-permute-start(bf16[24,1024]{1,0:T(8,128)(2,1)S(1)} %get-tuple-element.48), channel_id=1, source_target_pairs={{0,16},{1,17},{2,18},{3,19},{4,20},{5,21},{6,22},{7,23},{8,24},{9,... | collective-permute-start | bytes 147464 | tf_op jit(solution)/shard_map/ppermute | solution.py:36
  35.7 5.0 %collective-permute-start.17 = (bf16[24,256]{1,0:T(8,128)(2,1)S(1)}, bf16[24,256]{1,0:T(8,128)(2,1)S(1)}, u32[]{:S(2)}, u32[]{:S(2)}) collective-permute-start(bf16[24,256]{1,0:T(8,128)(2,1)S(1)} %get-tuple-element.49), channel_id=1, source_target_pairs={{0,19},{1,18},{2,17},{3,16},{4,23},{5,22},{6,21},{7,20},{8,27},{9,... | collective-permute-start | bytes 36872 | tf_op jit(solution)/shard_map/ppermute | solution.py:36
  37.8 4.0 %collective-permute-start.18 = (bf16[24,256]{1,0:T(8,128)(2,1)S(1)}, bf16[24,256]{1,0:T(8,128)(2,1)S(1)}, u32[]{:S(2)}, u32[]{:S(2)}) collective-permute-start(bf16[24,256]{1,0:T(8,128)(2,1)S(1)} %get-tuple-element.50), channel_id=1, source_target_pairs={{0,18},{1,19},{2,16},{3,17},{4,22},{5,23},{6,20},{7,21},{8,26},{9,... | collective-permute-start | bytes 36872 | tf_op jit(solution)/shard_map/ppermute | solution.py:36
  37.9 3.9 %collective-permute-start.19 = (bf16[24,256]{1,0:T(8,128)(2,1)S(1)}, bf16[24,256]{1,0:T(8,128)(2,1)S(1)}, u32[]{:S(2)}, u32[]{:S(2)}) collective-permute-start(bf16[24,256]{1,0:T(8,128)(2,1)S(1)} %get-tuple-element.51), channel_id=1, source_target_pairs={{0,17},{1,16},{2,19},{3,18},{4,21},{5,20},{6,23},{7,22},{8,25},{9,... | collective-permute-start | bytes 36872 | tf_op jit(solution)/shard_map/ppermute | solution.py:36
  39.5 2.2 %collective-permute-start.20 = (bf16[24,256]{1,0:T(8,128)(2,1)S(1)}, bf16[24,256]{1,0:T(8,128)(2,1)S(1)}, u32[]{:S(2)}, u32[]{:S(2)}) collective-permute-start(bf16[24,256]{1,0:T(8,128)(2,1)S(1)} %get-tuple-element.52), channel_id=1, source_target_pairs={{0,16},{1,17},{2,18},{3,19},{4,20},{5,21},{6,22},{7,23},{8,24},{9,... | collective-permute-start | bytes 36872 | tf_op jit(solution)/shard_map/ppermute | solution.py:36

commit v5 on v4

--- a/solution.py
+++ b/solution.py
@@ -12,7 +12,10 @@
 KVH = 4
 HD = 128
 LOW = -1e30
-CHUNKS = 4
+SUMS = 16
+TERM = 32
+CUTS = (0, 6, 12, 18, 24)
+CUT_OF = 24
 LAG = 1
 F32 = jnp.float32
 BF16 = jnp.bfloat16
@@ -62,7 +65,8 @@
     kv, q_in, len_ref, ids_ref, gates_ref, turn_s, q_s, score_s, num_s, max_s, sum_s, sems = refs[
         6 + kv_parts :
     ]
-    step = rows // CHUNKS
+    cuts = [rows * c // CUT_OF for c in CUTS]
+    chunks = list(zip(cuts, cuts[1:]))
     section = lax.axis_index("side")
     tp_index = lax.axis_index("tp")
     part = tp_index % kv_parts
@@ -74,7 +78,7 @@
         (len_hbm, len_ref),
         (ids_hbm, ids_ref),
         (gates_hbm, gates_ref),
-        *[(kv_hbm.at[pl.ds(c * step, step), 0], kv.at[pl.ds(c * step, step)]) for c in range(CHUNKS)],
+        *[(kv_hbm.at[pl.ds(a, b - a), 0], kv.at[pl.ds(a, b - a)]) for a, b in chunks],
     ]
     copies = [pltpu.make_async_copy(a, b, sems.at[i]) for i, (a, b) in enumerate(pairs)]
     for copy in copies:
@@ -112,9 +116,9 @@
                 weight.astype(BF16), kv[r, :, HD:], preferred_element_type=F32
             )
 
-    for c in range(CHUNKS):
+    for c, span_of in enumerate(chunks):
         copies[4 + c].wait()
-        for r in range(c * step, (c + 1) * step):
+        for r in range(*span_of):
             score_s[spot(r), :] = lax.dot_general(
                 q_s[spot(r), :].astype(BF16),
                 kv[r, :, :HD],
@@ -122,8 +126,8 @@
                 preferred_element_type=F32,
             )
         if c >= LAG:
-            values(range((c - LAG) * step, (c - LAG + 1) * step))
-    values(range((CHUNKS - LAG) * step, rows))
+            values(range(*chunks[c - LAG]))
+    values(range(cuts[-1 - LAG], rows))
     lane = lax.broadcasted_iota(jnp.int32, (rows, HD), 1)
     for mask, out in enumerate([own_ref, *send_refs]):
         first = (part ^ mask) * per_member
@@ -131,12 +135,14 @@
         for i in range(per_member):
             pick = pl.ds(first + i, rows, stride=group_heads)
             out[:, i * HD : (i + 1) * HD] = num_s[pick, :].astype(out.dtype)
-            for j, value in enumerate((max_s[pick, :], sum_s[pick, :])):
-                for k in range(3):
-                    term = value.astype(out.dtype).astype(F32)
-                    stats = jnp.where(lane == 6 * i + 3 * j + k, term, stats)
-                    value = value - term
-        out[:, per_member * HD :] = stats.astype(out.dtype)
+            stats = jnp.where(lane == i, max_s[pick, :], stats)
+            stats = jnp.where(lane == SUMS + i, sum_s[pick, :], stats)
+        sent = jnp.zeros((rows, HD), F32)
+        for k in range(3):
+            term = stats.astype(out.dtype).astype(F32)
+            sent = sent + (pltpu.roll(term, k * TERM, 1) if k else term)
+            stats = stats - term
+        out[:, per_member * HD :] = sent.astype(out.dtype)
 
 
 def fetch_kernel(parts, after_ref, *refs):
@@ -178,27 +184,28 @@
     packets = rest[:kv_parts]
     heads_ref, away_ref = rest[kv_parts:]
     scale = math.log2(math.e) / math.sqrt(HD)
-    stats = [p[:, per_member * HD :].astype(F32) for p in packets]
-
-    def whole(stat, at):
-        return stat[:, at : at + 1] + stat[:, at + 1 : at + 2] + stat[:, at + 2 : at + 3]
-
+    tops, sums = [], []
+    for p in packets:
+        stat = p[:, per_member * HD :].astype(F32)
+        whole = stat + pltpu.roll(stat, HD - TERM, 1) + pltpu.roll(stat, HD - 2 * TERM, 1)
+        tops.append(whole)
+        sums.append(pltpu.roll(whole, HD - SUMS, 1))
+    highest = functools.reduce(jnp.maximum, tops)
+    factors = [jnp.exp2((top - highest) * scale) for top in tops]
+    total_sum = functools.reduce(jnp.add, [f * v for f, v in zip(factors, sums)])
+    factors = [f / total_sum for f in factors]
     for i in range(per_member):
-        tops = [whole(stat, 6 * i) for stat in stats]
-        highest = functools.reduce(jnp.maximum, tops)
-        total, total_sum = 0.0, 0.0
-        for p, stat, top in zip(packets, stats, tops):
-            factor = jnp.exp2((top - highest) * scale)
-            total = total + p[:, i * HD : (i + 1) * HD].astype(F32) * factor
-            total_sum = total_sum + whole(stat, 6 * i + 3) * factor
-        heads_ref[:, i * HD : (i + 1) * HD] = (total / total_sum).astype(BF16)
+        total = 0.0
+        for p, f in zip(packets, factors):
+            total = total + p[:, i * HD : (i + 1) * HD].astype(F32) * f[:, i : i + 1]
+        heads_ref[:, i * HD : (i + 1) * HD] = total.astype(BF16)
     part_kernel(False, heads_ref, weight_ref, away_ref)
 
 
 def part_kernel(mine, heads_ref, weight_ref, out_ref):
     half = out_ref.shape[1]
     section = lax.axis_index("side")
-    cols = pl.ds(pl.multiple_of((section if mine else 1 - section) * half, half), half)
+    cols = pl.ds(pl.multiple_of((1 - section if mine else section) * half, half), half)
     out_ref[...] = jnp.dot(
         heads_ref[...], weight_ref[:, cols], preferred_element_type=F32
     ).astype(out_ref.dtype)
@@ -268,33 +275,31 @@
 
     for j in range(inner // tile):
         column(j, 0)
-    down(tile, act_ref, gate_ref, down_ref, away_ref, 1 - section)
-
-
-def down(tile, act_ref, gate_ref, down_ref, out_ref, side):
-    half = out_ref.shape[1]
+    down(tile, act_ref, gate_ref, down_ref, away_ref, (1 - section) * half)
+
+
+def down(tile, act_ref, gate_ref, down_ref, out_ref, start):
     gate = gate_ref[:, :1]
-
-    def column(j, carry):
-        at = pl.ds(pl.multiple_of(side * half + j * tile, HD), tile)
+    for j in range(out_ref.shape[1] // tile):
+        at = pl.ds(pl.multiple_of(start + j * tile, HD), tile)
         part = jnp.dot(act_ref[...], down_ref[0, :, at], preferred_element_type=F32)
-        out_ref[:, pl.ds(j * tile, tile)] = (part * gate).astype(
-            out_ref.dtype
-        )
-        return carry
-
-    for j in range(half // tile):
-        column(j, 0)
+        out_ref[:, j * tile : (j + 1) * tile] = (part * gate).astype(out_ref.dtype)
+
+
+def away_kernel(tile, half, first, act_ref, gate_ref, down_ref, out_ref):
+    start = (1 - lax.axis_index("side")) * half + first
+    down(tile, act_ref, gate_ref, down_ref, out_ref, start)
 
 
 def keep_kernel(tile, act_ref, gate_ref, down_ref, kept_ref):
-    down(tile, act_ref, gate_ref, down_ref, kept_ref, lax.axis_index("side"))
+    start = lax.axis_index("side") * kept_ref.shape[1]
+    down(tile, act_ref, gate_ref, down_ref, kept_ref, start)
 
 
 def fold_kernel(rows, kept_ref, came_ref, *sends):
+    total = kept_ref[...] + came_ref[...].astype(F32)
     for b, ref in enumerate(sends):
-        at = slice(b * rows, (b + 1) * rows)
-        ref[...] = (kept_ref[at, :] + came_ref[at, :].astype(F32)).astype(BF16)
+        ref[...] = total[b * rows : (b + 1) * rows].astype(BF16)
 
 
 def split_kernel(count, *refs):
@@ -367,10 +372,10 @@
             pltpu.VMEM((HD, HD), F32),
             pltpu.VMEM((many, HD), F32),
             pltpu.VMEM((many, span), F32),
-            pltpu.VMEM((many, HD), F32),
-            pltpu.VMEM((many, HD), F32),
-            pltpu.VMEM((many, HD), F32),
-            pltpu.SemaphoreType.DMA((4 + CHUNKS,)),
+            pltpu.VMEM((many + group_heads, HD), F32),
+            pltpu.VMEM((many + group_heads, HD), F32),
+            pltpu.VMEM((many + group_heads, HD), F32),
+            pltpu.SemaphoreType.DMA((3 + len(CUTS),)),
         ],
         far=range(5),
         limit=16,
@@ -394,7 +399,7 @@
     )[0]
     outgoing = call(add_kernel, [kept, away], [((rows, half), BF16)], name="pair")[0]
     w_gate_up, token = fetched(outgoing, w_gate_up)
-    parts = [outgoing] + [swapped(outgoing, "tp", mask) for mask in range(1, tp)]
+    parts = [crossed(outgoing, 0, mask) for mask in range(tp)]
     middle = call(
         functools.partial(middle_kernel, half),
         [token, resid, gate_lanes, *parts],

time: 42.6 us -> 42.5 us (level)
    ppermute x9 -> x6, starting transfers between devices: 9.03 us -> 4.04 us  [swapped(): return lax.ppermute(value, axis, pairs)]
    ppermute x12 -> x16, starting transfers between devices: 11.1 us -> 15.7 us  [crossed(): return lax.ppermute(value, ('side', 'grp', 'tp'), pairs)]
    ppermute x12 -> x16, waiting for transfers between devices: 7.06 us -> 8.75 us  [crossed(): return lax.ppermute(value, ('side', 'grp', 'tp'), pairs)]
    ppermute x9 -> x6, waiting for transfers between devices: 4.01 us -> 2.62 us  [swapped(): return lax.ppermute(value, axis, pairs)]
  transfers between devices with their start and end apart: 21 -> 22, of which waited for: 12 -> 12; matrix products, arithmetic and copies ran while one was open for 0% -> 0% of each run, Pallas kernels for 14% -> 14%
where the time goes in v5:
time: 42.5 us; the launch traced here: 42.4 us
  starting transfers between devices  19.7 us (46%)
  waiting for transfers between devices  11.4 us (27%)
  Pallas kernels  11.1 us (26%)
    ppermute x16, starting transfers between devices, crossed(): return lax.ppermute(value, ('side', 'grp', 'tp'), pairs)  15.7 us
    pallas_call x12, Pallas kernels, call(): pl.pallas_call(kernel, out_shape=[pltpu.VMEM(shape, dtype) for shape, dty...  10.5 us
    ppermute x16, waiting for transfers between devices, crossed(): return lax.ppermute(value, ('side', 'grp', 'tp'), pairs)  8.75 us
    ppermute x6, starting transfers between devices, swapped(): return lax.ppermute(value, axis, pairs)  4.04 us
    ppermute x6, waiting for transfers between devices, swapped(): return lax.ppermute(value, axis, pairs)  2.62 us
  transfers between devices with their start and end apart: 22, of which 12 were waited for; matrix products, arithmetic and copies ran while one was open for 0% of the time, Pallas kernels for 14%

profile of v5, /device:TPU:0, one launch (start us, length us, event | category | flops | bytes accessed | tf_op | source)
XLA Modules:
  0.0 42.4 jit_solution(17850138454157712683)
XLA Ops:
  0.0 3.2 %attention.1 = (f32[24,640]{1,0:T(8,128)S(1)}, bf16[24,640]{1,0:T(8,128)(2,1)S(1)}, bf16[24,128]{1,0:T(8,128)(2,1)S(1)}) custom-call(bf16[24,2048]{1,0:T(8,128)(2,1)} %refs_0_.3, s32[24]{0:T(128)} %refs_1_.2, s32[8,24]{1,0:T(8,128)} %bitcast.4, f32[8,24]{1,0:T(8,128)} %bitcast.5, bf16[24,1,384,256]{3,2,1,0:T(8,128)(2,1)} %refs_4_.1), custom_call_target="tpu_custom_call" | custom-call | tf_op jit(solution)/shard_map/attention/pallas_call | solution.py:48
  3.2 3.1 %collective-permute-start = (bf16[24,640]{1,0:T(8,128)(2,1)S(1)}, bf16[24,640]{1,0:T(8,128)(2,1)S(1)}, u32[]{:S(2)}, u32[]{:S(2)}) collective-permute-start(bf16[24,640]{1,0:T(8,128)(2,1)S(1)} %get-tuple-element.33), channel_id=1, source_target_pairs={{0,1},{1,0},{2,3},{3,2},{4,5},{5,4},{6,7},{7,6},{8,9},{9,8},{10,11... | collective-permute-start | bytes 92168 | tf_op jit(solution)/shard_map/ppermute | solution.py:28
  6.3 1.6 %fetch.2 = (bf16[512,2048]{1,0:T(8,128)(2,1)S(1)}, bf16[24,2048]{1,0:T(8,128)(2,1)S(1)}, f32[1,2048]{1,0:T(1,128)S(1)}, bf16[24,128]{1,0:T(8,128)(2,1)S(1)}) custom-call(bf16[24,128]{1,0:T(8,128)(2,1)S(1)} %get-tuple-element.29.after_ref.lanes_ref, bf16[512,2048]{1,0:T(8,128)(2,1)} %refs_0_.4, bf16[24,2048]{1,0:T(8,128)(2,1)} %refs_1_.3, f32[1,2048]{1,0:T(1,128)} %bitcast.3), custom_call_target="tpu_custom_call" | custom-call | bytes 4407296 | tf_op jit(solution)/shard_map/fetch/pallas_call | solution.py:48
  7.9 0.3 collective-permute-done.rest_1_
  8.2 0.5 %project.1 = (bf16[24,512]{1,0:T(8,128)(2,1)S(1)}, bf16[24,1024]{1,0:T(8,128)(2,1)S(1)}) custom-call(bf16[24,128]{1,0:T(8,128)(2,1)S(1)} %get-tuple-element.30.token_ref, bf16[512,2048]{1,0:T(8,128)(2,1)S(1)} %get-tuple-element.31.weight_ref, f32[24,640]{1,0:T(8,128)S(1)} %get-tuple-element.32.rest_0_, bf16[24,640]{1,0:T(8,128)(2,1)S(1)} %collective-permute-done.rest_1_), custom_call_target="tpu_custom_call" | custom-call | tf_op jit(solution)/shard_map/project/pallas_call | solution.py:48
  8.6 0.0 collective-permute-start.1
  8.7 0.3 kept.1.kept_ref
  8.9 0.9 %collective-permute-done.1.came_ref = bf16[24,1024]{1,0:T(8,128)(2,1)S(1)} collective-permute-done((bf16[24,1024]{1,0:T(8,128)(2,1)S(1)}, bf16[24,1024]{1,0:T(8,128)(2,1)S(1)}, u32[]{:S(2)}, u32[]{:S(2)}) %collective-permute-start.1) | collective-permute-done | bytes 49184 | tf_op jit(solution)/shard_map/ppermute | solution.py:28
  9.9 3.9 %collective-permute-start.5 = (bf16[24,1024]{1,0:T(8,128)(2,1)S(1)}, bf16[24,1024]{1,0:T(8,128)(2,1)S(1)}, u32[]{:S(2)}, u32[]{:S(2)}) collective-permute-start(bf16[24,1024]{1,0:T(8,128)(2,1)S(1)} %pair.1.after_ref), channel_id=1, source_target_pairs={{0,19},{1,18},{2,17},{3,16},{4,23},{5,22},{6,21},{7,20},{8,27},{9,... | collective-permute-start | bytes 147464 | tf_op jit(solution)/shard_map/ppermute | solution.py:39
  13.8 0.0 collective-permute-start.4
  13.8 0.6 %collective-permute-start.3 = (bf16[24,1024]{1,0:T(8,128)(2,1)S(1)}, bf16[24,1024]{1,0:T(8,128)(2,1)S(1)}, u32[]{:S(2)}, u32[]{:S(2)}) collective-permute-start(bf16[24,1024]{1,0:T(8,128)(2,1)S(1)} %pair.1.after_ref), channel_id=1, source_target_pairs={{0,17},{1,16},{2,19},{3,18},{4,21},{5,20},{6,23},{7,22},{8,25},{9,... | collective-permute-start | bytes 147464 | tf_op jit(solution)/shard_map/ppermute | solution.py:39
  14.4 0.2 collective-permute-start.2
  14.5 2.9 %fetch.3 = (bf16[1,2048,1536]{2,1,0:T(8,128)(2,1)S(1)}, bf16[24,128]{1,0:T(8,128)(2,1)S(1)}) custom-call(bf16[24,1024]{1,0:T(8,128)(2,1)S(1)} %pair.1.after_ref, bf16[1,2048,1536]{2,1,0:T(8,128)(2,1)} %refs_0_.5), custom_call_target="tpu_custom_call" | custom-call | bytes 12582912 | tf_op jit(solution)/shard_map/fetch/pallas_call | solution.py:48
  17.4 0.0 copy-start
  17.4 0.0 collective-permute-done.5.rest_3_
  17.4 1.0 %collective-permute-done.4.rest_2_ = bf16[24,1024]{1,0:T(8,128)(2,1)S(1)} collective-permute-done((bf16[24,1024]{1,0:T(8,128)(2,1)S(1)}, bf16[24,1024]{1,0:T(8,128)(2,1)S(1)}, u32[]{:S(2)}, u32[]{:S(2)}) %collective-permute-start.4) | collective-permute-done | bytes 49184 | tf_op jit(solution)/shard_map/ppermute | solution.py:39
  18.4 0.0 collective-permute-done.3.rest_1_
  18.4 0.0 collective-permute-done.2.rest_0_
  18.5 2.4 %collective-permute-start.9 = (bf16[24,1152]{1,0:T(8,128)(2,1)S(1)}, bf16[24,1152]{1,0:T(8,128)(2,1)S(1)}, u32[]{:S(2)}, u32[]{:S(2)}) collective-permute-start(bf16[24,1152]{1,0:T(8,128)(2,1)S(1)} %middle.1.rest_0_.middle_ref), channel_id=1, source_target_pairs={{0,28},{1,29},{2,30},{3,31},{4,24},{5,25},{6,26},{7,27},{8,20},{9,... | collective-permute-start | bytes 165896 | tf_op jit(solution)/shard_map/ppermute | solution.py:39
  20.9 0.4 collective-permute-start.8
  21.2 0.4 collective-permute-start.7
  21.6 0.3 collective-permute-start.6
  21.9 1.4 %collective-permute-done.9.rest_3_ = bf16[24,1152]{1,0:T(8,128)(2,1)S(1)} collective-permute-done((bf16[24,1152]{1,0:T(8,128)(2,1)S(1)}, bf16[24,1152]{1,0:T(8,128)(2,1)S(1)}, u32[]{:S(2)}, u32[]{:S(2)}) %collective-permute-start.9) | collective-permute-done | bytes 55328 | tf_op jit(solution)/shard_map/ppermute | solution.py:39
  23.3 0.2 collective-permute-start.12
  23.4 1.2 %collective-permute-done.8.rest_2_ = bf16[24,1152]{1,0:T(8,128)(2,1)S(1)} collective-permute-done((bf16[24,1152]{1,0:T(8,128)(2,1)S(1)}, bf16[24,1152]{1,0:T(8,128)(2,1)S(1)}, u32[]{:S(2)}, u32[]{:S(2)}) %collective-permute-start.8) | collective-permute-done | bytes 55328 | tf_op jit(solution)/shard_map/ppermute | solution.py:39
  24.7 0.5 %collective-permute-start.11 = (bf16[24,1152]{1,0:T(8,128)(2,1)S(1)}, bf16[24,1152]{1,0:T(8,128)(2,1)S(1)}, u32[]{:S(2)}, u32[]{:S(2)}) collective-permute-start(bf16[24,1152]{1,0:T(8,128)(2,1)S(1)} %collective-permute-done.8.rest_2_), channel_id=1, source_target_pairs={{0,16},{16,0},{1,17},{17,1},{2,18},{18,2},{3,19},{19,3},{4,20},{20... | collective-permute-start | bytes 165896 | tf_op jit(solution)/shard_map/ppermute | solution.py:28
  25.2 0.0 collective-permute-done.7.rest_1_
  25.2 0.1 collective-permute-start.10
  25.2 0.0 collective-permute-done.6.rest_0_
  25.2 0.6 %first_half.1 = (f32[96,1536]{1,0:T(8,128)S(1)}, f32[96,128]{1,0:T(8,128)S(1)}, f32[96,128]{1,0:T(8,128)S(1)}) custom-call(f32[1,2048]{1,0:T(1,128)S(1)} %get-tuple-element.38.gain_ref, bf16[1,2048,1536]{2,1,0:T(8,128)(2,1)S(1)} %get-tuple-element.39.w_ref, bf16[24,1152]{1,0:T(8,128)(2,1)S(1)} %collective-permute-done.6.rest_0_, ...), custom_call_target="tpu_custom_call" | custom-call | tf_op jit(solution)/shard_map/first_half/pallas_call | solution.py:48
  25.9 0.0 collective-permute-done.12.rest_3_
  25.9 0.2 collective-permute-done.11.rest_2_
  26.0 0.4 collective-permute-done.10.rest_1_
  26.4 0.0 copy-done
  26.4 1.0 %second_half.1 = (bf16[96,768]{1,0:T(8,128)(2,1)S(1)}, bf16[96,1024]{1,0:T(8,128)(2,1)S(1)}) custom-call(f32[1,2048]{1,0:T(1,128)S(1)} %get-tuple-element.38.gain_ref, bf16[1,2048,1536]{2,1,0:T(8,128)(2,1)S(1)} %get-tuple-element.39.w_ref, f32[96,1536]{1,0:T(8,128)S(1)} %get-tuple-element.40.hidden_ref, f32[96,128]{1,0:T(8,128)S(1)} %get-tuple-element.41.square_ref, ...), custom_call_target="tpu_custom_call" | custom-call | tf_op jit(solution)/shard_map/second_half/pallas_call | solution.py:48
  27.4 0.2 collective-permute-start.13
  27.6 0.4 keep.1.kept_ref
  28.0 0.9 %collective-permute-done.13.came_ref = bf16[96,1024]{1,0:T(8,128)(2,1)S(1)} collective-permute-done((bf16[96,1024]{1,0:T(8,128)(2,1)S(1)}, bf16[96,1024]{1,0:T(8,128)(2,1)S(1)}, u32[]{:S(2)}, u32[]{:S(2)}) %collective-permute-start.13) | collective-permute-done | bytes 196640 | tf_op jit(solution)/shard_map/ppermute | solution.py:28
  28.9 1.3 %collective-permute-start.14 = (bf16[24,1024]{1,0:T(8,128)(2,1)S(1)}, bf16[24,1024]{1,0:T(8,128)(2,1)S(1)}, u32[]{:S(2)}, u32[]{:S(2)}) collective-permute-start(bf16[24,1024]{1,0:T(8,128)(2,1)S(1)} %get-tuple-element.45), channel_id=1, source_target_pairs={{0,28},{1,29},{2,30},{3,31},{4,24},{5,25},{6,26},{7,27},{8,20},{9,... | collective-permute-start | bytes 147464 | tf_op jit(solution)/shard_map/ppermute | solution.py:39
  30.2 1.2 %collective-permute-start.15 = (bf16[24,1024]{1,0:T(8,128)(2,1)S(1)}, bf16[24,1024]{1,0:T(8,128)(2,1)S(1)}, u32[]{:S(2)}, u32[]{:S(2)}) collective-permute-start(bf16[24,1024]{1,0:T(8,128)(2,1)S(1)} %get-tuple-element.46), channel_id=1, source_target_pairs={{0,24},{1,25},{2,26},{3,27},{4,28},{5,29},{6,30},{7,31},{8,16},{9,... | collective-permute-start | bytes 147464 | tf_op jit(solution)/shard_map/ppermute | solution.py:39
  31.4 0.5 %collective-permute-start.16 = (bf16[24,1024]{1,0:T(8,128)(2,1)S(1)}, bf16[24,1024]{1,0:T(8,128)(2,1)S(1)}, u32[]{:S(2)}, u32[]{:S(2)}) collective-permute-start(bf16[24,1024]{1,0:T(8,128)(2,1)S(1)} %get-tuple-element.47), channel_id=1, source_target_pairs={{0,20},{1,21},{2,22},{3,23},{4,16},{5,17},{6,18},{7,19},{8,28},{9,... | collective-permute-start | bytes 147464 | tf_op jit(solution)/shard_map/ppermute | solution.py:39
  32.0 0.4 collective-permute-start.17
  32.3 1.3 %collective-permute-done.14.refs_0_ = bf16[24,1024]{1,0:T(8,128)(2,1)S(1)} collective-permute-done((bf16[24,1024]{1,0:T(8,128)(2,1)S(1)}, bf16[24,1024]{1,0:T(8,128)(2,1)S(1)}, u32[]{:S(2)}, u32[]{:S(2)}) %collective-permute-start.14) | collective-permute-done | bytes 49184 | tf_op jit(solution)/shard_map/ppermute | solution.py:39
  33.6 1.3 %collective-permute-done.15.refs_1_ = bf16[24,1024]{1,0:T(8,128)(2,1)S(1)} collective-permute-done((bf16[24,1024]{1,0:T(8,128)(2,1)S(1)}, bf16[24,1024]{1,0:T(8,128)(2,1)S(1)}, u32[]{:S(2)}, u32[]{:S(2)}) %collective-permute-start.15) | collective-permute-done | bytes 49184 | tf_op jit(solution)/shard_map/ppermute | solution.py:39
  34.9 0.0 collective-permute-done.16.refs_2_
  35.0 0.0 collective-permute-done.17.refs_3_
  35.0 2.7 %collective-permute-start.18 = (bf16[24,256]{1,0:T(8,128)(2,1)S(1)}, bf16[24,256]{1,0:T(8,128)(2,1)S(1)}, u32[]{:S(2)}, u32[]{:S(2)}) collective-permute-start(bf16[24,256]{1,0:T(8,128)(2,1)S(1)} %get-tuple-element.49), channel_id=1, source_target_pairs={{0,19},{1,18},{2,17},{3,16},{4,23},{5,22},{6,21},{7,20},{8,27},{9,... | collective-permute-start | bytes 36872 | tf_op jit(solution)/shard_map/ppermute | solution.py:39
  37.7 0.0 collective-permute-start.19
  37.7 1.4 %collective-permute-start.20 = (bf16[24,256]{1,0:T(8,128)(2,1)S(1)}, bf16[24,256]{1,0:T(8,128)(2,1)S(1)}, u32[]{:S(2)}, u32[]{:S(2)}) collective-permute-start(bf16[24,256]{1,0:T(8,128)(2,1)S(1)} %get-tuple-element.51), channel_id=1, source_target_pairs={{0,17},{1,16},{2,19},{3,18},{4,21},{5,20},{6,23},{7,22},{8,25},{9,... | collective-permute-start | bytes 36872 | tf_op jit(solution)/shard_map/ppermute | solution.py:39
  39.1 0.2 collective-permute-start.21
  39.3 0.7 %collective-permute-done.18.rest_0_ = bf16[24,256]{1,0:T(8,128)(2,1)S(1)} collective-permute-done((bf16[24,256]{1,0:T(8,128)(2,1)S(1)}, bf16[24,256]{1,0:T(8,128)(2,1)S(1)}, u32[]{:S(2)}, u32[]{:S(2)}) %collective-permute-start.18) | collective-permute-done | bytes 12320 | tf_op jit(solution)/shard_map/ppermute | solution.py:39
  40.0 1.8 %collective-permute-done.19.rest_1_ = bf16[24,256]{1,0:T(8,128)(2,1)S(1)} collective-permute-done((bf16[24,256]{1,0:T(8,128)(2,1)S(1)}, bf16[24,256]{1,0:T(8,128)(2,1)S(1)}, u32[]{:S(2)}, u32[]{:S(2)}) %collective-permute-start.19) | collective-permute-done | bytes 12320 | tf_op jit(solution)/shard_map/ppermute | solution.py:39
  41.7 0.0 collective-permute-done.20.rest_2_
  41.7 0.0 collective-permute-done.21.rest_3_
  41.7 0.6 %final.1 = bf16[24,256]{1,0:T(8,128)(2,1)} custom-call(bf16[24,1152]{1,0:T(8,128)(2,1)S(1)} %middle.1.rest_0_.middle_ref, bf16[24,256]{1,0:T(8,128)(2,1)S(1)} %collective-permute-done.18.rest_0_, bf16[24,256]{1,0:T(8,128)(2,1)S(1)} %collective-permute-done.19.rest_1_, bf16[24,256]{1,0:T(8,128)(2,1)S(1)} %collective-permute-done.20.rest_2_, ...), custom_call_target="tpu_custom_call" | custom-call | tf_op jit(solution)/shard_map/final/pallas_call | solution.py:448
  (4 shorter events, 0.1 us)
Async XLA Ops:
  3.2 5.0 %collective-permute-start = (bf16[24,640]{1,0:T(8,128)(2,1)S(1)}, bf16[24,640]{1,0:T(8,128)(2,1)S(1)}, u32[]{:S(2)}, u32[]{:S(2)}) collective-permute-start(bf16[24,640]{1,0:T(8,128)(2,1)S(1)} %get-tuple-element.33), channel_id=1, source_target_pairs={{0,1},{1,0},{2,3},{3,2},{4,5},{5,4},{6,7},{7,6},{8,9},{9,8},{10,11... | collective-permute-start | bytes 92168 | tf_op jit(solution)/shard_map/ppermute | solution.py:28
  8.6 1.2 %collective-permute-start.1 = (bf16[24,1024]{1,0:T(8,128)(2,1)S(1)}, bf16[24,1024]{1,0:T(8,128)(2,1)S(1)}, u32[]{:S(2)}, u32[]{:S(2)}) collective-permute-start(bf16[24,1024]{1,0:T(8,128)(2,1)S(1)} %get-tuple-element.35), channel_id=1, source_target_pairs={{0,16},{16,0},{1,17},{17,1},{2,18},{18,2},{3,19},{19,3},{4,20},{20... | collective-permute-start | bytes 147464 | tf_op jit(solution)/shard_map/ppermute | solution.py:28
  9.9 7.5 %collective-permute-start.5 = (bf16[24,1024]{1,0:T(8,128)(2,1)S(1)}, bf16[24,1024]{1,0:T(8,128)(2,1)S(1)}, u32[]{:S(2)}, u32[]{:S(2)}) collective-permute-start(bf16[24,1024]{1,0:T(8,128)(2,1)S(1)} %pair.1.after_ref), channel_id=1, source_target_pairs={{0,19},{1,18},{2,17},{3,16},{4,23},{5,22},{6,21},{7,20},{8,27},{9,... | collective-permute-start | bytes 147464 | tf_op jit(solution)/shard_map/ppermute | solution.py:39
  13.8 4.7 %collective-permute-start.4 = (bf16[24,1024]{1,0:T(8,128)(2,1)S(1)}, bf16[24,1024]{1,0:T(8,128)(2,1)S(1)}, u32[]{:S(2)}, u32[]{:S(2)}) collective-permute-start(bf16[24,1024]{1,0:T(8,128)(2,1)S(1)} %pair.1.after_ref), channel_id=1, source_target_pairs={{0,18},{1,19},{2,16},{3,17},{4,22},{5,23},{6,20},{7,21},{8,26},{9,... | collective-permute-start | bytes 147464 | tf_op jit(solution)/shard_map/ppermute | solution.py:39
  13.8 4.7 %collective-permute-start.3 = (bf16[24,1024]{1,0:T(8,128)(2,1)S(1)}, bf16[24,1024]{1,0:T(8,128)(2,1)S(1)}, u32[]{:S(2)}, u32[]{:S(2)}) collective-permute-start(bf16[24,1024]{1,0:T(8,128)(2,1)S(1)} %pair.1.after_ref), channel_id=1, source_target_pairs={{0,17},{1,16},{2,19},{3,18},{4,21},{5,20},{6,23},{7,22},{8,25},{9,... | collective-permute-start | bytes 147464 | tf_op jit(solution)/shard_map/ppermute | solution.py:39
  14.4 4.1 %collective-permute-start.2 = (bf16[24,1024]{1,0:T(8,128)(2,1)S(1)}, bf16[24,1024]{1,0:T(8,128)(2,1)S(1)}, u32[]{:S(2)}, u32[]{:S(2)}) collective-permute-start(bf16[24,1024]{1,0:T(8,128)(2,1)S(1)} %pair.1.after_ref), channel_id=1, source_target_pairs={{0,16},{1,17},{2,18},{3,19},{4,20},{5,21},{6,22},{7,23},{8,24},{9,... | collective-permute-start | bytes 147464 | tf_op jit(solution)/shard_map/ppermute | solution.py:39
  17.4 9.0 %copy-start = (bf16[1,768,2048]{2,1,0:T(8,128)(2,1)S(1)}, bf16[1,768,2048]{2,1,0:T(8,128)(2,1)}, u32[]{:S(2)}) copy-start(bf16[1,768,2048]{2,1,0:T(8,128)(2,1)} %down_ref.3) | copy-start | bytes 9437188
  18.5 4.8 %collective-permute-start.9 = (bf16[24,1152]{1,0:T(8,128)(2,1)S(1)}, bf16[24,1152]{1,0:T(8,128)(2,1)S(1)}, u32[]{:S(2)}, u32[]{:S(2)}) collective-permute-start(bf16[24,1152]{1,0:T(8,128)(2,1)S(1)} %middle.1.rest_0_.middle_ref), channel_id=1, source_target_pairs={{0,28},{1,29},{2,30},{3,31},{4,24},{5,25},{6,26},{7,27},{8,20},{9,... | collective-permute-start | bytes 165896 | tf_op jit(solution)/shard_map/ppermute | solution.py:39
  20.9 3.8 %collective-permute-start.8 = (bf16[24,1152]{1,0:T(8,128)(2,1)S(1)}, bf16[24,1152]{1,0:T(8,128)(2,1)S(1)}, u32[]{:S(2)}, u32[]{:S(2)}) collective-permute-start(bf16[24,1152]{1,0:T(8,128)(2,1)S(1)} %middle.1.rest_0_.middle_ref), channel_id=1, source_target_pairs={{0,24},{1,25},{2,26},{3,27},{4,28},{5,29},{6,30},{7,31},{8,16},{9,... | collective-permute-start | bytes 165896 | tf_op jit(solution)/shard_map/ppermute | solution.py:39
  21.2 3.9 %collective-permute-start.7 = (bf16[24,1152]{1,0:T(8,128)(2,1)S(1)}, bf16[24,1152]{1,0:T(8,128)(2,1)S(1)}, u32[]{:S(2)}, u32[]{:S(2)}) collective-permute-start(bf16[24,1152]{1,0:T(8,128)(2,1)S(1)} %middle.1.rest_0_.middle_ref), channel_id=1, source_target_pairs={{0,20},{1,21},{2,22},{3,23},{4,16},{5,17},{6,18},{7,19},{8,28},{9,... | collective-permute-start | bytes 165896 | tf_op jit(solution)/shard_map/ppermute | solution.py:39
  21.6 3.6 %collective-permute-start.6 = (bf16[24,1152]{1,0:T(8,128)(2,1)S(1)}, bf16[24,1152]{1,0:T(8,128)(2,1)S(1)}, u32[]{:S(2)}, u32[]{:S(2)}) collective-permute-start(bf16[24,1152]{1,0:T(8,128)(2,1)S(1)} %middle.1.rest_0_.middle_ref), channel_id=1, source_target_pairs={{0,16},{1,17},{2,18},{3,19},{4,20},{5,21},{6,22},{7,23},{8,24},{9,... | collective-permute-start | bytes 165896 | tf_op jit(solution)/shard_map/ppermute | solution.py:39
  23.3 2.6 %collective-permute-start.12 = (bf16[24,1152]{1,0:T(8,128)(2,1)S(1)}, bf16[24,1152]{1,0:T(8,128)(2,1)S(1)}, u32[]{:S(2)}, u32[]{:S(2)}) collective-permute-start(bf16[24,1152]{1,0:T(8,128)(2,1)S(1)} %collective-permute-done.9.rest_3_), channel_id=1, source_target_pairs={{0,16},{16,0},{1,17},{17,1},{2,18},{18,2},{3,19},{19,3},{4,20},{20... | collective-permute-start | bytes 165896 | tf_op jit(solution)/shard_map/ppermute | solution.py:28
  24.7 1.4 %collective-permute-start.11 = (bf16[24,1152]{1,0:T(8,128)(2,1)S(1)}, bf16[24,1152]{1,0:T(8,128)(2,1)S(1)}, u32[]{:S(2)}, u32[]{:S(2)}) collective-permute-start(bf16[24,1152]{1,0:T(8,128)(2,1)S(1)} %collective-permute-done.8.rest_2_), channel_id=1, source_target_pairs={{0,16},{16,0},{1,17},{17,1},{2,18},{18,2},{3,19},{19,3},{4,20},{20... | collective-permute-start | bytes 165896 | tf_op jit(solution)/shard_map/ppermute | solution.py:28
  25.2 1.2 %collective-permute-start.10 = (bf16[24,1152]{1,0:T(8,128)(2,1)S(1)}, bf16[24,1152]{1,0:T(8,128)(2,1)S(1)}, u32[]{:S(2)}, u32[]{:S(2)}) collective-permute-start(bf16[24,1152]{1,0:T(8,128)(2,1)S(1)} %collective-permute-done.7.rest_1_), channel_id=1, source_target_pairs={{0,16},{16,0},{1,17},{17,1},{2,18},{18,2},{3,19},{19,3},{4,20},{20... | collective-permute-start | bytes 165896 | tf_op jit(solution)/shard_map/ppermute | solution.py:28
  27.4 1.5 %collective-permute-start.13 = (bf16[96,1024]{1,0:T(8,128)(2,1)S(1)}, bf16[96,1024]{1,0:T(8,128)(2,1)S(1)}, u32[]{:S(2)}, u32[]{:S(2)}) collective-permute-start(bf16[96,1024]{1,0:T(8,128)(2,1)S(1)} %get-tuple-element.44), channel_id=1, source_target_pairs={{0,16},{16,0},{1,17},{17,1},{2,18},{18,2},{3,19},{19,3},{4,20},{20... | collective-permute-start | bytes 589832 | tf_op jit(solution)/shard_map/ppermute | solution.py:28
  28.9 4.7 %collective-permute-start.14 = (bf16[24,1024]{1,0:T(8,128)(2,1)S(1)}, bf16[24,1024]{1,0:T(8,128)(2,1)S(1)}, u32[]{:S(2)}, u32[]{:S(2)}) collective-permute-start(bf16[24,1024]{1,0:T(8,128)(2,1)S(1)} %get-tuple-element.45), channel_id=1, source_target_pairs={{0,28},{1,29},{2,30},{3,31},{4,24},{5,25},{6,26},{7,27},{8,20},{9,... | collective-permute-start | bytes 147464 | tf_op jit(solution)/shard_map/ppermute | solution.py:39
  30.2 4.7 %collective-permute-start.15 = (bf16[24,1024]{1,0:T(8,128)(2,1)S(1)}, bf16[24,1024]{1,0:T(8,128)(2,1)S(1)}, u32[]{:S(2)}, u32[]{:S(2)}) collective-permute-start(bf16[24,1024]{1,0:T(8,128)(2,1)S(1)} %get-tuple-element.46), channel_id=1, source_target_pairs={{0,24},{1,25},{2,26},{3,27},{4,28},{5,29},{6,30},{7,31},{8,16},{9,... | collective-permute-start | bytes 147464 | tf_op jit(solution)/shard_map/ppermute | solution.py:39
  31.4 3.5 %collective-permute-start.16 = (bf16[24,1024]{1,0:T(8,128)(2,1)S(1)}, bf16[24,1024]{1,0:T(8,128)(2,1)S(1)}, u32[]{:S(2)}, u32[]{:S(2)}) collective-permute-start(bf16[24,1024]{1,0:T(8,128)(2,1)S(1)} %get-tuple-element.47), channel_id=1, source_target_pairs={{0,20},{1,21},{2,22},{3,23},{4,16},{5,17},{6,18},{7,19},{8,28},{9,... | collective-permute-start | bytes 147464 | tf_op jit(solution)/shard_map/ppermute | solution.py:39
  32.0 3.0 %collective-permute-start.17 = (bf16[24,1024]{1,0:T(8,128)(2,1)S(1)}, bf16[24,1024]{1,0:T(8,128)(2,1)S(1)}, u32[]{:S(2)}, u32[]{:S(2)}) collective-permute-start(bf16[24,1024]{1,0:T(8,128)(2,1)S(1)} %get-tuple-element.48), channel_id=1, source_target_pairs={{0,16},{1,17},{2,18},{3,19},{4,20},{5,21},{6,22},{7,23},{8,24},{9,... | collective-permute-start | bytes 147464 | tf_op jit(solution)/shard_map/ppermute | solution.py:39
  35.0 5.0 %collective-permute-start.18 = (bf16[24,256]{1,0:T(8,128)(2,1)S(1)}, bf16[24,256]{1,0:T(8,128)(2,1)S(1)}, u32[]{:S(2)}, u32[]{:S(2)}) collective-permute-start(bf16[24,256]{1,0:T(8,128)(2,1)S(1)} %get-tuple-element.49), channel_id=1, source_target_pairs={{0,19},{1,18},{2,17},{3,16},{4,23},{5,22},{6,21},{7,20},{8,27},{9,... | collective-permute-start | bytes 36872 | tf_op jit(solution)/shard_map/ppermute | solution.py:39
  37.7 4.0 %collective-permute-start.19 = (bf16[24,256]{1,0:T(8,128)(2,1)S(1)}, bf16[24,256]{1,0:T(8,128)(2,1)S(1)}, u32[]{:S(2)}, u32[]{:S(2)}) collective-permute-start(bf16[24,256]{1,0:T(8,128)(2,1)S(1)} %get-tuple-element.50), channel_id=1, source_target_pairs={{0,18},{1,19},{2,16},{3,17},{4,22},{5,23},{6,20},{7,21},{8,26},{9,... | collective-permute-start | bytes 36872 | tf_op jit(solution)/shard_map/ppermute | solution.py:39
  37.7 4.0 %collective-permute-start.20 = (bf16[24,256]{1,0:T(8,128)(2,1)S(1)}, bf16[24,256]{1,0:T(8,128)(2,1)S(1)}, u32[]{:S(2)}, u32[]{:S(2)}) collective-permute-start(bf16[24,256]{1,0:T(8,128)(2,1)S(1)} %get-tuple-element.51), channel_id=1, source_target_pairs={{0,17},{1,16},{2,19},{3,18},{4,21},{5,20},{6,23},{7,22},{8,25},{9,... | collective-permute-start | bytes 36872 | tf_op jit(solution)/shard_map/ppermute | solution.py:39
  39.1 2.6 %collective-permute-start.21 = (bf16[24,256]{1,0:T(8,128)(2,1)S(1)}, bf16[24,256]{1,0:T(8,128)(2,1)S(1)}, u32[]{:S(2)}, u32[]{:S(2)}) collective-permute-start(bf16[24,256]{1,0:T(8,128)(2,1)S(1)} %get-tuple-element.52), channel_id=1, source_target_pairs={{0,16},{1,17},{2,18},{3,19},{4,20},{5,21},{6,22},{7,23},{8,24},{9,... | collective-permute-start | bytes 36872 | tf_op jit(solution)/shard_map/ppermute | solution.py:39

commit v6 on v5

--- a/solution.py
+++ b/solution.py
@@ -16,7 +16,7 @@
 TERM = 32
 CUTS = (0, 6, 12, 18, 24)
 CUT_OF = 24
-LAG = 1
+LAG = 2
 F32 = jnp.float32
 BF16 = jnp.bfloat16
 MIB = 1024 * 1024
@@ -62,7 +62,7 @@
     q_hbm, len_hbm, ids_hbm, gates_hbm, kv_hbm = refs[:5]
     own_ref, *send_refs = refs[5 : 5 + kv_parts]
     lanes_ref = refs[5 + kv_parts]
-    kv, q_in, len_ref, ids_ref, gates_ref, turn_s, q_s, score_s, num_s, max_s, sum_s, sems = refs[
+    kv, q_in, len_ref, ids_ref, gates_ref, q_s, score_s, num_s, max_s, sum_s, sems = refs[
         6 + kv_parts :
     ]
     cuts = [rows * c // CUT_OF for c in CUTS]
@@ -87,16 +87,14 @@
         copy.wait()
     for g in range(group_heads):
         q_s[pl.ds(g, rows, stride=group_heads), :] = q_in[:, g * HD : (g + 1) * HD].astype(F32)
-    place = lax.broadcasted_iota(jnp.int32, (HD, rows), 0)
-    target = place % (HD // 2)
-    expert = jnp.where(target < grp, ((1 - section) * grp + target) * tp + tp_index, -1)
-    gate = jnp.zeros((HD, rows), F32)
+    place = lax.broadcasted_iota(jnp.int32, (2 * grp, rows), 0)
+    expert = ((1 - section) * grp + place % grp) * tp + tp_index
+    gate = jnp.zeros((2 * grp, rows), F32)
     for k in range(top):
         gate = gate + jnp.where(ids_ref[k : k + 1, :] == expert, gates_ref[k : k + 1, :], 0.0)
     high = gate.astype(BF16).astype(F32)
-    turn_s[...] = jnp.zeros((HD, HD), F32)
-    turn_s[:, :rows] = jnp.where(place < HD // 2, high, gate - high)
-    lanes_ref[...] = turn_s[...].T[:rows].astype(BF16)
+    lanes_ref[...] = jnp.zeros(lanes_ref.shape, F32)
+    lanes_ref[:, :rows] = jnp.where(place < grp, high, gate - high)
     scale = math.log2(math.e) / math.sqrt(HD)
     place = part * span + lax.broadcasted_iota(jnp.int32, (group_heads, span), 1)
     def spot(r):
@@ -118,10 +116,14 @@
 
     for c, span_of in enumerate(chunks):
         copies[4 + c].wait()
-        for r in range(*span_of):
-            score_s[spot(r), :] = lax.dot_general(
-                q_s[spot(r), :].astype(BF16),
-                kv[r, :, :HD],
+        for r in range(span_of[0], span_of[1], 2):
+            both = pl.ds(r * group_heads, 2 * group_heads)
+            q = q_s[both, :]
+            upper = lax.broadcasted_iota(jnp.int32, q.shape, 0) < group_heads
+            q = jnp.concatenate([jnp.where(upper, q, 0.0), jnp.where(upper, 0.0, q)], axis=1)
+            score_s[both, :] = lax.dot_general(
+                q.astype(BF16),
+                jnp.concatenate([kv[r, :, :HD], kv[r + 1, :, :HD]], axis=1),
                 (((1,), (1,)), ((), ())),
                 preferred_element_type=F32,
             )
@@ -169,7 +171,7 @@
     return call(
         functools.partial(fetch_kernel, parts),
         [after, *arrays],
-        [(a.shape, a.dtype) for a in arrays] + [((rows, HD), BF16)],
+        [(a.shape, a.dtype) for a in arrays] + [((rows, HD), after.dtype)],
         [pltpu.SemaphoreType.DMA((sum(parts),))],
         far=range(1, len(arrays) + 1),
         name="fetch",
@@ -216,36 +218,46 @@
 
 
 def middle_kernel(half, token_ref, resid_ref, lanes_ref, *rest):
-    *parts, out_ref = rest
+    *parts, middle_ref, packet_ref = rest
     cols = pl.ds(pl.multiple_of(lax.axis_index("side") * half, half), half)
     total = parts[0][...].astype(F32)
     for part in parts[1:]:
         total = total + part[...].astype(F32)
-    out_ref[:, :half] = (resid_ref[:, cols].astype(F32) + total).astype(BF16)
-    out_ref[:, half:] = lanes_ref[...]
-
-
-def scaled_rows(packets, gain_ref, side, half):
-    x = jnp.concatenate([p[:, :half].astype(F32) for p in packets], axis=0)
+    middle = (resid_ref[:, cols].astype(F32) + total).astype(BF16)
+    middle_ref[...] = middle
+    middle = middle.astype(F32)
+    blocks = [middle[:, c : c + HD] for c in range(0, half, HD)]
+    packet_ref[...] = jnp.concatenate([*blocks, lanes_ref[...]], axis=0).astype(BF16)
+
+
+def packet_rows(packet, rows, half):
+    packet = packet[...].astype(F32)
+    return jnp.concatenate([packet[c * rows : (c + 1) * rows] for c in range(half // HD)], axis=1)
+
+
+def scaled_rows(packets, rows, gain_ref, side, half):
+    x = jnp.concatenate([packet_rows(p, rows, half) for p in packets], axis=0)
     gain = gain_ref[:, pl.ds(pl.multiple_of(side * half, half), half)]
     return (x * gain).astype(BF16), jnp.sum(x * x, axis=1, keepdims=True)
 
 
-def first_half_kernel(tile, half, gain_ref, w_ref, *rest):
+def first_half_kernel(tile, rows, half, gain_ref, w_ref, *rest):
     *packets, hidden_ref, square_ref, gate_ref = rest
     section = lax.axis_index("side")
     me = lax.axis_index("grp")
-    x, square = scaled_rows(packets, gain_ref, 1 - section, half)
+    x, square = scaled_rows(packets, rows, gain_ref, 1 - section, half)
     square_ref[...] = jnp.broadcast_to(square, square_ref.shape)
-    lanes = jnp.concatenate([p[:, half:].astype(F32) for p in packets], axis=0)
-    lane = lax.broadcasted_iota(jnp.int32, lanes.shape, 1)
-    gate = jnp.sum(jnp.where(lane % (HD // 2) == me, lanes, 0.0), axis=1, keepdims=True)
-    gate_ref[...] = jnp.broadcast_to(gate, gate_ref.shape)
-    rows = pl.ds(pl.multiple_of((1 - section) * half, half), half)
+    for b, packet in enumerate(packets):
+        lanes = packet[...].astype(F32)[half // HD * rows :]
+        row = lax.broadcasted_iota(jnp.int32, lanes.shape, 0)
+        groups = lanes.shape[0] // 2
+        gate = jnp.sum(jnp.where(row % groups == me, lanes, 0.0), axis=0, keepdims=True)
+        gate_ref[b * rows : (b + 1) * rows, :] = jnp.broadcast_to(gate, (HD, HD)).T[:rows]
+    depth = pl.ds(pl.multiple_of((1 - section) * half, half), half)
 
     def column(j, carry):
         cols = pl.ds(j * tile, tile)
-        hidden_ref[:, cols] = jnp.dot(x, w_ref[0, rows, cols], preferred_element_type=F32)
+        hidden_ref[:, cols] = jnp.dot(x, w_ref[0, depth, cols], preferred_element_type=F32)
         return carry
 
     for j in range(hidden_ref.shape[1] // tile):
@@ -253,21 +265,21 @@
 
 
 def second_half_kernel(
-    tile, half, gain_ref, w_ref, hidden_ref, square_ref, gate_ref, down_ref, *rest
+    tile, rows, half, gain_ref, w_ref, hidden_ref, square_ref, gate_ref, down_ref, *rest
 ):
     *packets, act_ref, away_ref = rest
     inner = act_ref.shape[1]
     section = lax.axis_index("side")
-    x, square = scaled_rows(packets, gain_ref, section, half)
+    x, square = scaled_rows(packets, rows, gain_ref, section, half)
     square = square + square_ref[:, :1]
     inv = lax.rsqrt(square / (half * lax.axis_size("side")) + 1e-6)
-    rows = pl.ds(pl.multiple_of(section * half, half), half)
+    depth = pl.ds(pl.multiple_of(section * half, half), half)
 
     def column(j, carry):
         both = []
         for base in (0, inner):
             cols = pl.ds(base + j * tile, tile)
-            part = jnp.dot(x, w_ref[0, rows, cols], preferred_element_type=F32)
+            part = jnp.dot(x, w_ref[0, depth, cols], preferred_element_type=F32)
             both.append((hidden_ref[:, cols] + part) * inv)
         act = both[0] / (1.0 + jnp.exp(-both[0])) * both[1]
         act_ref[:, pl.ds(j * tile, tile)] = act.astype(BF16)
@@ -349,7 +361,7 @@
     piece = width // group_size
     rows, top = expert_ids.shape
     inner = w_down.shape[1]
-    packet = (rows, (per_member + 1) * HD)
+    partial_shape = (rows, (per_member + 1) * HD)
     sizes = (tp, grp, sides, kv_parts, group_heads, per_member, rows, span, top)
     many = rows * group_heads
     results = call(
@@ -361,15 +373,14 @@
             expert_gates.T,
             kv_cache,
         ],
-        [(packet, F32)] + [(packet, BF16)] * (kv_parts - 1)
-        + [((rows, HD), BF16)],
+        [(partial_shape, F32)] + [(partial_shape, BF16)] * (kv_parts - 1)
+        + [((2 * grp, HD), F32)],
         [
             pltpu.VMEM((rows, span, 2 * HD), BF16),
             pltpu.VMEM((rows, group_heads * HD), BF16),
             pltpu.SMEM((rows,), jnp.int32),
             pltpu.VMEM((top, rows), jnp.int32),
             pltpu.VMEM((top, rows), F32),
-            pltpu.VMEM((HD, HD), F32),
             pltpu.VMEM((many, HD), F32),
             pltpu.VMEM((many, span), F32),
             pltpu.VMEM((many + group_heads, HD), F32),
@@ -400,25 +411,25 @@
     outgoing = call(add_kernel, [kept, away], [((rows, half), BF16)], name="pair")[0]
     w_gate_up, token = fetched(outgoing, w_gate_up)
     parts = [crossed(outgoing, 0, mask) for mask in range(tp)]
-    middle = call(
+    middle, packet = call(
         functools.partial(middle_kernel, half),
         [token, resid, gate_lanes, *parts],
-        [((rows, half + HD), BF16)],
+        [((rows, half), BF16), ((half // HD * rows + 2 * grp, HD), BF16)],
         name="middle",
-    )[0]
-    packets = [crossed(middle, mask) for mask in [*range(1, grp), 0]]
+    )
+    packets = [crossed(packet, mask) for mask in [*range(1, grp), 0]]
     packets = [packets[-1], *packets[:-1]]
-    near_packets = [middle] + [swapped(p, "side", 1) for p in packets[1:]]
+    near_packets = [packet] + [swapped(p, "side", 1) for p in packets[1:]]
     total = grp * rows
     tile = 256
     hidden, square, gate = call(
-        functools.partial(first_half_kernel, tile, half),
+        functools.partial(first_half_kernel, tile, rows, half),
         [gain, w_gate_up, *packets],
         [((total, 2 * inner), F32), ((total, HD), F32), ((total, HD), F32)],
         name="first_half",
     )
     act, sent = call(
-        functools.partial(second_half_kernel, tile, half),
+        functools.partial(second_half_kernel, tile, rows, half),
         [gain, w_gate_up, hidden, square, gate, w_down, *near_packets],
         [((total, inner), BF16), ((total, half), BF16)],
         name="second_half",

time: 42.5 us -> 42.2 us (level)
  no operation moved by 1% of the time
where the time goes in v6:
time: 42.2 us; the launch traced here: 42.1 us
  starting transfers between devices  19.7 us (47%)
  waiting for transfers between devices  11.2 us (27%)
  Pallas kernels  11.1 us (26%)
    ppermute x16, starting transfers between devices, crossed(): return lax.ppermute(value, ('side', 'grp', 'tp'), pairs)  15.7 us
    pallas_call x12, Pallas kernels, call(): pl.pallas_call(kernel, out_shape=[pltpu.VMEM(shape, dtype) for shape, dty...  10.4 us
    ppermute x16, waiting for transfers between devices, crossed(): return lax.ppermute(value, ('side', 'grp', 'tp'), pairs)  8.57 us
    ppermute x6, starting transfers between devices, swapped(): return lax.ppermute(value, axis, pairs)  4.04 us
    ppermute x6, waiting for transfers between devices, swapped(): return lax.ppermute(value, axis, pairs)  2.62 us
  transfers between devices with their start and end apart: 22, of which 12 were waited for; matrix products, arithmetic and copies ran while one was open for 0% of the time, Pallas kernels for 14%

profile of v6, /device:TPU:0, one launch (start us, length us, event | category | flops | bytes accessed | tf_op | source)
XLA Modules:
  0.0 42.1 jit_solution(12075124634143443827)
XLA Ops:
  0.0 3.1 %attention.1 = (f32[24,640]{1,0:T(8,128)S(1)}, bf16[24,640]{1,0:T(8,128)(2,1)S(1)}, f32[8,128]{1,0:T(8,128)S(1)}) custom-call(bf16[24,2048]{1,0:T(8,128)(2,1)} %refs_0_.3, s32[24]{0:T(128)} %refs_1_.2, s32[8,24]{1,0:T(8,128)} %bitcast.4, f32[8,24]{1,0:T(8,128)} %bitcast.5, bf16[24,1,384,256]{3,2,1,0:T(8,128)(2,1)} %refs_4_.1), custom_call_target="tpu_custom_call" | custom-call | tf_op jit(solution)/shard_map/attention/pallas_call | solution.py:48
  3.1 3.1 %collective-permute-start = (bf16[24,640]{1,0:T(8,128)(2,1)S(1)}, bf16[24,640]{1,0:T(8,128)(2,1)S(1)}, u32[]{:S(2)}, u32[]{:S(2)}) collective-permute-start(bf16[24,640]{1,0:T(8,128)(2,1)S(1)} %get-tuple-element.35), channel_id=1, source_target_pairs={{0,1},{1,0},{2,3},{3,2},{4,5},{5,4},{6,7},{7,6},{8,9},{9,8},{10,11... | collective-permute-start | bytes 92168 | tf_op jit(solution)/shard_map/ppermute | solution.py:28
  6.2 1.6 %fetch.2 = (bf16[512,2048]{1,0:T(8,128)(2,1)S(1)}, bf16[24,2048]{1,0:T(8,128)(2,1)S(1)}, f32[1,2048]{1,0:T(1,128)S(1)}, f32[8,128]{1,0:T(8,128)S(1)}) custom-call(f32[8,128]{1,0:T(8,128)S(1)} %get-tuple-element.31.after_ref.lanes_ref, bf16[512,2048]{1,0:T(8,128)(2,1)} %refs_0_.4, bf16[24,2048]{1,0:T(8,128)(2,1)} %refs_1_.3, f32[1,2048]{1,0:T(1,128)} %bitcast.3), custom_call_target="tpu_custom_call" | custom-call | bytes 4407296 | tf_op jit(solution)/shard_map/fetch/pallas_call | solution.py:48
  7.8 0.3 collective-permute-done.rest_1_
  8.1 0.5 %project.1 = (bf16[24,512]{1,0:T(8,128)(2,1)S(1)}, bf16[24,1024]{1,0:T(8,128)(2,1)S(1)}) custom-call(f32[8,128]{1,0:T(8,128)S(1)} %get-tuple-element.32.token_ref, bf16[512,2048]{1,0:T(8,128)(2,1)S(1)} %get-tuple-element.33.weight_ref, f32[24,640]{1,0:T(8,128)S(1)} %get-tuple-element.34.rest_0_, bf16[24,640]{1,0:T(8,128)(2,1)S(1)} %collective-permute-done.rest_1_), custom_call_target="tpu_custom_call" | custom-call | tf_op jit(solution)/shard_map/project/pallas_call | solution.py:48
  8.5 0.0 collective-permute-start.1
  8.6 0.3 kept.1.kept_ref
  8.8 0.9 %collective-permute-done.1.came_ref = bf16[24,1024]{1,0:T(8,128)(2,1)S(1)} collective-permute-done((bf16[24,1024]{1,0:T(8,128)(2,1)S(1)}, bf16[24,1024]{1,0:T(8,128)(2,1)S(1)}, u32[]{:S(2)}, u32[]{:S(2)}) %collective-permute-start.1) | collective-permute-done | bytes 49184 | tf_op jit(solution)/shard_map/ppermute | solution.py:28
  9.8 3.9 %collective-permute-start.5 = (bf16[24,1024]{1,0:T(8,128)(2,1)S(1)}, bf16[24,1024]{1,0:T(8,128)(2,1)S(1)}, u32[]{:S(2)}, u32[]{:S(2)}) collective-permute-start(bf16[24,1024]{1,0:T(8,128)(2,1)S(1)} %pair.1.after_ref), channel_id=1, source_target_pairs={{0,19},{1,18},{2,17},{3,16},{4,23},{5,22},{6,21},{7,20},{8,27},{9,... | collective-permute-start | bytes 147464 | tf_op jit(solution)/shard_map/ppermute | solution.py:39
  13.7 0.0 collective-permute-start.4
  13.7 0.6 %collective-permute-start.3 = (bf16[24,1024]{1,0:T(8,128)(2,1)S(1)}, bf16[24,1024]{1,0:T(8,128)(2,1)S(1)}, u32[]{:S(2)}, u32[]{:S(2)}) collective-permute-start(bf16[24,1024]{1,0:T(8,128)(2,1)S(1)} %pair.1.after_ref), channel_id=1, source_target_pairs={{0,17},{1,16},{2,19},{3,18},{4,21},{5,20},{6,23},{7,22},{8,25},{9,... | collective-permute-start | bytes 147464 | tf_op jit(solution)/shard_map/ppermute | solution.py:39
  14.3 0.2 collective-permute-start.2
  14.4 2.9 %fetch.3 = (bf16[1,2048,1536]{2,1,0:T(8,128)(2,1)S(1)}, bf16[24,128]{1,0:T(8,128)(2,1)S(1)}) custom-call(bf16[24,1024]{1,0:T(8,128)(2,1)S(1)} %pair.1.after_ref, bf16[1,2048,1536]{2,1,0:T(8,128)(2,1)} %refs_0_.5), custom_call_target="tpu_custom_call" | custom-call | bytes 12582912 | tf_op jit(solution)/shard_map/fetch/pallas_call | solution.py:48
  17.3 0.0 copy-start
  17.3 0.0 collective-permute-done.5.rest_3_
  17.3 1.0 %collective-permute-done.4.rest_2_ = bf16[24,1024]{1,0:T(8,128)(2,1)S(1)} collective-permute-done((bf16[24,1024]{1,0:T(8,128)(2,1)S(1)}, bf16[24,1024]{1,0:T(8,128)(2,1)S(1)}, u32[]{:S(2)}, u32[]{:S(2)}) %collective-permute-start.4) | collective-permute-done | bytes 49184 | tf_op jit(solution)/shard_map/ppermute | solution.py:39
  18.3 0.0 collective-permute-done.3.rest_1_
  18.3 0.0 collective-permute-done.2.rest_0_
  18.4 2.4 %collective-permute-start.9 = (bf16[200,128]{1,0:T(8,128)(2,1)S(1)}, bf16[200,128]{1,0:T(8,128)(2,1)S(1)}, u32[]{:S(2)}, u32[]{:S(2)}) collective-permute-start(bf16[200,128]{1,0:T(8,128)(2,1)S(1)} %get-tuple-element.43.rest_0_), channel_id=1, source_target_pairs={{0,28},{1,29},{2,30},{3,31},{4,24},{5,25},{6,26},{7,27},{8,20},{9,... | collective-permute-start | bytes 153608 | tf_op jit(solution)/shard_map/ppermute | solution.py:39
  20.8 0.4 collective-permute-start.8
  21.1 0.4 collective-permute-start.7
  21.5 0.3 collective-permute-start.6
  21.8 1.3 %collective-permute-done.9.rest_3_ = bf16[200,128]{1,0:T(8,128)(2,1)S(1)} collective-permute-done((bf16[200,128]{1,0:T(8,128)(2,1)S(1)}, bf16[200,128]{1,0:T(8,128)(2,1)S(1)}, u32[]{:S(2)}, u32[]{:S(2)}) %collective-permute-start.9) | collective-permute-done | bytes 51232 | tf_op jit(solution)/shard_map/ppermute | solution.py:39
  23.1 0.2 collective-permute-start.12
  23.3 1.2 %collective-permute-done.8.rest_2_ = bf16[200,128]{1,0:T(8,128)(2,1)S(1)} collective-permute-done((bf16[200,128]{1,0:T(8,128)(2,1)S(1)}, bf16[200,128]{1,0:T(8,128)(2,1)S(1)}, u32[]{:S(2)}, u32[]{:S(2)}) %collective-permute-start.8) | collective-permute-done | bytes 51232 | tf_op jit(solution)/shard_map/ppermute | solution.py:39
  24.5 0.5 %collective-permute-start.11 = (bf16[200,128]{1,0:T(8,128)(2,1)S(1)}, bf16[200,128]{1,0:T(8,128)(2,1)S(1)}, u32[]{:S(2)}, u32[]{:S(2)}) collective-permute-start(bf16[200,128]{1,0:T(8,128)(2,1)S(1)} %collective-permute-done.8.rest_2_), channel_id=1, source_target_pairs={{0,16},{16,0},{1,17},{17,1},{2,18},{18,2},{3,19},{19,3},{4,20},{20... | collective-permute-start | bytes 153608 | tf_op jit(solution)/shard_map/ppermute | solution.py:28
  25.0 0.0 collective-permute-done.7.rest_1_
  25.0 0.1 collective-permute-start.10
  25.0 0.0 collective-permute-done.6.rest_0_
  25.0 0.6 %first_half.1 = (f32[96,1536]{1,0:T(8,128)S(1)}, f32[96,128]{1,0:T(8,128)S(1)}, f32[96,128]{1,0:T(8,128)S(1)}) custom-call(f32[1,2048]{1,0:T(1,128)S(1)} %get-tuple-element.41.gain_ref, bf16[1,2048,1536]{2,1,0:T(8,128)(2,1)S(1)} %get-tuple-element.42.w_ref, bf16[200,128]{1,0:T(8,128)(2,1)S(1)} %collective-permute-done.6.rest_0_, ...), custom_call_target="tpu_custom_call" | custom-call | tf_op jit(solution)/shard_map/first_half/pallas_call | solution.py:48
  25.7 0.0 collective-permute-done.12.rest_3_
  25.7 0.2 collective-permute-done.11.rest_2_
  25.9 0.4 collective-permute-done.10.rest_1_
  26.2 0.0 copy-done
  26.2 1.0 %second_half.1 = (bf16[96,768]{1,0:T(8,128)(2,1)S(1)}, bf16[96,1024]{1,0:T(8,128)(2,1)S(1)}) custom-call(f32[1,2048]{1,0:T(1,128)S(1)} %get-tuple-element.41.gain_ref, bf16[1,2048,1536]{2,1,0:T(8,128)(2,1)S(1)} %get-tuple-element.42.w_ref, f32[96,1536]{1,0:T(8,128)S(1)} %get-tuple-element.44.hidden_ref, f32[96,128]{1,0:T(8,128)S(1)} %get-tuple-element.45.square_ref, ...), custom_call_target="tpu_custom_call" | custom-call | tf_op jit(solution)/shard_map/second_half/pallas_call | solution.py:48
  27.2 0.2 collective-permute-start.13
  27.4 0.4 keep.1.kept_ref
  27.8 0.9 %collective-permute-done.13.came_ref = bf16[96,1024]{1,0:T(8,128)(2,1)S(1)} collective-permute-done((bf16[96,1024]{1,0:T(8,128)(2,1)S(1)}, bf16[96,1024]{1,0:T(8,128)(2,1)S(1)}, u32[]{:S(2)}, u32[]{:S(2)}) %collective-permute-start.13) | collective-permute-done | bytes 196640 | tf_op jit(solution)/shard_map/ppermute | solution.py:28
  28.7 1.3 %collective-permute-start.14 = (bf16[24,1024]{1,0:T(8,128)(2,1)S(1)}, bf16[24,1024]{1,0:T(8,128)(2,1)S(1)}, u32[]{:S(2)}, u32[]{:S(2)}) collective-permute-start(bf16[24,1024]{1,0:T(8,128)(2,1)S(1)} %get-tuple-element.49), channel_id=1, source_target_pairs={{0,28},{1,29},{2,30},{3,31},{4,24},{5,25},{6,26},{7,27},{8,20},{9,... | collective-permute-start | bytes 147464 | tf_op jit(solution)/shard_map/ppermute | solution.py:39
  30.1 1.1 %collective-permute-start.15 = (bf16[24,1024]{1,0:T(8,128)(2,1)S(1)}, bf16[24,1024]{1,0:T(8,128)(2,1)S(1)}, u32[]{:S(2)}, u32[]{:S(2)}) collective-permute-start(bf16[24,1024]{1,0:T(8,128)(2,1)S(1)} %get-tuple-element.50), channel_id=1, source_target_pairs={{0,24},{1,25},{2,26},{3,27},{4,28},{5,29},{6,30},{7,31},{8,16},{9,... | collective-permute-start | bytes 147464 | tf_op jit(solution)/shard_map/ppermute | solution.py:39
  31.2 0.6 %collective-permute-start.16 = (bf16[24,1024]{1,0:T(8,128)(2,1)S(1)}, bf16[24,1024]{1,0:T(8,128)(2,1)S(1)}, u32[]{:S(2)}, u32[]{:S(2)}) collective-permute-start(bf16[24,1024]{1,0:T(8,128)(2,1)S(1)} %get-tuple-element.51), channel_id=1, source_target_pairs={{0,20},{1,21},{2,22},{3,23},{4,16},{5,17},{6,18},{7,19},{8,28},{9,... | collective-permute-start | bytes 147464 | tf_op jit(solution)/shard_map/ppermute | solution.py:39
  31.8 0.4 collective-permute-start.17
  32.1 1.3 %collective-permute-done.14.refs_0_ = bf16[24,1024]{1,0:T(8,128)(2,1)S(1)} collective-permute-done((bf16[24,1024]{1,0:T(8,128)(2,1)S(1)}, bf16[24,1024]{1,0:T(8,128)(2,1)S(1)}, u32[]{:S(2)}, u32[]{:S(2)}) %collective-permute-start.14) | collective-permute-done | bytes 49184 | tf_op jit(solution)/shard_map/ppermute | solution.py:39
  33.4 1.3 %collective-permute-done.15.refs_1_ = bf16[24,1024]{1,0:T(8,128)(2,1)S(1)} collective-permute-done((bf16[24,1024]{1,0:T(8,128)(2,1)S(1)}, bf16[24,1024]{1,0:T(8,128)(2,1)S(1)}, u32[]{:S(2)}, u32[]{:S(2)}) %collective-permute-start.15) | collective-permute-done | bytes 49184 | tf_op jit(solution)/shard_map/ppermute | solution.py:39
  34.7 0.0 collective-permute-done.16.refs_2_
  34.7 0.0 collective-permute-done.17.refs_3_
  34.8 2.7 %collective-permute-start.18 = (bf16[24,256]{1,0:T(8,128)(2,1)S(1)}, bf16[24,256]{1,0:T(8,128)(2,1)S(1)}, u32[]{:S(2)}, u32[]{:S(2)}) collective-permute-start(bf16[24,256]{1,0:T(8,128)(2,1)S(1)} %get-tuple-element.53), channel_id=1, source_target_pairs={{0,19},{1,18},{2,17},{3,16},{4,23},{5,22},{6,21},{7,20},{8,27},{9,... | collective-permute-start | bytes 36872 | tf_op jit(solution)/shard_map/ppermute | solution.py:39
  37.5 0.0 collective-permute-start.19
  37.5 1.4 %collective-permute-start.20 = (bf16[24,256]{1,0:T(8,128)(2,1)S(1)}, bf16[24,256]{1,0:T(8,128)(2,1)S(1)}, u32[]{:S(2)}, u32[]{:S(2)}) collective-permute-start(bf16[24,256]{1,0:T(8,128)(2,1)S(1)} %get-tuple-element.55), channel_id=1, source_target_pairs={{0,17},{1,16},{2,19},{3,18},{4,21},{5,20},{6,23},{7,22},{8,25},{9,... | collective-permute-start | bytes 36872 | tf_op jit(solution)/shard_map/ppermute | solution.py:39
  38.9 0.2 collective-permute-start.21
  39.1 0.7 %collective-permute-done.18.rest_0_ = bf16[24,256]{1,0:T(8,128)(2,1)S(1)} collective-permute-done((bf16[24,256]{1,0:T(8,128)(2,1)S(1)}, bf16[24,256]{1,0:T(8,128)(2,1)S(1)}, u32[]{:S(2)}, u32[]{:S(2)}) %collective-permute-start.18) | collective-permute-done | bytes 12320 | tf_op jit(solution)/shard_map/ppermute | solution.py:39
  39.8 1.7 %collective-permute-done.19.rest_1_ = bf16[24,256]{1,0:T(8,128)(2,1)S(1)} collective-permute-done((bf16[24,256]{1,0:T(8,128)(2,1)S(1)}, bf16[24,256]{1,0:T(8,128)(2,1)S(1)}, u32[]{:S(2)}, u32[]{:S(2)}) %collective-permute-start.19) | collective-permute-done | bytes 12320 | tf_op jit(solution)/shard_map/ppermute | solution.py:39
  41.5 0.0 collective-permute-done.20.rest_2_
  41.5 0.0 collective-permute-done.21.rest_3_
  41.5 0.6 %final.1 = bf16[24,256]{1,0:T(8,128)(2,1)} custom-call(bf16[24,1024]{1,0:T(8,128)(2,1)S(1)} %get-tuple-element.40.middle_ref, bf16[24,256]{1,0:T(8,128)(2,1)S(1)} %collective-permute-done.18.rest_0_, bf16[24,256]{1,0:T(8,128)(2,1)S(1)} %collective-permute-done.19.rest_1_, bf16[24,256]{1,0:T(8,128)(2,1)S(1)} %collective-permute-done.20.rest_2_, ...), custom_call_target="tpu_custom_call" | custom-call | tf_op jit(solution)/shard_map/final/pallas_call | solution.py:459
  (4 shorter events, 0.1 us)
Async XLA Ops:
  3.1 5.0 %collective-permute-start = (bf16[24,640]{1,0:T(8,128)(2,1)S(1)}, bf16[24,640]{1,0:T(8,128)(2,1)S(1)}, u32[]{:S(2)}, u32[]{:S(2)}) collective-permute-start(bf16[24,640]{1,0:T(8,128)(2,1)S(1)} %get-tuple-element.35), channel_id=1, source_target_pairs={{0,1},{1,0},{2,3},{3,2},{4,5},{5,4},{6,7},{7,6},{8,9},{9,8},{10,11... | collective-permute-start | bytes 92168 | tf_op jit(solution)/shard_map/ppermute | solution.py:28
  8.5 1.2 %collective-permute-start.1 = (bf16[24,1024]{1,0:T(8,128)(2,1)S(1)}, bf16[24,1024]{1,0:T(8,128)(2,1)S(1)}, u32[]{:S(2)}, u32[]{:S(2)}) collective-permute-start(bf16[24,1024]{1,0:T(8,128)(2,1)S(1)} %get-tuple-element.37), channel_id=1, source_target_pairs={{0,16},{16,0},{1,17},{17,1},{2,18},{18,2},{3,19},{19,3},{4,20},{20... | collective-permute-start | bytes 147464 | tf_op jit(solution)/shard_map/ppermute | solution.py:28
  9.8 7.5 %collective-permute-start.5 = (bf16[24,1024]{1,0:T(8,128)(2,1)S(1)}, bf16[24,1024]{1,0:T(8,128)(2,1)S(1)}, u32[]{:S(2)}, u32[]{:S(2)}) collective-permute-start(bf16[24,1024]{1,0:T(8,128)(2,1)S(1)} %pair.1.after_ref), channel_id=1, source_target_pairs={{0,19},{1,18},{2,17},{3,16},{4,23},{5,22},{6,21},{7,20},{8,27},{9,... | collective-permute-start | bytes 147464 | tf_op jit(solution)/shard_map/ppermute | solution.py:39
  13.7 4.7 %collective-permute-start.4 = (bf16[24,1024]{1,0:T(8,128)(2,1)S(1)}, bf16[24,1024]{1,0:T(8,128)(2,1)S(1)}, u32[]{:S(2)}, u32[]{:S(2)}) collective-permute-start(bf16[24,1024]{1,0:T(8,128)(2,1)S(1)} %pair.1.after_ref), channel_id=1, source_target_pairs={{0,18},{1,19},{2,16},{3,17},{4,22},{5,23},{6,20},{7,21},{8,26},{9,... | collective-permute-start | bytes 147464 | tf_op jit(solution)/shard_map/ppermute | solution.py:39
  13.7 4.7 %collective-permute-start.3 = (bf16[24,1024]{1,0:T(8,128)(2,1)S(1)}, bf16[24,1024]{1,0:T(8,128)(2,1)S(1)}, u32[]{:S(2)}, u32[]{:S(2)}) collective-permute-start(bf16[24,1024]{1,0:T(8,128)(2,1)S(1)} %pair.1.after_ref), channel_id=1, source_target_pairs={{0,17},{1,16},{2,19},{3,18},{4,21},{5,20},{6,23},{7,22},{8,25},{9,... | collective-permute-start | bytes 147464 | tf_op jit(solution)/shard_map/ppermute | solution.py:39
  14.3 4.1 %collective-permute-start.2 = (bf16[24,1024]{1,0:T(8,128)(2,1)S(1)}, bf16[24,1024]{1,0:T(8,128)(2,1)S(1)}, u32[]{:S(2)}, u32[]{:S(2)}) collective-permute-start(bf16[24,1024]{1,0:T(8,128)(2,1)S(1)} %pair.1.after_ref), channel_id=1, source_target_pairs={{0,16},{1,17},{2,18},{3,19},{4,20},{5,21},{6,22},{7,23},{8,24},{9,... | collective-permute-start | bytes 147464 | tf_op jit(solution)/shard_map/ppermute | solution.py:39
  17.3 8.9 %copy-start = (bf16[1,768,2048]{2,1,0:T(8,128)(2,1)S(1)}, bf16[1,768,2048]{2,1,0:T(8,128)(2,1)}, u32[]{:S(2)}) copy-start(bf16[1,768,2048]{2,1,0:T(8,128)(2,1)} %down_ref.3) | copy-start | bytes 9437188
  18.4 4.7 %collective-permute-start.9 = (bf16[200,128]{1,0:T(8,128)(2,1)S(1)}, bf16[200,128]{1,0:T(8,128)(2,1)S(1)}, u32[]{:S(2)}, u32[]{:S(2)}) collective-permute-start(bf16[200,128]{1,0:T(8,128)(2,1)S(1)} %get-tuple-element.43.rest_0_), channel_id=1, source_target_pairs={{0,28},{1,29},{2,30},{3,31},{4,24},{5,25},{6,26},{7,27},{8,20},{9,... | collective-permute-start | bytes 153608 | tf_op jit(solution)/shard_map/ppermute | solution.py:39
  20.8 3.7 %collective-permute-start.8 = (bf16[200,128]{1,0:T(8,128)(2,1)S(1)}, bf16[200,128]{1,0:T(8,128)(2,1)S(1)}, u32[]{:S(2)}, u32[]{:S(2)}) collective-permute-start(bf16[200,128]{1,0:T(8,128)(2,1)S(1)} %get-tuple-element.43.rest_0_), channel_id=1, source_target_pairs={{0,24},{1,25},{2,26},{3,27},{4,28},{5,29},{6,30},{7,31},{8,16},{9,... | collective-permute-start | bytes 153608 | tf_op jit(solution)/shard_map/ppermute | solution.py:39
  21.1 3.8 %collective-permute-start.7 = (bf16[200,128]{1,0:T(8,128)(2,1)S(1)}, bf16[200,128]{1,0:T(8,128)(2,1)S(1)}, u32[]{:S(2)}, u32[]{:S(2)}) collective-permute-start(bf16[200,128]{1,0:T(8,128)(2,1)S(1)} %get-tuple-element.43.rest_0_), channel_id=1, source_target_pairs={{0,20},{1,21},{2,22},{3,23},{4,16},{5,17},{6,18},{7,19},{8,28},{9,... | collective-permute-start | bytes 153608 | tf_op jit(solution)/shard_map/ppermute | solution.py:39
  21.5 3.5 %collective-permute-start.6 = (bf16[200,128]{1,0:T(8,128)(2,1)S(1)}, bf16[200,128]{1,0:T(8,128)(2,1)S(1)}, u32[]{:S(2)}, u32[]{:S(2)}) collective-permute-start(bf16[200,128]{1,0:T(8,128)(2,1)S(1)} %get-tuple-element.43.rest_0_), channel_id=1, source_target_pairs={{0,16},{1,17},{2,18},{3,19},{4,20},{5,21},{6,22},{7,23},{8,24},{9,... | collective-permute-start | bytes 153608 | tf_op jit(solution)/shard_map/ppermute | solution.py:39
  23.1 2.6 %collective-permute-start.12 = (bf16[200,128]{1,0:T(8,128)(2,1)S(1)}, bf16[200,128]{1,0:T(8,128)(2,1)S(1)}, u32[]{:S(2)}, u32[]{:S(2)}) collective-permute-start(bf16[200,128]{1,0:T(8,128)(2,1)S(1)} %collective-permute-done.9.rest_3_), channel_id=1, source_target_pairs={{0,16},{16,0},{1,17},{17,1},{2,18},{18,2},{3,19},{19,3},{4,20},{20... | collective-permute-start | bytes 153608 | tf_op jit(solution)/shard_map/ppermute | solution.py:28
  24.5 1.4 %collective-permute-start.11 = (bf16[200,128]{1,0:T(8,128)(2,1)S(1)}, bf16[200,128]{1,0:T(8,128)(2,1)S(1)}, u32[]{:S(2)}, u32[]{:S(2)}) collective-permute-start(bf16[200,128]{1,0:T(8,128)(2,1)S(1)} %collective-permute-done.8.rest_2_), channel_id=1, source_target_pairs={{0,16},{16,0},{1,17},{17,1},{2,18},{18,2},{3,19},{19,3},{4,20},{20... | collective-permute-start | bytes 153608 | tf_op jit(solution)/shard_map/ppermute | solution.py:28
  25.0 1.2 %collective-permute-start.10 = (bf16[200,128]{1,0:T(8,128)(2,1)S(1)}, bf16[200,128]{1,0:T(8,128)(2,1)S(1)}, u32[]{:S(2)}, u32[]{:S(2)}) collective-permute-start(bf16[200,128]{1,0:T(8,128)(2,1)S(1)} %collective-permute-done.7.rest_1_), channel_id=1, source_target_pairs={{0,16},{16,0},{1,17},{17,1},{2,18},{18,2},{3,19},{19,3},{4,20},{20... | collective-permute-start | bytes 153608 | tf_op jit(solution)/shard_map/ppermute | solution.py:28
  27.2 1.5 %collective-permute-start.13 = (bf16[96,1024]{1,0:T(8,128)(2,1)S(1)}, bf16[96,1024]{1,0:T(8,128)(2,1)S(1)}, u32[]{:S(2)}, u32[]{:S(2)}) collective-permute-start(bf16[96,1024]{1,0:T(8,128)(2,1)S(1)} %get-tuple-element.48), channel_id=1, source_target_pairs={{0,16},{16,0},{1,17},{17,1},{2,18},{18,2},{3,19},{19,3},{4,20},{20... | collective-permute-start | bytes 589832 | tf_op jit(solution)/shard_map/ppermute | solution.py:28
  28.7 4.7 %collective-permute-start.14 = (bf16[24,1024]{1,0:T(8,128)(2,1)S(1)}, bf16[24,1024]{1,0:T(8,128)(2,1)S(1)}, u32[]{:S(2)}, u32[]{:S(2)}) collective-permute-start(bf16[24,1024]{1,0:T(8,128)(2,1)S(1)} %get-tuple-element.49), channel_id=1, source_target_pairs={{0,28},{1,29},{2,30},{3,31},{4,24},{5,25},{6,26},{7,27},{8,20},{9,... | collective-permute-start | bytes 147464 | tf_op jit(solution)/shard_map/ppermute | solution.py:39
  30.1 4.7 %collective-permute-start.15 = (bf16[24,1024]{1,0:T(8,128)(2,1)S(1)}, bf16[24,1024]{1,0:T(8,128)(2,1)S(1)}, u32[]{:S(2)}, u32[]{:S(2)}) collective-permute-start(bf16[24,1024]{1,0:T(8,128)(2,1)S(1)} %get-tuple-element.50), channel_id=1, source_target_pairs={{0,24},{1,25},{2,26},{3,27},{4,28},{5,29},{6,30},{7,31},{8,16},{9,... | collective-permute-start | bytes 147464 | tf_op jit(solution)/shard_map/ppermute | solution.py:39
  31.2 3.6 %collective-permute-start.16 = (bf16[24,1024]{1,0:T(8,128)(2,1)S(1)}, bf16[24,1024]{1,0:T(8,128)(2,1)S(1)}, u32[]{:S(2)}, u32[]{:S(2)}) collective-permute-start(bf16[24,1024]{1,0:T(8,128)(2,1)S(1)} %get-tuple-element.51), channel_id=1, source_target_pairs={{0,20},{1,21},{2,22},{3,23},{4,16},{5,17},{6,18},{7,19},{8,28},{9,... | collective-permute-start | bytes 147464 | tf_op jit(solution)/shard_map/ppermute | solution.py:39
  31.8 3.0 %collective-permute-start.17 = (bf16[24,1024]{1,0:T(8,128)(2,1)S(1)}, bf16[24,1024]{1,0:T(8,128)(2,1)S(1)}, u32[]{:S(2)}, u32[]{:S(2)}) collective-permute-start(bf16[24,1024]{1,0:T(8,128)(2,1)S(1)} %get-tuple-element.52), channel_id=1, source_target_pairs={{0,16},{1,17},{2,18},{3,19},{4,20},{5,21},{6,22},{7,23},{8,24},{9,... | collective-permute-start | bytes 147464 | tf_op jit(solution)/shard_map/ppermute | solution.py:39
  34.8 5.0 %collective-permute-start.18 = (bf16[24,256]{1,0:T(8,128)(2,1)S(1)}, bf16[24,256]{1,0:T(8,128)(2,1)S(1)}, u32[]{:S(2)}, u32[]{:S(2)}) collective-permute-start(bf16[24,256]{1,0:T(8,128)(2,1)S(1)} %get-tuple-element.53), channel_id=1, source_target_pairs={{0,19},{1,18},{2,17},{3,16},{4,23},{5,22},{6,21},{7,20},{8,27},{9,... | collective-permute-start | bytes 36872 | tf_op jit(solution)/shard_map/ppermute | solution.py:39
  37.5 4.0 %collective-permute-start.19 = (bf16[24,256]{1,0:T(8,128)(2,1)S(1)}, bf16[24,256]{1,0:T(8,128)(2,1)S(1)}, u32[]{:S(2)}, u32[]{:S(2)}) collective-permute-start(bf16[24,256]{1,0:T(8,128)(2,1)S(1)} %get-tuple-element.54), channel_id=1, source_target_pairs={{0,18},{1,19},{2,16},{3,17},{4,22},{5,23},{6,20},{7,21},{8,26},{9,... | collective-permute-start | bytes 36872 | tf_op jit(solution)/shard_map/ppermute | solution.py:39
  37.5 4.0 %collective-permute-start.20 = (bf16[24,256]{1,0:T(8,128)(2,1)S(1)}, bf16[24,256]{1,0:T(8,128)(2,1)S(1)}, u32[]{:S(2)}, u32[]{:S(2)}) collective-permute-start(bf16[24,256]{1,0:T(8,128)(2,1)S(1)} %get-tuple-element.55), channel_id=1, source_target_pairs={{0,17},{1,16},{2,19},{3,18},{4,21},{5,20},{6,23},{7,22},{8,25},{9,... | collective-permute-start | bytes 36872 | tf_op jit(solution)/shard_map/ppermute | solution.py:39
  38.9 2.6 %collective-permute-start.21 = (bf16[24,256]{1,0:T(8,128)(2,1)S(1)}, bf16[24,256]{1,0:T(8,128)(2,1)S(1)}, u32[]{:S(2)}, u32[]{:S(2)}) collective-permute-start(bf16[24,256]{1,0:T(8,128)(2,1)S(1)} %get-tuple-element.56), channel_id=1, source_target_pairs={{0,16},{1,17},{2,18},{3,19},{4,20},{5,21},{6,22},{7,23},{8,24},{9,... | collective-permute-start | bytes 36872 | tf_op jit(solution)/shard_map/ppermute | solution.py:39

commit v7 on v6

--- a/solution.py
+++ b/solution.py
@@ -196,12 +196,22 @@
     factors = [jnp.exp2((top - highest) * scale) for top in tops]
     total_sum = functools.reduce(jnp.add, [f * v for f, v in zip(factors, sums)])
     factors = [f / total_sum for f in factors]
-    for i in range(per_member):
-        total = 0.0
-        for p, f in zip(packets, factors):
-            total = total + p[:, i * HD : (i + 1) * HD].astype(F32) * f[:, i : i + 1]
-        heads_ref[:, i * HD : (i + 1) * HD] = total.astype(BF16)
-    part_kernel(False, heads_ref, weight_ref, away_ref)
+    section = lax.axis_index("side")
+    cols = pl.ds(pl.multiple_of(section * half, half), half)
+    projected = 0.0
+    for first in range(0, per_member, 2):
+        pair = []
+        for i in range(first, min(first + 2, per_member)):
+            total = 0.0
+            for p, f in zip(packets, factors):
+                total = total + p[:, i * HD : (i + 1) * HD].astype(F32) * f[:, i : i + 1]
+            pair.append(total.astype(BF16))
+            heads_ref[:, i * HD : (i + 1) * HD] = pair[-1]
+        depth = slice(first * HD, (first + len(pair)) * HD)
+        projected = projected + jnp.dot(
+            jnp.concatenate(pair, axis=1), weight_ref[depth, cols], preferred_element_type=F32
+        )
+    away_ref[...] = projected.astype(BF16)
 
 
 def part_kernel(mine, heads_ref, weight_ref, out_ref):

time: 42.2 us -> 42.3 us (level)
  no operation moved by 1% of the time
where the time goes in v7:
time: 42.3 us; the launch traced here: 42.1 us
  starting transfers between devices  19.8 us (47%)
  waiting for transfers between devices  11.2 us (26%)
  Pallas kernels  11 us (26%)
    ppermute x16, starting transfers between devices, crossed(): return lax.ppermute(value, ('side', 'grp', 'tp'), pairs)  15.7 us
    pallas_call x12, Pallas kernels, call(): pl.pallas_call(kernel, out_shape=[pltpu.VMEM(shape, dtype) for shape, dty...  10.4 us
    ppermute x16, waiting for transfers between devices, crossed(): return lax.ppermute(value, ('side', 'grp', 'tp'), pairs)  8.58 us
    ppermute x6, starting transfers between devices, swapped(): return lax.ppermute(value, axis, pairs)  4.08 us
    ppermute x6, waiting for transfers between devices, swapped(): return lax.ppermute(value, axis, pairs)  2.61 us
  transfers between devices with their start and end apart: 22, of which 12 were waited for; matrix products, arithmetic and copies ran while one was open for 0% of the time, Pallas kernels for 14%

profile of v7, /device:TPU:0, one launch (start us, length us, event | category | flops | bytes accessed | tf_op | source)
XLA Modules:
  0.0 42.1 jit_solution(1830104724180204277)
XLA Ops:
  0.0 3.1 %attention.1 = (f32[24,640]{1,0:T(8,128)S(1)}, bf16[24,640]{1,0:T(8,128)(2,1)S(1)}, f32[8,128]{1,0:T(8,128)S(1)}) custom-call(bf16[24,2048]{1,0:T(8,128)(2,1)} %refs_0_.3, s32[24]{0:T(128)} %refs_1_.2, s32[8,24]{1,0:T(8,128)} %bitcast.4, f32[8,24]{1,0:T(8,128)} %bitcast.5, bf16[24,1,384,256]{3,2,1,0:T(8,128)(2,1)} %refs_4_.1), custom_call_target="tpu_custom_call" | custom-call | tf_op jit(solution)/shard_map/attention/pallas_call | solution.py:48
  3.1 3.1 %collective-permute-start = (bf16[24,640]{1,0:T(8,128)(2,1)S(1)}, bf16[24,640]{1,0:T(8,128)(2,1)S(1)}, u32[]{:S(2)}, u32[]{:S(2)}) collective-permute-start(bf16[24,640]{1,0:T(8,128)(2,1)S(1)} %get-tuple-element.35), channel_id=1, source_target_pairs={{0,1},{1,0},{2,3},{3,2},{4,5},{5,4},{6,7},{7,6},{8,9},{9,8},{10,11... | collective-permute-start | bytes 92168 | tf_op jit(solution)/shard_map/ppermute | solution.py:28
  6.2 1.6 %fetch.2 = (bf16[512,2048]{1,0:T(8,128)(2,1)S(1)}, bf16[24,2048]{1,0:T(8,128)(2,1)S(1)}, f32[1,2048]{1,0:T(1,128)S(1)}, f32[8,128]{1,0:T(8,128)S(1)}) custom-call(f32[8,128]{1,0:T(8,128)S(1)} %get-tuple-element.31.after_ref.lanes_ref, bf16[512,2048]{1,0:T(8,128)(2,1)} %refs_0_.4, bf16[24,2048]{1,0:T(8,128)(2,1)} %refs_1_.3, f32[1,2048]{1,0:T(1,128)} %bitcast.3), custom_call_target="tpu_custom_call" | custom-call | bytes 4407296 | tf_op jit(solution)/shard_map/fetch/pallas_call | solution.py:48
  7.8 0.3 collective-permute-done.rest_1_
  8.1 0.5 %project.1 = (bf16[24,512]{1,0:T(8,128)(2,1)S(1)}, bf16[24,1024]{1,0:T(8,128)(2,1)S(1)}) custom-call(f32[8,128]{1,0:T(8,128)S(1)} %get-tuple-element.32.token_ref, bf16[512,2048]{1,0:T(8,128)(2,1)S(1)} %get-tuple-element.33.weight_ref, f32[24,640]{1,0:T(8,128)S(1)} %get-tuple-element.34.rest_0_, bf16[24,640]{1,0:T(8,128)(2,1)S(1)} %collective-permute-done.rest_1_), custom_call_target="tpu_custom_call" | custom-call | tf_op jit(solution)/shard_map/project/pallas_call | solution.py:48
  8.5 0.1 collective-permute-start.1
  8.6 0.3 kept.1.kept_ref
  8.9 0.9 %collective-permute-done.1.came_ref = bf16[24,1024]{1,0:T(8,128)(2,1)S(1)} collective-permute-done((bf16[24,1024]{1,0:T(8,128)(2,1)S(1)}, bf16[24,1024]{1,0:T(8,128)(2,1)S(1)}, u32[]{:S(2)}, u32[]{:S(2)}) %collective-permute-start.1) | collective-permute-done | bytes 49184 | tf_op jit(solution)/shard_map/ppermute | solution.py:28
  9.8 3.9 %collective-permute-start.5 = (bf16[24,1024]{1,0:T(8,128)(2,1)S(1)}, bf16[24,1024]{1,0:T(8,128)(2,1)S(1)}, u32[]{:S(2)}, u32[]{:S(2)}) collective-permute-start(bf16[24,1024]{1,0:T(8,128)(2,1)S(1)} %pair.1.after_ref), channel_id=1, source_target_pairs={{0,19},{1,18},{2,17},{3,16},{4,23},{5,22},{6,21},{7,20},{8,27},{9,... | collective-permute-start | bytes 147464 | tf_op jit(solution)/shard_map/ppermute | solution.py:39
  13.7 0.0 collective-permute-start.4
  13.7 0.6 %collective-permute-start.3 = (bf16[24,1024]{1,0:T(8,128)(2,1)S(1)}, bf16[24,1024]{1,0:T(8,128)(2,1)S(1)}, u32[]{:S(2)}, u32[]{:S(2)}) collective-permute-start(bf16[24,1024]{1,0:T(8,128)(2,1)S(1)} %pair.1.after_ref), channel_id=1, source_target_pairs={{0,17},{1,16},{2,19},{3,18},{4,21},{5,20},{6,23},{7,22},{8,25},{9,... | collective-permute-start | bytes 147464 | tf_op jit(solution)/shard_map/ppermute | solution.py:39
  14.3 0.2 collective-permute-start.2
  14.5 2.9 %fetch.3 = (bf16[1,2048,1536]{2,1,0:T(8,128)(2,1)S(1)}, bf16[24,128]{1,0:T(8,128)(2,1)S(1)}) custom-call(bf16[24,1024]{1,0:T(8,128)(2,1)S(1)} %pair.1.after_ref, bf16[1,2048,1536]{2,1,0:T(8,128)(2,1)} %refs_0_.5), custom_call_target="tpu_custom_call" | custom-call | bytes 12582912 | tf_op jit(solution)/shard_map/fetch/pallas_call | solution.py:48
  17.3 0.0 copy-start
  17.3 0.0 collective-permute-done.5.rest_3_
  17.4 1.0 %collective-permute-done.4.rest_2_ = bf16[24,1024]{1,0:T(8,128)(2,1)S(1)} collective-permute-done((bf16[24,1024]{1,0:T(8,128)(2,1)S(1)}, bf16[24,1024]{1,0:T(8,128)(2,1)S(1)}, u32[]{:S(2)}, u32[]{:S(2)}) %collective-permute-start.4) | collective-permute-done | bytes 49184 | tf_op jit(solution)/shard_map/ppermute | solution.py:39
  18.4 0.0 collective-permute-done.3.rest_1_
  18.4 0.0 collective-permute-done.2.rest_0_
  18.4 2.4 %collective-permute-start.9 = (bf16[200,128]{1,0:T(8,128)(2,1)S(1)}, bf16[200,128]{1,0:T(8,128)(2,1)S(1)}, u32[]{:S(2)}, u32[]{:S(2)}) collective-permute-start(bf16[200,128]{1,0:T(8,128)(2,1)S(1)} %get-tuple-element.43.rest_0_), channel_id=1, source_target_pairs={{0,28},{1,29},{2,30},{3,31},{4,24},{5,25},{6,26},{7,27},{8,20},{9,... | collective-permute-start | bytes 153608 | tf_op jit(solution)/shard_map/ppermute | solution.py:39
  20.8 0.4 collective-permute-start.8
  21.2 0.4 collective-permute-start.7
  21.5 0.3 collective-permute-start.6
  21.8 1.3 %collective-permute-done.9.rest_3_ = bf16[200,128]{1,0:T(8,128)(2,1)S(1)} collective-permute-done((bf16[200,128]{1,0:T(8,128)(2,1)S(1)}, bf16[200,128]{1,0:T(8,128)(2,1)S(1)}, u32[]{:S(2)}, u32[]{:S(2)}) %collective-permute-start.9) | collective-permute-done | bytes 51232 | tf_op jit(solution)/shard_map/ppermute | solution.py:39
  23.1 0.2 collective-permute-start.12
  23.3 1.2 %collective-permute-done.8.rest_2_ = bf16[200,128]{1,0:T(8,128)(2,1)S(1)} collective-permute-done((bf16[200,128]{1,0:T(8,128)(2,1)S(1)}, bf16[200,128]{1,0:T(8,128)(2,1)S(1)}, u32[]{:S(2)}, u32[]{:S(2)}) %collective-permute-start.8) | collective-permute-done | bytes 51232 | tf_op jit(solution)/shard_map/ppermute | solution.py:39
  24.5 0.5 %collective-permute-start.11 = (bf16[200,128]{1,0:T(8,128)(2,1)S(1)}, bf16[200,128]{1,0:T(8,128)(2,1)S(1)}, u32[]{:S(2)}, u32[]{:S(2)}) collective-permute-start(bf16[200,128]{1,0:T(8,128)(2,1)S(1)} %collective-permute-done.8.rest_2_), channel_id=1, source_target_pairs={{0,16},{16,0},{1,17},{17,1},{2,18},{18,2},{3,19},{19,3},{4,20},{20... | collective-permute-start | bytes 153608 | tf_op jit(solution)/shard_map/ppermute | solution.py:28
  25.0 0.0 collective-permute-done.7.rest_1_
  25.0 0.1 collective-permute-start.10
  25.1 0.0 collective-permute-done.6.rest_0_
  25.1 0.6 %first_half.1 = (f32[96,1536]{1,0:T(8,128)S(1)}, f32[96,128]{1,0:T(8,128)S(1)}, f32[96,128]{1,0:T(8,128)S(1)}) custom-call(f32[1,2048]{1,0:T(1,128)S(1)} %get-tuple-element.41.gain_ref, bf16[1,2048,1536]{2,1,0:T(8,128)(2,1)S(1)} %get-tuple-element.42.w_ref, bf16[200,128]{1,0:T(8,128)(2,1)S(1)} %collective-permute-done.6.rest_0_, ...), custom_call_target="tpu_custom_call" | custom-call | tf_op jit(solution)/shard_map/first_half/pallas_call | solution.py:48
  25.7 0.0 collective-permute-done.12.rest_3_
  25.7 0.2 collective-permute-done.11.rest_2_
  25.9 0.4 collective-permute-done.10.rest_1_
  26.2 0.0 copy-done
  26.2 1.0 %second_half.1 = (bf16[96,768]{1,0:T(8,128)(2,1)S(1)}, bf16[96,1024]{1,0:T(8,128)(2,1)S(1)}) custom-call(f32[1,2048]{1,0:T(1,128)S(1)} %get-tuple-element.41.gain_ref, bf16[1,2048,1536]{2,1,0:T(8,128)(2,1)S(1)} %get-tuple-element.42.w_ref, f32[96,1536]{1,0:T(8,128)S(1)} %get-tuple-element.44.hidden_ref, f32[96,128]{1,0:T(8,128)S(1)} %get-tuple-element.45.square_ref, ...), custom_call_target="tpu_custom_call" | custom-call | tf_op jit(solution)/shard_map/second_half/pallas_call | solution.py:48
  27.2 0.2 collective-permute-start.13
  27.4 0.4 keep.1.kept_ref
  27.8 0.9 %collective-permute-done.13.came_ref = bf16[96,1024]{1,0:T(8,128)(2,1)S(1)} collective-permute-done((bf16[96,1024]{1,0:T(8,128)(2,1)S(1)}, bf16[96,1024]{1,0:T(8,128)(2,1)S(1)}, u32[]{:S(2)}, u32[]{:S(2)}) %collective-permute-start.13) | collective-permute-done | bytes 196640 | tf_op jit(solution)/shard_map/ppermute | solution.py:28
  28.8 1.3 %collective-permute-start.14 = (bf16[24,1024]{1,0:T(8,128)(2,1)S(1)}, bf16[24,1024]{1,0:T(8,128)(2,1)S(1)}, u32[]{:S(2)}, u32[]{:S(2)}) collective-permute-start(bf16[24,1024]{1,0:T(8,128)(2,1)S(1)} %get-tuple-element.49), channel_id=1, source_target_pairs={{0,28},{1,29},{2,30},{3,31},{4,24},{5,25},{6,26},{7,27},{8,20},{9,... | collective-permute-start | bytes 147464 | tf_op jit(solution)/shard_map/ppermute | solution.py:39
  30.1 1.1 %collective-permute-start.15 = (bf16[24,1024]{1,0:T(8,128)(2,1)S(1)}, bf16[24,1024]{1,0:T(8,128)(2,1)S(1)}, u32[]{:S(2)}, u32[]{:S(2)}) collective-permute-start(bf16[24,1024]{1,0:T(8,128)(2,1)S(1)} %get-tuple-element.50), channel_id=1, source_target_pairs={{0,24},{1,25},{2,26},{3,27},{4,28},{5,29},{6,30},{7,31},{8,16},{9,... | collective-permute-start | bytes 147464 | tf_op jit(solution)/shard_map/ppermute | solution.py:39
  31.2 0.6 %collective-permute-start.16 = (bf16[24,1024]{1,0:T(8,128)(2,1)S(1)}, bf16[24,1024]{1,0:T(8,128)(2,1)S(1)}, u32[]{:S(2)}, u32[]{:S(2)}) collective-permute-start(bf16[24,1024]{1,0:T(8,128)(2,1)S(1)} %get-tuple-element.51), channel_id=1, source_target_pairs={{0,20},{1,21},{2,22},{3,23},{4,16},{5,17},{6,18},{7,19},{8,28},{9,... | collective-permute-start | bytes 147464 | tf_op jit(solution)/shard_map/ppermute | solution.py:39
  31.8 0.4 collective-permute-start.17
  32.1 1.3 %collective-permute-done.14.refs_0_ = bf16[24,1024]{1,0:T(8,128)(2,1)S(1)} collective-permute-done((bf16[24,1024]{1,0:T(8,128)(2,1)S(1)}, bf16[24,1024]{1,0:T(8,128)(2,1)S(1)}, u32[]{:S(2)}, u32[]{:S(2)}) %collective-permute-start.14) | collective-permute-done | bytes 49184 | tf_op jit(solution)/shard_map/ppermute | solution.py:39
  33.5 1.3 %collective-permute-done.15.refs_1_ = bf16[24,1024]{1,0:T(8,128)(2,1)S(1)} collective-permute-done((bf16[24,1024]{1,0:T(8,128)(2,1)S(1)}, bf16[24,1024]{1,0:T(8,128)(2,1)S(1)}, u32[]{:S(2)}, u32[]{:S(2)}) %collective-permute-start.15) | collective-permute-done | bytes 49184 | tf_op jit(solution)/shard_map/ppermute | solution.py:39
  34.8 0.0 collective-permute-done.16.refs_2_
  34.8 0.0 collective-permute-done.17.refs_3_
  34.8 2.7 %collective-permute-start.18 = (bf16[24,256]{1,0:T(8,128)(2,1)S(1)}, bf16[24,256]{1,0:T(8,128)(2,1)S(1)}, u32[]{:S(2)}, u32[]{:S(2)}) collective-permute-start(bf16[24,256]{1,0:T(8,128)(2,1)S(1)} %get-tuple-element.53), channel_id=1, source_target_pairs={{0,19},{1,18},{2,17},{3,16},{4,23},{5,22},{6,21},{7,20},{8,27},{9,... | collective-permute-start | bytes 36872 | tf_op jit(solution)/shard_map/ppermute | solution.py:39
  37.5 0.0 collective-permute-start.19
  37.5 1.4 %collective-permute-start.20 = (bf16[24,256]{1,0:T(8,128)(2,1)S(1)}, bf16[24,256]{1,0:T(8,128)(2,1)S(1)}, u32[]{:S(2)}, u32[]{:S(2)}) collective-permute-start(bf16[24,256]{1,0:T(8,128)(2,1)S(1)} %get-tuple-element.55), channel_id=1, source_target_pairs={{0,17},{1,16},{2,19},{3,18},{4,21},{5,20},{6,23},{7,22},{8,25},{9,... | collective-permute-start | bytes 36872 | tf_op jit(solution)/shard_map/ppermute | solution.py:39
  38.9 0.2 collective-permute-start.21
  39.1 0.7 %collective-permute-done.18.rest_0_ = bf16[24,256]{1,0:T(8,128)(2,1)S(1)} collective-permute-done((bf16[24,256]{1,0:T(8,128)(2,1)S(1)}, bf16[24,256]{1,0:T(8,128)(2,1)S(1)}, u32[]{:S(2)}, u32[]{:S(2)}) %collective-permute-start.18) | collective-permute-done | bytes 12320 | tf_op jit(solution)/shard_map/ppermute | solution.py:39
  39.8 1.7 %collective-permute-done.19.rest_1_ = bf16[24,256]{1,0:T(8,128)(2,1)S(1)} collective-permute-done((bf16[24,256]{1,0:T(8,128)(2,1)S(1)}, bf16[24,256]{1,0:T(8,128)(2,1)S(1)}, u32[]{:S(2)}, u32[]{:S(2)}) %collective-permute-start.19) | collective-permute-done | bytes 12320 | tf_op jit(solution)/shard_map/ppermute | solution.py:39
  41.5 0.0 collective-permute-done.20.rest_2_
  41.5 0.0 collective-permute-done.21.rest_3_
  41.5 0.6 %final.1 = bf16[24,256]{1,0:T(8,128)(2,1)} custom-call(bf16[24,1024]{1,0:T(8,128)(2,1)S(1)} %get-tuple-element.40.middle_ref, bf16[24,256]{1,0:T(8,128)(2,1)S(1)} %collective-permute-done.18.rest_0_, bf16[24,256]{1,0:T(8,128)(2,1)S(1)} %collective-permute-done.19.rest_1_, bf16[24,256]{1,0:T(8,128)(2,1)S(1)} %collective-permute-done.20.rest_2_, ...), custom_call_target="tpu_custom_call" | custom-call | tf_op jit(solution)/shard_map/final/pallas_call | solution.py:469
  (4 shorter events, 0.1 us)
Async XLA Ops:
  3.1 5.0 %collective-permute-start = (bf16[24,640]{1,0:T(8,128)(2,1)S(1)}, bf16[24,640]{1,0:T(8,128)(2,1)S(1)}, u32[]{:S(2)}, u32[]{:S(2)}) collective-permute-start(bf16[24,640]{1,0:T(8,128)(2,1)S(1)} %get-tuple-element.35), channel_id=1, source_target_pairs={{0,1},{1,0},{2,3},{3,2},{4,5},{5,4},{6,7},{7,6},{8,9},{9,8},{10,11... | collective-permute-start | bytes 92168 | tf_op jit(solution)/shard_map/ppermute | solution.py:28
  8.5 1.3 %collective-permute-start.1 = (bf16[24,1024]{1,0:T(8,128)(2,1)S(1)}, bf16[24,1024]{1,0:T(8,128)(2,1)S(1)}, u32[]{:S(2)}, u32[]{:S(2)}) collective-permute-start(bf16[24,1024]{1,0:T(8,128)(2,1)S(1)} %get-tuple-element.37), channel_id=1, source_target_pairs={{0,16},{16,0},{1,17},{17,1},{2,18},{18,2},{3,19},{19,3},{4,20},{20... | collective-permute-start | bytes 147464 | tf_op jit(solution)/shard_map/ppermute | solution.py:28
  9.8 7.5 %collective-permute-start.5 = (bf16[24,1024]{1,0:T(8,128)(2,1)S(1)}, bf16[24,1024]{1,0:T(8,128)(2,1)S(1)}, u32[]{:S(2)}, u32[]{:S(2)}) collective-permute-start(bf16[24,1024]{1,0:T(8,128)(2,1)S(1)} %pair.1.after_ref), channel_id=1, source_target_pairs={{0,19},{1,18},{2,17},{3,16},{4,23},{5,22},{6,21},{7,20},{8,27},{9,... | collective-permute-start | bytes 147464 | tf_op jit(solution)/shard_map/ppermute | solution.py:39
  13.7 4.7 %collective-permute-start.4 = (bf16[24,1024]{1,0:T(8,128)(2,1)S(1)}, bf16[24,1024]{1,0:T(8,128)(2,1)S(1)}, u32[]{:S(2)}, u32[]{:S(2)}) collective-permute-start(bf16[24,1024]{1,0:T(8,128)(2,1)S(1)} %pair.1.after_ref), channel_id=1, source_target_pairs={{0,18},{1,19},{2,16},{3,17},{4,22},{5,23},{6,20},{7,21},{8,26},{9,... | collective-permute-start | bytes 147464 | tf_op jit(solution)/shard_map/ppermute | solution.py:39
  13.7 4.7 %collective-permute-start.3 = (bf16[24,1024]{1,0:T(8,128)(2,1)S(1)}, bf16[24,1024]{1,0:T(8,128)(2,1)S(1)}, u32[]{:S(2)}, u32[]{:S(2)}) collective-permute-start(bf16[24,1024]{1,0:T(8,128)(2,1)S(1)} %pair.1.after_ref), channel_id=1, source_target_pairs={{0,17},{1,16},{2,19},{3,18},{4,21},{5,20},{6,23},{7,22},{8,25},{9,... | collective-permute-start | bytes 147464 | tf_op jit(solution)/shard_map/ppermute | solution.py:39
  14.3 4.1 %collective-permute-start.2 = (bf16[24,1024]{1,0:T(8,128)(2,1)S(1)}, bf16[24,1024]{1,0:T(8,128)(2,1)S(1)}, u32[]{:S(2)}, u32[]{:S(2)}) collective-permute-start(bf16[24,1024]{1,0:T(8,128)(2,1)S(1)} %pair.1.after_ref), channel_id=1, source_target_pairs={{0,16},{1,17},{2,18},{3,19},{4,20},{5,21},{6,22},{7,23},{8,24},{9,... | collective-permute-start | bytes 147464 | tf_op jit(solution)/shard_map/ppermute | solution.py:39
  17.3 8.9 %copy-start = (bf16[1,768,2048]{2,1,0:T(8,128)(2,1)S(1)}, bf16[1,768,2048]{2,1,0:T(8,128)(2,1)}, u32[]{:S(2)}) copy-start(bf16[1,768,2048]{2,1,0:T(8,128)(2,1)} %down_ref.3) | copy-start | bytes 9437188
  18.4 4.7 %collective-permute-start.9 = (bf16[200,128]{1,0:T(8,128)(2,1)S(1)}, bf16[200,128]{1,0:T(8,128)(2,1)S(1)}, u32[]{:S(2)}, u32[]{:S(2)}) collective-permute-start(bf16[200,128]{1,0:T(8,128)(2,1)S(1)} %get-tuple-element.43.rest_0_), channel_id=1, source_target_pairs={{0,28},{1,29},{2,30},{3,31},{4,24},{5,25},{6,26},{7,27},{8,20},{9,... | collective-permute-start | bytes 153608 | tf_op jit(solution)/shard_map/ppermute | solution.py:39
  20.8 3.7 %collective-permute-start.8 = (bf16[200,128]{1,0:T(8,128)(2,1)S(1)}, bf16[200,128]{1,0:T(8,128)(2,1)S(1)}, u32[]{:S(2)}, u32[]{:S(2)}) collective-permute-start(bf16[200,128]{1,0:T(8,128)(2,1)S(1)} %get-tuple-element.43.rest_0_), channel_id=1, source_target_pairs={{0,24},{1,25},{2,26},{3,27},{4,28},{5,29},{6,30},{7,31},{8,16},{9,... | collective-permute-start | bytes 153608 | tf_op jit(solution)/shard_map/ppermute | solution.py:39
  21.2 3.8 %collective-permute-start.7 = (bf16[200,128]{1,0:T(8,128)(2,1)S(1)}, bf16[200,128]{1,0:T(8,128)(2,1)S(1)}, u32[]{:S(2)}, u32[]{:S(2)}) collective-permute-start(bf16[200,128]{1,0:T(8,128)(2,1)S(1)} %get-tuple-element.43.rest_0_), channel_id=1, source_target_pairs={{0,20},{1,21},{2,22},{3,23},{4,16},{5,17},{6,18},{7,19},{8,28},{9,... | collective-permute-start | bytes 153608 | tf_op jit(solution)/shard_map/ppermute | solution.py:39
  21.5 3.5 %collective-permute-start.6 = (bf16[200,128]{1,0:T(8,128)(2,1)S(1)}, bf16[200,128]{1,0:T(8,128)(2,1)S(1)}, u32[]{:S(2)}, u32[]{:S(2)}) collective-permute-start(bf16[200,128]{1,0:T(8,128)(2,1)S(1)} %get-tuple-element.43.rest_0_), channel_id=1, source_target_pairs={{0,16},{1,17},{2,18},{3,19},{4,20},{5,21},{6,22},{7,23},{8,24},{9,... | collective-permute-start | bytes 153608 | tf_op jit(solution)/shard_map/ppermute | solution.py:39
  23.1 2.6 %collective-permute-start.12 = (bf16[200,128]{1,0:T(8,128)(2,1)S(1)}, bf16[200,128]{1,0:T(8,128)(2,1)S(1)}, u32[]{:S(2)}, u32[]{:S(2)}) collective-permute-start(bf16[200,128]{1,0:T(8,128)(2,1)S(1)} %collective-permute-done.9.rest_3_), channel_id=1, source_target_pairs={{0,16},{16,0},{1,17},{17,1},{2,18},{18,2},{3,19},{19,3},{4,20},{20... | collective-permute-start | bytes 153608 | tf_op jit(solution)/shard_map/ppermute | solution.py:28
  24.5 1.4 %collective-permute-start.11 = (bf16[200,128]{1,0:T(8,128)(2,1)S(1)}, bf16[200,128]{1,0:T(8,128)(2,1)S(1)}, u32[]{:S(2)}, u32[]{:S(2)}) collective-permute-start(bf16[200,128]{1,0:T(8,128)(2,1)S(1)} %collective-permute-done.8.rest_2_), channel_id=1, source_target_pairs={{0,16},{16,0},{1,17},{17,1},{2,18},{18,2},{3,19},{19,3},{4,20},{20... | collective-permute-start | bytes 153608 | tf_op jit(solution)/shard_map/ppermute | solution.py:28
  25.0 1.2 %collective-permute-start.10 = (bf16[200,128]{1,0:T(8,128)(2,1)S(1)}, bf16[200,128]{1,0:T(8,128)(2,1)S(1)}, u32[]{:S(2)}, u32[]{:S(2)}) collective-permute-start(bf16[200,128]{1,0:T(8,128)(2,1)S(1)} %collective-permute-done.7.rest_1_), channel_id=1, source_target_pairs={{0,16},{16,0},{1,17},{17,1},{2,18},{18,2},{3,19},{19,3},{4,20},{20... | collective-permute-start | bytes 153608 | tf_op jit(solution)/shard_map/ppermute | solution.py:28
  27.2 1.5 %collective-permute-start.13 = (bf16[96,1024]{1,0:T(8,128)(2,1)S(1)}, bf16[96,1024]{1,0:T(8,128)(2,1)S(1)}, u32[]{:S(2)}, u32[]{:S(2)}) collective-permute-start(bf16[96,1024]{1,0:T(8,128)(2,1)S(1)} %get-tuple-element.48), channel_id=1, source_target_pairs={{0,16},{16,0},{1,17},{17,1},{2,18},{18,2},{3,19},{19,3},{4,20},{20... | collective-permute-start | bytes 589832 | tf_op jit(solution)/shard_map/ppermute | solution.py:28
  28.8 4.7 %collective-permute-start.14 = (bf16[24,1024]{1,0:T(8,128)(2,1)S(1)}, bf16[24,1024]{1,0:T(8,128)(2,1)S(1)}, u32[]{:S(2)}, u32[]{:S(2)}) collective-permute-start(bf16[24,1024]{1,0:T(8,128)(2,1)S(1)} %get-tuple-element.49), channel_id=1, source_target_pairs={{0,28},{1,29},{2,30},{3,31},{4,24},{5,25},{6,26},{7,27},{8,20},{9,... | collective-permute-start | bytes 147464 | tf_op jit(solution)/shard_map/ppermute | solution.py:39
  30.1 4.7 %collective-permute-start.15 = (bf16[24,1024]{1,0:T(8,128)(2,1)S(1)}, bf16[24,1024]{1,0:T(8,128)(2,1)S(1)}, u32[]{:S(2)}, u32[]{:S(2)}) collective-permute-start(bf16[24,1024]{1,0:T(8,128)(2,1)S(1)} %get-tuple-element.50), channel_id=1, source_target_pairs={{0,24},{1,25},{2,26},{3,27},{4,28},{5,29},{6,30},{7,31},{8,16},{9,... | collective-permute-start | bytes 147464 | tf_op jit(solution)/shard_map/ppermute | solution.py:39
  31.2 3.6 %collective-permute-start.16 = (bf16[24,1024]{1,0:T(8,128)(2,1)S(1)}, bf16[24,1024]{1,0:T(8,128)(2,1)S(1)}, u32[]{:S(2)}, u32[]{:S(2)}) collective-permute-start(bf16[24,1024]{1,0:T(8,128)(2,1)S(1)} %get-tuple-element.51), channel_id=1, source_target_pairs={{0,20},{1,21},{2,22},{3,23},{4,16},{5,17},{6,18},{7,19},{8,28},{9,... | collective-permute-start | bytes 147464 | tf_op jit(solution)/shard_map/ppermute | solution.py:39
  31.8 3.0 %collective-permute-start.17 = (bf16[24,1024]{1,0:T(8,128)(2,1)S(1)}, bf16[24,1024]{1,0:T(8,128)(2,1)S(1)}, u32[]{:S(2)}, u32[]{:S(2)}) collective-permute-start(bf16[24,1024]{1,0:T(8,128)(2,1)S(1)} %get-tuple-element.52), channel_id=1, source_target_pairs={{0,16},{1,17},{2,18},{3,19},{4,20},{5,21},{6,22},{7,23},{8,24},{9,... | collective-permute-start | bytes 147464 | tf_op jit(solution)/shard_map/ppermute | solution.py:39
  34.8 5.0 %collective-permute-start.18 = (bf16[24,256]{1,0:T(8,128)(2,1)S(1)}, bf16[24,256]{1,0:T(8,128)(2,1)S(1)}, u32[]{:S(2)}, u32[]{:S(2)}) collective-permute-start(bf16[24,256]{1,0:T(8,128)(2,1)S(1)} %get-tuple-element.53), channel_id=1, source_target_pairs={{0,19},{1,18},{2,17},{3,16},{4,23},{5,22},{6,21},{7,20},{8,27},{9,... | collective-permute-start | bytes 36872 | tf_op jit(solution)/shard_map/ppermute | solution.py:39
  37.5 4.0 %collective-permute-start.19 = (bf16[24,256]{1,0:T(8,128)(2,1)S(1)}, bf16[24,256]{1,0:T(8,128)(2,1)S(1)}, u32[]{:S(2)}, u32[]{:S(2)}) collective-permute-start(bf16[24,256]{1,0:T(8,128)(2,1)S(1)} %get-tuple-element.54), channel_id=1, source_target_pairs={{0,18},{1,19},{2,16},{3,17},{4,22},{5,23},{6,20},{7,21},{8,26},{9,... | collective-permute-start | bytes 36872 | tf_op jit(solution)/shard_map/ppermute | solution.py:39
  37.5 4.0 %collective-permute-start.20 = (bf16[24,256]{1,0:T(8,128)(2,1)S(1)}, bf16[24,256]{1,0:T(8,128)(2,1)S(1)}, u32[]{:S(2)}, u32[]{:S(2)}) collective-permute-start(bf16[24,256]{1,0:T(8,128)(2,1)S(1)} %get-tuple-element.55), channel_id=1, source_target_pairs={{0,17},{1,16},{2,19},{3,18},{4,21},{5,20},{6,23},{7,22},{8,25},{9,... | collective-permute-start | bytes 36872 | tf_op jit(solution)/shard_map/ppermute | solution.py:39
  38.9 2.6 %collective-permute-start.21 = (bf16[24,256]{1,0:T(8,128)(2,1)S(1)}, bf16[24,256]{1,0:T(8,128)(2,1)S(1)}, u32[]{:S(2)}, u32[]{:S(2)}) collective-permute-start(bf16[24,256]{1,0:T(8,128)(2,1)S(1)} %get-tuple-element.56), channel_id=1, source_target_pairs={{0,16},{1,17},{2,18},{3,19},{4,20},{5,21},{6,22},{7,23},{8,24},{9,... | collective-permute-start | bytes 36872 | tf_op jit(solution)/shard_map/ppermute | solution.py:39
